TPU v7x, 128 devices: a whole 4x4x4 slice. The times are simulated.
128 devices in a mesh: attn: 16 (over z_hi, x, core), ffn: 8 (over z_lo, y).
Axes of the slice: x: 4, y: 4, z: 4 (z_hi: 2, z_lo: 2; z = z_hi * 2 + z_lo), core: 2. Of those that a mesh axis runs over, the one named last changes fastest.
Arguments:
- queries: bfloat16 [2, 512, 64, 256], P(None, ('attn', 'ffn')), may hold values from -128 to 128
- cache_keys: bfloat16 [2, 512, 1536, 256], P(None, ('attn', 'ffn')), may hold values from -8 to 8
- cache_values: bfloat16 [2, 512, 1536, 256], P(None, ('attn', 'ffn')), may hold values from -6 to 6
- lengths: int32 [2, 512], P(None, ('attn', 'ffn')), may hold values from 2 to 1536, as said below
- residual: bfloat16 [2, 512, 7168], P(None, None, 'ffn'), may hold values from -6 to 6
- norm_gain: bfloat16 [7168], P('ffn'), may hold values from 0.5 to 1.5
- out_weight: bfloat16 [16384, 7168], P('attn', 'ffn'), may hold values from -0.375 to 0.375
- gate_weight: bfloat16 [7168, 18432], P('ffn', 'attn'), may hold values from -0.0625 to 0.0625
- up_weight: bfloat16 [7168, 18432], P('ffn', 'attn'), may hold values from -0.0625 to 0.0625
- down_weight: bfloat16 [18432, 7168], P('attn', 'ffn'), may hold values from -0.046875 to 0.046875
Outputs:
- mixed: bfloat16 [2, 512, 7168], P(None, 'attn', 'ffn')
Inputs may be any that keep to these rules, and one draw needn't show every extreme that they name: `lengths`: each micro-batch's first sequence has 1536 valid positions.
All inputs are finite; a program needn't handle non-finite values. Where the computation divides by a largest or mean magnitude, that divisor is 1e-20 or more.
Results may differ from a plain program's by a relative error of at most 0.023.
Values may be sent and summed in bfloat16 or wider, within the bound.
No kernel may reach another device: no remote copies, remote signals or barrier semaphores. Data moves between devices by JAX's collectives and lax.ppermute only.
A program may use at most 128 MiB of HBM per device.

v0:
```python
import math

import jax
import jax.numpy as jnp
from jax import lax
from jax.sharding import PartitionSpec as P

D = 7168
QB = 128


negative_fill = -1e30


def attend_full(query_rows, key_cache, value_cache, length):
    scores = jnp.einsum(
        "rhd,rld->rhl", query_rows, key_cache, preferred_element_type=jnp.float32
    ) / math.sqrt(query_rows.shape[2])
    offsets = lax.broadcasted_iota(jnp.int32, (1, 1, key_cache.shape[1]), 2)
    valid_mask = offsets < length[:, None, None]
    scores = jnp.where(valid_mask, scores, negative_fill)
    row_peak = jnp.max(scores, axis=2, keepdims=True)
    weights = jnp.where(valid_mask, jnp.exp(scores - row_peak), 0.0)
    totals = jnp.sum(weights, axis=2, keepdims=True)
    weighted = jnp.einsum(
        "rhl,rld->rhd",
        weights.astype(jnp.bfloat16),
        value_cache,
        preferred_element_type=jnp.float32,
    )
    return (weighted / totals).reshape(query_rows.shape[0], -1)


def local(
    queries,
    cache_keys,
    cache_values,
    lengths,
    residual,
    norm_gain,
    out_weight,
    gate_weight,
    up_weight,
    down_weight,
):
    micro_count = queries.shape[0]
    row_count = queries.shape[1]
    n_attn = lax.axis_size("attn")
    attn_index = lax.axis_index("attn")
    width_part = residual.shape[2]
    outputs = []
    for micro in range(micro_count):
        attn_out = attend_full(
            queries[micro], cache_keys[micro], cache_values[micro], lengths[micro]
        )
        blocks = attn_out.reshape(row_count, -1, QB)
        block_scales = (jnp.max(jnp.abs(blocks), axis=2) + 1e-06).astype(jnp.bfloat16)
        levels = jnp.floor(127.0 * blocks / block_scales.astype(jnp.float32)[:, :, None] + 0.5)
        quantized = jnp.clip(levels, -127.0, 127.0).astype(jnp.bfloat16).reshape(row_count, -1)
        row_values, row_scales = (
            lax.all_gather(quantized, "ffn", axis=0, tiled=True),
            lax.all_gather(block_scales, "ffn", axis=0, tiled=True),
        )
        moved_values, moved_scales = (
            lax.all_to_all(row_values, "attn", split_axis=1, concat_axis=0, tiled=True),
            lax.all_to_all(row_scales, "attn", split_axis=1, concat_axis=0, tiled=True),
        )
        tokens = moved_values.shape[0]
        group_blocks = moved_scales.shape[1]
        out_blocks = out_weight.reshape(group_blocks, QB, width_part)
        block_products = jnp.einsum(
            "hmn,mnr->hmr",
            moved_values.reshape(tokens, group_blocks, QB),
            out_blocks,
            preferred_element_type=jnp.float32,
        )
        partial_sum = jnp.sum(
            block_products * (moved_scales.astype(jnp.float32) / 127.0)[:, :, None], axis=1
        )
        projected = lax.psum(partial_sum.astype(jnp.bfloat16), "attn").astype(jnp.float32)
        stream = residual[micro].astype(jnp.float32) + projected
        scaled = (stream * norm_gain.astype(jnp.float32)).astype(jnp.bfloat16)
        gate_part = jnp.dot(scaled, gate_weight, preferred_element_type=jnp.float32)
        up_part = jnp.dot(scaled, up_weight, preferred_element_type=jnp.float32)
        square_part = jnp.sum(stream * stream, axis=1)
        gate_sum, up_sum, square_sum = (
            lax.psum(gate_part.astype(jnp.bfloat16), "ffn").astype(jnp.float32),
            lax.psum(up_part.astype(jnp.bfloat16), "ffn").astype(jnp.float32),
            lax.psum(square_part.astype(jnp.bfloat16), "ffn").astype(jnp.float32),
        )
        inv_rms = lax.rsqrt(square_sum / D + 1e-06)
        activated = (jax.nn.silu(gate_sum * inv_rms[:, None]) * (up_sum * inv_rms[:, None])).astype(
            jnp.bfloat16
        )
        share_rows = tokens // n_attn
        down_whole = lax.psum(
            jnp.dot(activated, down_weight, preferred_element_type=jnp.float32).astype(
                jnp.bfloat16
            ),
            "attn",
        ).astype(jnp.float32)
        down_rows = lax.dynamic_slice_in_dim(down_whole, attn_index * share_rows, share_rows, 0)
        stream_rows = lax.dynamic_slice_in_dim(stream, attn_index * share_rows, share_rows, 0)
        outputs.append((stream_rows + down_rows).astype(jnp.bfloat16))
    return jnp.stack(outputs)


def solution(mesh):
    in_specs = (
        P(None, ("attn", "ffn"), None, None),
        P(None, ("attn", "ffn"), None, None),
        P(None, ("attn", "ffn"), None, None),
        P(None, ("attn", "ffn")),
        P(None, None, "ffn"),
        P("ffn"),
        P("attn", "ffn"),
        P("ffn", "attn"),
        P("ffn", "attn"),
        P("attn", "ffn"),
    )
    out_specs = P(None, "attn", "ffn")
    return jax.shard_map(local, mesh=mesh, in_specs=in_specs, out_specs=out_specs, check_vma=False)
```

profile of v0, /device:TPU:0, one launch (start us, length us, event | category | flops | bytes accessed | tf_op | source)
XLA Modules:
  0.0 565.9 jit_solution(1899498525613450584)
XLA Ops:
  6.5 0.8 slice_bitcast_fusion.1
  7.5 4.1 fusion.61
  11.6 2.8 multiply_bitcast_fusion
  14.4 0.2 copy.30
  14.9 0.9 fusion.51
  15.9 4.0 fusion.60
  19.9 2.8 multiply_bitcast_fusion.1
  22.7 0.2 copy.27
  23.2 0.9 fusion.50
  24.1 19.5 %all-gather.3 = bf16[8,4,128]{2,1,0:T(4,128)(2,1)S(1)} all-gather(bf16[1,4,128]{2,1,0:T(4,128)(2,1)S(1)} %get-tuple-element.26), channel_id=1, replica_groups=mesh['attn'=16,'ffn'=8] {'ffn'}, dimensions={0}, use_global_device_ids=true | all-gather | bytes 9216 | tf_op jit(solution)/shard_map/all_gather | solution.py:62
  43.7 0.2 all_to_all.52
  43.9 0.2 copy.25
  44.0 0.7 reshape.140
  44.7 7.4 %all-to-all-start.3 = ((bf16[16,2,128]{2,1,0:T(2,128)(2,1)}), bf16[16,2,128]{2,1,0:T(2,128)(2,1)S(1)}, u32[]{:S(2)}, u32[]{:S(2)}) async-start(bf16[16,2,128]{2,1,0:T(2,128)(2,1)} %reshape.140), calls=%async_computation.3 | async-start | bytes 16384 | tf_op jit(solution)/shard_map/all_to_all | solution.py:66
  52.2 15.1 %all-gather.1 = bf16[8,4,128]{2,1,0:T(4,128)(2,1)S(1)} all-gather(bf16[1,4,128]{2,1,0:T(4,128)(2,1)S(1)} %get-tuple-element.24), channel_id=1, replica_groups=mesh['attn'=16,'ffn'=8] {'ffn'}, dimensions={0}, use_global_device_ids=true | all-gather | bytes 9216 | tf_op jit(solution)/shard_map/all_gather | solution.py:62
  67.3 0.2 all_to_all.47
  67.4 0.2 copy.21
  67.6 0.7 reshape.142
  68.3 7.2 %all-to-all-start.1 = ((bf16[16,2,128]{2,1,0:T(2,128)(2,1)}), bf16[16,2,128]{2,1,0:T(2,128)(2,1)S(1)}, u32[]{:S(2)}, u32[]{:S(2)}) async-start(bf16[16,2,128]{2,1,0:T(2,128)(2,1)} %reshape.142), calls=%async_computation.1 | async-start | bytes 16384 | tf_op jit(solution)/shard_map/all_to_all | solution.py:66
  75.5 1.8 all_to_all.49
  77.4 1.6 copy.23
  79.0 4.1 all-to-all-done.1
  83.1 3.7 all-to-all-start.2
  86.7 12.6 %all-gather.7.cloned.1.call-done = bf16[8,4,16384]{2,1,0:T(4,128)(2,1)} async-done(((bf16[1,4,16384]{2,1,0:T(4,128)(2,1)}), bf16[8,4,16384]{2,1,0:T(4,128)(2,1)}) %all-gather.7.cloned.1.call-update) | async-done | bytes 1048592 | tf_op jit(solution)/shard_map/all_gather | solution.py:61
  99.3 2.6 all_to_all.44
  101.9 2.8 copy.19
  104.7 7.1 %all-to-all-start = ((bf16[32,16,1024]{2,0,1:T(8,128)(2,1)}), bf16[32,16,1024]{2,0,1:T(8,128)(2,1)}, u32[]{:S(2)}, u32[]{:S(2)}) async-start(bf16[32,16,1024]{2,0,1:T(8,128)(2,1)} %copy.19), calls=%async_computation | async-start | bytes 2097152 | tf_op jit(solution)/shard_map/all_to_all | solution.py:65
  112.2 1.3 copy.32
  113.5 16.3 %all-to-all-done = bf16[32,16,1024]{2,0,1:T(8,128)(2,1)} async-done(((bf16[32,16,1024]{2,0,1:T(8,128)(2,1)}), bf16[32,16,1024]{2,0,1:T(8,128)(2,1)}, u32[]{:S(2)}, u32[]{:S(2)}) %all-to-all-start) | async-done | bytes 1048608 | tf_op jit(solution)/shard_map/all_to_all | solution.py:65
  129.8 1.5 copy.29
  131.3 5.0 fusion.2
  136.3 3.4 fusion.3
  139.8 0.2 all-reduce.12.cloned.1.call-start
  140.0 0.4 copy-done.5
  140.5 137.0 %all-reduce.10.cloned.1.call-done = (bf16[512,896]{1,0:T(8,128)(2,1)}, bf16[512,896]{1,0:T(8,128)(2,1)}) async-done(((bf16[512,896]{1,0:T(8,128)(2,1)}, bf16[512,896]{1,0:T(8,128)(2,1)}), (bf16[512,896]{1,0:T(8,128)(2,1)}, bf16[512,896]{1,0:T(8,128)(2,1)})) %all-reduce.10.cloned.1.call-update) | async-done | bytes 1835024 | tf_op jit(solution)/shard_map/psum | solution.py:80
  277.5 4.2 convolution_convert_fusion
  281.8 2.6 convolution_convert_fusion.1
  284.3 2.6 convolution_convert_fusion.2
  286.9 2.6 convolution_convert_fusion.3
  289.6 4.1 multiply_reduce_fusion.1
  293.7 19.2 %all-reduce.2 = (bf16[512]{0:T(512)(128)(2,1)S(1)}, bf16[512]{0:T(512)(128)(2,1)S(1)}) all-reduce(bf16[512]{0:T(512)(128)(2,1)S(1)} %get-tuple-element.6, bf16[512]{0:T(512)(128)(2,1)S(1)} %get-tuple-element.5), channel_id=1, replica_groups=mesh['attn'=16,'ffn'=8] {'ffn'}, use_global_device_ids=true, to_apply=%region_17.18 | all-reduce | flops 1024 | bytes 4096 | tf_op jit(solution)/shard_map/psum | solution.py:89
  312.9 93.9 %all-reduce.12.cloned.1.call-done = (bf16[512,1152]{1,0:T(8,128)(2,1)}, bf16[512,1152]{1,0:T(8,128)(2,1)}, bf16[512,1152]{1,0:T(8,128)(2,1)}, bf16[512,1152]{1,0:T(8,128)(2,1)}) async-done(((bf16[512,1152]{1,0:T(8,128)(2,1)}, bf16[512,1152]{1,0:T(8,128)(2,1)}, bf16[512,1152]{1,0:T(8,128)(2,1)}, bf16[512,1152]{1,0:T(8,128)(2,1)}), (bf16[512,1152]{1,0:T(8,128)(2,1)}, bf16[512,1152]{1,0:T(8,128)(2,1)}, ...) | async-done | bytes 4718608 | tf_op jit(solution)/shard_map/psum | solution.py:88
  406.8 5.2 convolution_convert_fusion.4
  412.0 2.7 convolution_convert_fusion.5
  414.7 142.1 %all-reduce.8.cloned.1.call-done = (bf16[512,896]{1,0:T(8,128)(2,1)}, bf16[512,896]{1,0:T(8,128)(2,1)}) async-done(((bf16[512,896]{1,0:T(8,128)(2,1)}, bf16[512,896]{1,0:T(8,128)(2,1)}), (bf16[512,896]{1,0:T(8,128)(2,1)}, bf16[512,896]{1,0:T(8,128)(2,1)})) %all-reduce.8.cloned.1.call-update) | async-done | bytes 1835024 | tf_op jit(solution)/shard_map/psum | solution.py:96
  556.9 0.9 fusion.52
  557.8 0.9 fusion.53
  558.7 0.7 pad_maximum_fusion
  (55 shorter events, 1.4 us)
Async XLA Ops:
  6.5 271.0 %copy-start = (bf16[896,1152]{1,0:T(8,128)(2,1)S(1)}, bf16[896,1152]{1,0:T(8,128)(2,1)}, u32[]{:S(2)}) copy-start(bf16[896,1152]{1,0:T(8,128)(2,1)} %param.18) | copy-start | bytes 6193156
  6.5 69.0 %all-gather.9.cloned.1.call-start = ((), (), s32[]{:S(2)}) async-start(), calls=%async_computation.5 | async-start | bytes 1179648 | tf_op jit(solution)/shard_map/all_gather | solution.py:61
  14.4 1.5 copy-start.11
  15.8 83.5 %all-gather.7.cloned.1.call-start = ((), (), s32[]{:S(2)}) async-start(), calls=%async_computation.4 | async-start | bytes 1179648 | tf_op jit(solution)/shard_map/all_gather | solution.py:61
  44.7 23.6 %all-to-all-start.3 = ((bf16[16,2,128]{2,1,0:T(2,128)(2,1)}), bf16[16,2,128]{2,1,0:T(2,128)(2,1)S(1)}, u32[]{:S(2)}, u32[]{:S(2)}) async-start(bf16[16,2,128]{2,1,0:T(2,128)(2,1)} %reshape.140), calls=%async_computation.3 | async-start | bytes 16384 | tf_op jit(solution)/shard_map/all_to_all | solution.py:66
  68.3 14.8 %all-to-all-start.1 = ((bf16[16,2,128]{2,1,0:T(2,128)(2,1)}), bf16[16,2,128]{2,1,0:T(2,128)(2,1)S(1)}, u32[]{:S(2)}, u32[]{:S(2)}) async-start(bf16[16,2,128]{2,1,0:T(2,128)(2,1)} %reshape.142), calls=%async_computation.1 | async-start | bytes 16384 | tf_op jit(solution)/shard_map/all_to_all | solution.py:66
  83.1 21.6 %all-to-all-start.2 = ((bf16[32,16,1024]{2,0,1:T(8,128)(2,1)}), bf16[32,16,1024]{2,0,1:T(8,128)(2,1)S(1)}, u32[]{:S(2)}, u32[]{:S(2)}) async-start(bf16[32,16,1024]{2,0,1:T(8,128)(2,1)} %copy.23), calls=%async_computation.2 | async-start | bytes 2097152 | tf_op jit(solution)/shard_map/all_to_all | solution.py:65
  104.7 25.1 %all-to-all-start = ((bf16[32,16,1024]{2,0,1:T(8,128)(2,1)}), bf16[32,16,1024]{2,0,1:T(8,128)(2,1)}, u32[]{:S(2)}, u32[]{:S(2)}) async-start(bf16[32,16,1024]{2,0,1:T(8,128)(2,1)} %copy.19), calls=%async_computation | async-start | bytes 2097152 | tf_op jit(solution)/shard_map/all_to_all | solution.py:65
  111.7 165.8 %all-reduce.10.cloned.1.call-start = ((), (), s32[]{:S(2)}) async-start(), calls=%async_computation.7 | async-start | bytes 3670016 | tf_op jit(solution)/shard_map/psum | solution.py:80
  113.5 17.8 %copy-start.2 = (bf16[64,8,8,128]{3,2,1,0:T(8,128)(2,1)S(1)}, bf16[64,8,8,128]{3,2,1,0:T(8,128)(2,1)}, u32[]{:S(2)}) copy-start(bf16[64,8,8,128]{3,2,1,0:T(8,128)(2,1)} %copy.32) | copy-start | bytes 3145732
  131.3 5.0 copy-start.8
  139.8 0.7 copy-start.5
  139.8 267.0 %all-reduce.12.cloned.1.call-start = ((), (), s32[]{:S(2)}) async-start(), calls=%async_computation.8 | async-start | bytes 9437184 | tf_op jit(solution)/shard_map/psum | solution.py:88
  277.5 4.2 copy-start.1
  277.5 4.2 copy-start.3
  277.5 4.2 copy-start.6
  281.7 2.6 copy-start.4
  289.5 267.3 %all-reduce.8.cloned.1.call-start = ((), (), s32[]{:S(2)}) async-start(), calls=%async_computation.6 | async-start | bytes 3670016 | tf_op jit(solution)/shard_map/psum | solution.py:96
  406.8 5.2 copy-start.7
  406.8 5.2 copy-start.9
  406.8 5.2 copy-start.10
Sparse Core Ops, SparseCore 0:
  15.9 41.4 all-gather.8
  59.1 40.1 all-gather.6
  139.9 137.5 all-reduce.9
  289.6 117.1 all-reduce.11
  414.8 141.9 all-reduce.7
where the time goes:
time: 567 us; the launch traced here: 566 us
  waiting for transfers between devices  406 us (72%)
  blocking collectives  53.8 us (9%)
  matrix products  42 us (7%)
  starting transfers between devices  25.7 us (5%)
  local copies, waits for them, and re-layouts  15.9 us (3%)
  between operations  13.4 us (2%)
  other arithmetic  8.81 us (2%)
    psum x1, waiting for transfers between devices, local(): lax.psum(jnp.dot(activated, down_weight, preferred_element_type=jnp.float...  142 us
    psum x1, waiting for transfers between devices, local(): lax.psum(partial_sum.astype(jnp.bfloat16), 'attn').astype(jnp.float32)  137 us
    psum x1, waiting for transfers between devices, local(): lax.psum(up_part.astype(jnp.bfloat16), 'ffn').astype(jnp.float32)  93.9 us
    all_gather x2, blocking collectives, local(): lax.all_gather(block_scales, 'ffn', axis=0, tiled=True)  34.6 us
    psum x1, blocking collectives, local(): lax.psum(square_part.astype(jnp.bfloat16), 'ffn').astype(jnp.float32)  19.2 us
    all_to_all x2, waiting for transfers between devices, local(): lax.all_to_all(row_values, 'attn', split_axis=1, concat_axis=0, tiled=True)  16.3 us
    all_to_all x2, starting transfers between devices, local(): lax.all_to_all(row_scales, 'attn', split_axis=1, concat_axis=0, tiled=True)  14.6 us
    all_gather x2, waiting for transfers between devices, local(): lax.all_gather(quantized, 'ffn', axis=0, tiled=True)  12.6 us
  transfers between devices with their start and end apart: 9, of which 6 were waited for; matrix products, arithmetic and copies ran while one was open for 4% of the time, Pallas kernels for 0%

commit v1 on v0

v1 whole, which is shorter than its diff:
```python
import functools
import math

import jax
import jax.numpy as jnp
from jax import lax
from jax.experimental import pallas as pl
from jax.experimental.pallas import tpu as pltpu
from jax.sharding import PartitionSpec as P

D = 7168
QB = 128
N_ATTN = 16
N_FFN = 8
NEG = -1e30
BF = jnp.bfloat16
F32 = jnp.float32
GROUPS = ((0, 1),)


def attend_kernel(len_ref, q_ref, k_ref, v_ref, o_ref):
    s = pl.program_id(0)
    q = q_ref[0]
    scores = lax.dot_general(
        q, k_ref[0], (((1,), (1,)), ((), ())), preferred_element_type=F32
    ) * (1.0 / math.sqrt(q.shape[1]))
    offsets = lax.broadcasted_iota(jnp.int32, scores.shape, 1)
    scores = jnp.where(offsets < len_ref[s], scores, NEG)
    peak = jnp.max(scores, axis=1, keepdims=True)
    weights = jnp.exp(scores - peak)
    totals = jnp.sum(weights, axis=1, keepdims=True)
    out = jnp.dot(weights.astype(BF), v_ref[0], preferred_element_type=F32) / totals
    for b in range(out.shape[1] // QB):
        block = out[:, b * QB : (b + 1) * QB]
        scale = (jnp.max(jnp.abs(block), axis=1, keepdims=True) + 1e-06).astype(BF).astype(F32)
        levels = jnp.clip(jnp.floor(127.0 * block / scale + 0.5), -127.0, 127.0)
        o_ref[0, :, b * QB : (b + 1) * QB] = (levels * scale / 127.0).astype(BF)


def attend(q, k, v, lengths):
    n, h, hd = q.shape
    l = k.shape[1]
    return pl.pallas_call(
        attend_kernel,
        out_shape=jax.ShapeDtypeStruct((n, h, hd), BF),
        grid_spec=pltpu.PrefetchScalarGridSpec(
            num_scalar_prefetch=1,
            grid=(n,),
            in_specs=[
                pl.BlockSpec((1, h, hd), lambda i, _: (i, 0, 0)),
                pl.BlockSpec((1, l, hd), lambda i, _: (i, 0, 0)),
                pl.BlockSpec((1, l, hd), lambda i, _: (i, 0, 0)),
            ],
            out_specs=pl.BlockSpec((1, h, hd), lambda i, _: (i, 0, 0)),
        ),
        compiler_params=pltpu.CompilerParams(vmem_limit_bytes=32 * 2**20),
        cost_estimate=pl.CostEstimate(
            flops=4 * n * h * l * hd, bytes_accessed=4 * n * l * hd, transcendentals=n * h * l
        ),
    )(lengths, q, k, v)


def ax(x, k):
    return lax.ppermute(x, "attn", [(i, i ^ k) for i in range(N_ATTN)])


def fx(x, k):
    return lax.ppermute(x, "ffn", [(i, i ^ k) for i in range(N_FFN)])


def total(parts):
    t = parts[0].astype(F32)
    for p in parts[1:]:
        t = t + p.astype(F32)
    return t


def flip_bits(x, axis, index):
    s = x.shape
    y = x.reshape(s[:axis] + (2, 2, 2) + s[axis + 1 :])
    for b in range(3):
        bit = (index >> (2 - b)) & 1
        y = jnp.where(bit == 1, jnp.flip(y, axis + b), y)
    return y.reshape(s)


def pick(x, i, axis):
    return lax.dynamic_index_in_dim(x, i, axis, keepdims=False)


def gather_ffn_zy(x):
    b = jnp.stack([x, fx(x, 4)])
    return jnp.stack([b] + [fx(b, k) for k in range(1, 4)], 1)


def gather_ffn_yz(x):
    b = jnp.stack([x] + [fx(x, k) for k in range(1, 4)])
    return jnp.stack([b, fx(b, 4)])


def scatter_ffn_zy(x):
    s = total([x[0], fx(x[1], 4)]).astype(BF)
    return total([s[0]] + [fx(s[k], k) for k in range(1, 4)])


def scatter_ffn_yz(x):
    s = total([x[:, 0]] + [fx(x[:, k], k) for k in range(1, 4)]).astype(BF)
    return total([s[0], fx(s[1], 4)])


def half(queries, cache_keys, cache_values, lengths, residual, gain, wo, wg, wu, wd):
    nm, r = queries.shape[:2]
    n = nm * r
    a = lax.axis_index("attn")
    f = lax.axis_index("ffn")
    zh, xi, c = a // 8, (a // 2) % 4, a % 2
    w = residual.shape[2]
    hid = wg.shape[1]

    out = attend(
        queries.reshape(n, *queries.shape[2:]),
        cache_keys.reshape(n, *cache_keys.shape[2:]),
        cache_values.reshape(n, *cache_values.shape[2:]),
        lengths.reshape(n),
    )
    groups = out.reshape(n, N_ATTN, -1).transpose(1, 0, 2)
    got = lax.all_to_all(groups, "attn", 0, 0)
    x0, x1 = got[:, :, :512], got[:, :, 512:]
    h0 = gather_ffn_zy(x0).reshape(N_FFN, N_ATTN, n, -1)
    h1 = gather_ffn_yz(x1).reshape(N_FFN, N_ATTN, n, -1)
    h0 = h0.transpose(1, 0, 2, 3).reshape(N_ATTN * N_FFN * n, -1)
    h1 = h1.transpose(1, 0, 2, 3).reshape(N_ATTN * N_FFN * n, -1)
    rows = N_FFN * n
    part = jnp.dot(h0, wo[:512], preferred_element_type=F32) + jnp.dot(
        h1, wo[512:], preferred_element_type=F32
    )
    part = part.astype(BF).reshape(8, 2, rows, w)

    other = ax(pick(part, 1 - c, 1), 1)
    s = (pick(part, c, 1).astype(F32) + other.astype(F32)).astype(BF).reshape(2, 4, rows, w)
    s = total(
        [pick(s, xi, 1)] + [ax(pick(s, xi ^ k, 1), 2 * k) for k in range(1, 4)]
    ).astype(BF)
    projected = total([pick(s, zh, 0), ax(pick(s, 1 - zh, 0), 8)])

    res = lax.dynamic_slice_in_dim(
        residual.reshape(nm, N_ATTN, N_FFN, r, w), a, 1, 1
    )[:, 0]
    res = flip_bits(res, 1, f).transpose(1, 0, 2, 3).reshape(rows, w)
    stream = res.astype(F32) + projected
    scaled = (stream * gain.astype(F32)).astype(BF)

    b = jnp.stack([scaled, ax(scaled, 8)])
    q4 = jnp.stack([b] + [ax(b, 2 * k) for k in range(1, 4)])
    full = jnp.stack([q4, ax(q4, 1)])
    full = full.reshape(N_ATTN * rows, w)
    square = jnp.sum((full.astype(F32) / gain.astype(F32)) ** 2, axis=1)
    gate = jnp.dot(full, wg, preferred_element_type=F32).astype(BF)
    up = jnp.dot(full, wu, preferred_element_type=F32).astype(BF)
    square = jnp.broadcast_to(square.astype(BF)[:, None], (N_ATTN * rows, 128))
    gate = jnp.concatenate([gate, square], axis=1)

    def by_owner(t):
        return t.reshape(N_ATTN, 2, 4, n, -1).transpose(1, 2, 0, 3, 4).reshape(
            2, 4, N_ATTN * n, -1
        )

    up_sum = scatter_ffn_zy(by_owner(up))
    gate_sum = scatter_ffn_yz(by_owner(gate))
    inv = lax.rsqrt(gate_sum[:, hid : hid + 1] / D + 1e-06)
    gate_sum = gate_sum[:, :hid]
    act = (jax.nn.silu(gate_sum * inv) * (up_sum * inv)).astype(BF)

    cut = 640
    a0 = gather_ffn_zy(act[:, :cut]).reshape(N_FFN, N_ATTN, n, -1)
    a1 = gather_ffn_yz(act[:, cut:]).reshape(N_FFN, N_ATTN, n, -1)
    a0 = a0.transpose(1, 0, 2, 3).reshape(N_ATTN * rows, -1)
    a1 = a1.transpose(1, 0, 2, 3).reshape(N_ATTN * rows, -1)
    down = jnp.dot(a0, wd[:cut], preferred_element_type=F32) + jnp.dot(
        a1, wd[cut:], preferred_element_type=F32
    )
    down = down.astype(BF).reshape(2, 4, 2, rows, w)
    s = (down[0].astype(F32) + ax(down[1], 1).astype(F32)).astype(BF)
    s = total([s[0]] + [ax(s[k], 2 * k) for k in range(1, 4)]).astype(BF)
    final = stream + total([s[0], ax(s[1], 8)])
    final = final.astype(BF).reshape(N_FFN, nm, r, w)
    final = flip_bits(final, 0, f).transpose(1, 0, 2, 3).reshape(nm, N_FFN * r, w)
    return final


def local(
    queries,
    cache_keys,
    cache_values,
    lengths,
    residual,
    norm_gain,
    out_weight,
    gate_weight,
    up_weight,
    down_weight,
):
    outs = []
    for g in GROUPS:
        sl = slice(g[0], g[-1] + 1)
        outs.append(
            half(
                queries[sl],
                cache_keys[sl],
                cache_values[sl],
                lengths[sl],
                residual[sl],
                norm_gain,
                out_weight,
                gate_weight,
                up_weight,
                down_weight,
            )
        )
    return jnp.concatenate(outs, axis=0)


def solution(mesh):
    in_specs = (
        P(None, ("attn", "ffn"), None, None),
        P(None, ("attn", "ffn"), None, None),
        P(None, ("attn", "ffn"), None, None),
        P(None, ("attn", "ffn")),
        P(None, None, "ffn"),
        P("ffn"),
        P("attn", "ffn"),
        P("ffn", "attn"),
        P("ffn", "attn"),
        P("attn", "ffn"),
    )
    out_specs = P(None, "attn", "ffn")
    return jax.shard_map(local, mesh=mesh, in_specs=in_specs, out_specs=out_specs, check_vma=False)
```

time: 567 us -> 245 us (0.43)
  waiting for transfers between devices: 406 us -> 125 us
  blocking collectives: 53.8 us -> 17 us
  matrix products: 42 us -> 12.8 us
  starting transfers between devices: 25.7 us -> 52 us
  between operations: 13.4 us -> 0.56 us
  Pallas kernels: 0 us -> 7.7 us
    psum x3 -> x0, waiting for transfers between devices: 373 us -> none  [the longest x1 142 us: local(): lax.psum(jnp.dot(activated, down_weight, preferred_element_type=jnp.float...]
    ppermute x0 -> x39, waiting for transfers between devices: none -> 125 us  [the longest x24 75.5 us: fx(): return lax.ppermute(x, 'ffn', [(i, i ^ k) for i in range(N_FFN)])]
    ppermute x0 -> x39, starting transfers between devices: none -> 52 us  [the longest x24 32.1 us: fx(): return lax.ppermute(x, 'ffn', [(i, i ^ k) for i in range(N_FFN)])]
    all_gather x2 -> x0, blocking collectives: 34.6 us -> none  [local(): lax.all_gather(block_scales, 'ffn', axis=0, tiled=True)]
    all_to_all x4 -> x0, starting transfers between devices: 25.3 us -> none  [the longest x2 14.6 us: local(): lax.all_to_all(row_scales, 'attn', split_axis=1, concat_axis=0, tiled=True)]
    dot_general x10 -> x6, matrix products: 33.9 us -> 12.8 us  [the longest x1 4.32 us: half(): gate = jnp.dot(full, wg, preferred_element_type=F32).astype(BF)]
    all_to_all x4 -> x0, waiting for transfers between devices: 20.4 us -> none  [the longest x2 16.3 us: local(): lax.all_to_all(row_values, 'attn', split_axis=1, concat_axis=0, tiled=True)]
    psum x1 -> x0, blocking collectives: 19.2 us -> none  [local(): lax.psum(square_part.astype(jnp.bfloat16), 'ffn').astype(jnp.float32)]
  transfers between devices with their start and end apart: 9 -> 39, of which waited for: 6 -> 30; matrix products, arithmetic and copies ran while one was open for 4% -> 6% of each run, Pallas kernels for 0% -> 0%
where the time goes in v1:
time: 245 us
  waiting for transfers between devices  125 us (51%)
  starting transfers between devices  52 us (21%)
  local copies, waits for them, and re-layouts  19.7 us (8%)
  blocking collectives  17 us (7%)
  matrix products  12.8 us (5%)
  other arithmetic  9.78 us (4%)
  Pallas kernels  7.7 us (3%)
    ppermute x24, waiting for transfers between devices, fx(): return lax.ppermute(x, 'ffn', [(i, i ^ k) for i in range(N_FFN)])  75.5 us
    ppermute x15, waiting for transfers between devices, ax(): return lax.ppermute(x, 'attn', [(i, i ^ k) for i in range(N_ATTN)])  49.6 us
    ppermute x24, starting transfers between devices, fx(): return lax.ppermute(x, 'ffn', [(i, i ^ k) for i in range(N_FFN)])  32.1 us
    ppermute x15, starting transfers between devices, ax(): return lax.ppermute(x, 'attn', [(i, i ^ k) for i in range(N_ATTN)])  19.9 us
    all_to_all x1, blocking collectives, half(): got = lax.all_to_all(groups, 'attn', 0, 0)  17 us
    unnamed x22, local copies, waits for them, and re-layouts  9.48 us
    pallas_call x1, Pallas kernels, attend(): pl.pallas_call(attend_kernel, out_shape=jax.ShapeDtypeStruct((n, h, hd),...  7.7 us
  transfers between devices with their start and end apart: 39, of which 30 were waited for; matrix products, arithmetic and copies ran while one was open for 6% of the time, Pallas kernels for 0%

profile of v1, /device:TPU:0, one launch (start us, length us, event | category | flops | bytes accessed | tf_op | source)
XLA Modules:
  0.0 244.6 jit_solution(9608867878733108631)
XLA Ops:
  0.9 2.8 %copy-done.2 = bf16[2,4,1536,256]{3,2,1,0:T(8,128)(2,1)S(1)} copy-done((bf16[2,4,1536,256]{3,2,1,0:T(8,128)(2,1)S(1)}, bf16[2,4,1536,256]{3,2,1,0:T(8,128)(2,1)}, u32[]{:S(2)}) %copy-start.2) | copy-done | bytes 6291480
  3.7 2.8 %copy-done.3 = bf16[2,4,1536,256]{3,2,1,0:T(8,128)(2,1)S(1)} copy-done((bf16[2,4,1536,256]{3,2,1,0:T(8,128)(2,1)S(1)}, bf16[2,4,1536,256]{3,2,1,0:T(8,128)(2,1)}, u32[]{:S(2)}) %copy-start.3) | copy-done | bytes 6291480
  7.4 7.7 %shard_map.100 = bf16[8,64,256]{2,1,0:T(8,128)(2,1)S(1)} custom-call(s32[8]{0:T(128)S(1)} %reshape.116.len_ref, bf16[8,64,256]{2,1,0:T(8,128)(2,1)S(1)} %bitcast.189, bf16[8,1536,256]{2,1,0:T(8,128)(2,1)S(1)} %bitcast.187, bf16[8,1536,256]{2,1,0:T(8,128)(2,1)S(1)} %bitcast.188), custom_call_target="tpu_custom_call" | custom-call | flops 805306368 | bytes 12582912 | tf_op jit(solution)/shard_map/pallas_call | solution.py:43
  15.5 17.0 %all_to_all.5 = bf16[16,8,1024]{2,1,0:T(8,128)(2,1)S(1)} all-to-all(bf16[16,8,1024]{2,1,0:T(8,128)(2,1)S(1)} %bitcast.213), channel_id=1, replica_groups=mesh['attn'=16,'ffn'=8] {'attn'}, dimensions={0} | all-to-all | bytes 524288 | tf_op jit(solution)/shard_map/all_to_all | solution.py:127
  35.2 2.9 %collective-permute-start.5 = (bf16[16,8,512]{2,1,0:T(8,128)(2,1)S(1)}, bf16[16,8,512]{2,1,0:T(8,128)(2,1)S(1)}, u32[]{:S(2)}, u32[]{:S(2)}) collective-permute-start(bf16[16,8,512]{2,1,0:T(8,128)(2,1)S(1)} %get-tuple-element.33), channel_id=1, source_target_pairs={{0,2},{1,3},{2,0},{3,1},{4,6},{5,7},{6,4},{7,5},{8,10},{9,11},{10,... | collective-permute-start | bytes 393224 | tf_op jit(solution)/shard_map/ppermute | solution.py:68
  39.4 3.5 %collective-permute-start.2 = (bf16[2,16,8,512]{3,2,1,0:T(8,128)(2,1)S(1)}, bf16[2,16,8,512]{3,2,1,0:T(8,128)(2,1)}, u32[]{:S(2)}, u32[]{:S(2)}) collective-permute-start(bf16[2,16,8,512]{3,2,1,0:T(8,128)(2,1)S(1)} %get-tuple-element.36), channel_id=1, source_target_pairs={{0,2},{1,3},{2,0},{3,1},{4,6},{5,7},{6,4},{7,5},{8,10},{9,11},{10,... | collective-permute-start | bytes 786440 | tf_op jit(solution)/shard_map/ppermute | solution.py:68
  43.1 2.2 collective-permute-done.5
  48.3 6.8 %collective-permute-done.2 = bf16[2,16,8,512]{3,2,1,0:T(8,128)(2,1)} collective-permute-done((bf16[2,16,8,512]{3,2,1,0:T(8,128)(2,1)S(1)}, bf16[2,16,8,512]{3,2,1,0:T(8,128)(2,1)}, u32[]{:S(2)}, u32[]{:S(2)}) %collective-permute-start.2) | collective-permute-done | bytes 262176 | tf_op jit(solution)/shard_map/ppermute | solution.py:68
  55.1 1.8 collective-permute-done.3
  64.8 4.1 %reshape.115 = bf16[2,16,8,4,896]{4,3,2,1,0:T(4,128)(2,1)} reshape(bf16[2,512,896]{2,1,0:T(8,128)(2,1)} %param.14) | data formatting | bytes 3670016 | tf_op jit(solution)/shard_map/reshape | solution.py:147
  71.5 2.3 collective-permute-start.10
  73.9 2.0 collective-permute-start.11
  75.9 5.6 %collective-permute-done.10 = bf16[2,64,896]{2,1,0:T(8,128)(2,1)S(1)} collective-permute-done((bf16[2,64,896]{2,1,0:T(8,128)(2,1)S(1)}, bf16[2,64,896]{2,1,0:T(8,128)(2,1)S(1)}, u32[]{:S(2)}, u32[]{:S(2)}) %collective-permute-start.10) | collective-permute-done | bytes 229408 | tf_op jit(solution)/shard_map/ppermute | solution.py:64
  81.5 4.5 %collective-permute-done.11 = bf16[2,64,896]{2,1,0:T(8,128)(2,1)S(1)} collective-permute-done((bf16[2,64,896]{2,1,0:T(8,128)(2,1)S(1)}, bf16[2,64,896]{2,1,0:T(8,128)(2,1)S(1)}, u32[]{:S(2)}, u32[]{:S(2)}) %collective-permute-start.11) | collective-permute-done | bytes 229408 | tf_op jit(solution)/shard_map/ppermute | solution.py:64
  86.2 1.9 collective-permute-start.12
  88.2 4.7 %collective-permute-done.12 = bf16[64,896]{1,0:T(8,128)(2,1)S(1)} collective-permute-done((bf16[64,896]{1,0:T(8,128)(2,1)S(1)}, bf16[64,896]{1,0:T(8,128)(2,1)S(1)}, u32[]{:S(2)}, u32[]{:S(2)}) %collective-permute-start.12) | collective-permute-done | bytes 114720 | tf_op jit(solution)/shard_map/ppermute | solution.py:64
  92.9 1.9 collective-permute-start.13
  94.8 4.5 %collective-permute-done.13 = bf16[64,896]{1,0:T(8,128)(2,1)S(1)} collective-permute-done((bf16[64,896]{1,0:T(8,128)(2,1)S(1)}, bf16[64,896]{1,0:T(8,128)(2,1)S(1)}, u32[]{:S(2)}, u32[]{:S(2)}) %collective-permute-start.13) | collective-permute-done | bytes 114720 | tf_op jit(solution)/shard_map/ppermute | solution.py:64
  100.4 2.7 %collective-permute-start.15 = (bf16[2,64,896]{2,1,0:T(8,128)(2,1)S(1)}, bf16[2,64,896]{2,1,0:T(8,128)(2,1)S(1)}, u32[]{:S(2)}, u32[]{:S(2)}) collective-permute-start(bf16[2,64,896]{2,1,0:T(8,128)(2,1)S(1)} %get-tuple-element.38), channel_id=1, source_target_pairs={{0,32},{8,40},{16,48},{24,56},{32,0},{40,8},{48,16},{56,24},{64,96... | collective-permute-start | bytes 688136 | tf_op jit(solution)/shard_map/ppermute | solution.py:64
  104.1 3.3 %collective-permute-done.14 = bf16[2,64,896]{2,1,0:T(8,128)(2,1)S(1)} collective-permute-done((bf16[2,64,896]{2,1,0:T(8,128)(2,1)S(1)}, bf16[2,64,896]{2,1,0:T(8,128)(2,1)S(1)}, u32[]{:S(2)}, u32[]{:S(2)}) %collective-permute-start.14) | collective-permute-done | bytes 229408 | tf_op jit(solution)/shard_map/ppermute | solution.py:64
  107.4 4.2 %collective-permute-done.15 = bf16[2,64,896]{2,1,0:T(8,128)(2,1)S(1)} collective-permute-done((bf16[2,64,896]{2,1,0:T(8,128)(2,1)S(1)}, bf16[2,64,896]{2,1,0:T(8,128)(2,1)S(1)}, u32[]{:S(2)}, u32[]{:S(2)}) %collective-permute-start.15) | collective-permute-done | bytes 229408 | tf_op jit(solution)/shard_map/ppermute | solution.py:64
  111.6 2.4 collective-permute-done.16
  114.5 2.5 %collective-permute-done.17 = bf16[4,2,64,896]{3,2,1,0:T(8,128)(2,1)S(1)} collective-permute-done((bf16[4,2,64,896]{3,2,1,0:T(8,128)(2,1)S(1)}, bf16[4,2,64,896]{3,2,1,0:T(8,128)(2,1)S(1)}, u32[]{:S(2)}, u32[]{:S(2)}) %collective-permute-start.17) | collective-permute-done | bytes 917536 | tf_op jit(solution)/shard_map/ppermute | solution.py:64
  119.0 4.3 %convolution_convert_fusion.1 = bf16[1024,1152]{1,0:T(8,128)(2,1)S(1)} fusion(bf16[1024,896]{1,0:T(8,128)(2,1)} %bitcast.210, bf16[896,1152]{1,0:T(8,128)(2,1)S(1)} %copy-done), kind=kOutput, calls=%fused_computation.1 | convolution fusion | flops 2115108864 | bytes 6258688 | tf_op jit(solution)/shard_map/dot_general | solution.py:158
  124.2 2.0 collective-permute-start.19
  126.3 2.6 %collective-permute-start.20 = (bf16[2,128,1280]{2,1,0:T(8,128)(2,1)S(1)}, bf16[2,128,1280]{2,1,0:T(8,128)(2,1)S(1)}, u32[]{:S(2)}, u32[]{:S(2)}) collective-permute-start(bf16[2,128,1280]{2,1,0:T(8,128)(2,1)S(1)} %get-tuple-element.6), channel_id=1, source_target_pairs={{0,3},{1,2},{2,1},{3,0},{4,7},{5,6},{6,5},{7,4},{8,11},{9,10},{10,... | collective-permute-start | bytes 1966088 | tf_op jit(solution)/shard_map/ppermute | solution.py:68
  128.9 3.0 %convolution_convert_fusion = bf16[1024,1152]{1,0:T(8,128)(2,1)S(1)} fusion(bf16[1024,896]{1,0:T(8,128)(2,1)S(1)} %bitcast.211, bf16[896,1152]{1,0:T(8,128)(2,1)S(1)} %copy-done.10), kind=kOutput, calls=%fused_computation | convolution fusion | flops 2115108864 | bytes 6258688 | tf_op jit(solution)/shard_map/dot_general | solution.py:159
  133.4 8.3 %collective-permute-done.18 = bf16[2,128,1280]{2,1,0:T(8,128)(2,1)S(1)} collective-permute-done((bf16[2,128,1280]{2,1,0:T(8,128)(2,1)S(1)}, bf16[2,128,1280]{2,1,0:T(8,128)(2,1)S(1)}, u32[]{:S(2)}, u32[]{:S(2)}) %collective-permute-start.18) | collective-permute-done | bytes 655392 | tf_op jit(solution)/shard_map/ppermute | solution.py:68
  141.8 13.4 %collective-permute-done.19 = bf16[2,128,1280]{2,1,0:T(8,128)(2,1)S(1)} collective-permute-done((bf16[2,128,1280]{2,1,0:T(8,128)(2,1)S(1)}, bf16[2,128,1280]{2,1,0:T(8,128)(2,1)S(1)}, u32[]{:S(2)}, u32[]{:S(2)}) %collective-permute-start.19) | collective-permute-done | bytes 655392 | tf_op jit(solution)/shard_map/ppermute | solution.py:68
  155.1 2.6 %collective-permute-done.20 = bf16[2,128,1280]{2,1,0:T(8,128)(2,1)S(1)} collective-permute-done((bf16[2,128,1280]{2,1,0:T(8,128)(2,1)S(1)}, bf16[2,128,1280]{2,1,0:T(8,128)(2,1)S(1)}, u32[]{:S(2)}, u32[]{:S(2)}) %collective-permute-start.20) | collective-permute-done | bytes 655392 | tf_op jit(solution)/shard_map/ppermute | solution.py:68
  160.2 3.5 %collective-permute-start.24 = (bf16[128,1152]{1,0:T(8,128)(2,1)S(1)}, bf16[128,1152]{1,0:T(8,128)(2,1)S(1)}, u32[]{:S(2)}, u32[]{:S(2)}) collective-permute-start(bf16[128,1152]{1,0:T(8,128)(2,1)S(1)} %get-tuple-element.12), channel_id=1, source_target_pairs={{0,2},{1,3},{2,0},{3,1},{4,6},{5,7},{6,4},{7,5},{8,10},{9,11},{10,... | collective-permute-start | bytes 884744 | tf_op jit(solution)/shard_map/ppermute | solution.py:68
  166.8 3.3 %collective-permute-done.23 = bf16[128,1152]{1,0:T(8,128)(2,1)S(1)} collective-permute-done((bf16[128,1152]{1,0:T(8,128)(2,1)S(1)}, bf16[128,1152]{1,0:T(8,128)(2,1)S(1)}, u32[]{:S(2)}, u32[]{:S(2)}) %collective-permute-start.23) | collective-permute-done | bytes 294944 | tf_op jit(solution)/shard_map/ppermute | solution.py:68
  170.1 5.3 %collective-permute-done.24 = bf16[128,1152]{1,0:T(8,128)(2,1)S(1)} collective-permute-done((bf16[128,1152]{1,0:T(8,128)(2,1)S(1)}, bf16[128,1152]{1,0:T(8,128)(2,1)S(1)}, u32[]{:S(2)}, u32[]{:S(2)}) %collective-permute-start.24) | collective-permute-done | bytes 294944 | tf_op jit(solution)/shard_map/ppermute | solution.py:68
  175.4 2.6 %collective-permute-done.25 = bf16[128,1152]{1,0:T(8,128)(2,1)S(1)} collective-permute-done((bf16[128,1152]{1,0:T(8,128)(2,1)S(1)}, bf16[128,1152]{1,0:T(8,128)(2,1)S(1)}, u32[]{:S(2)}, u32[]{:S(2)}) %collective-permute-start.25) | collective-permute-done | bytes 294944 | tf_op jit(solution)/shard_map/ppermute | solution.py:68
  179.6 4.2 %collective-permute-done.26 = bf16[128,640]{1,0:T(8,128)(2,1)S(1)} collective-permute-done((bf16[128,640]{1,0:T(8,128)(2,1)S(1)}, bf16[128,640]{1,0:T(8,128)(2,1)S(1)}, u32[]{:S(2)}, u32[]{:S(2)}) %collective-permute-start.26) | collective-permute-done | bytes 163872 | tf_op jit(solution)/shard_map/ppermute | solution.py:68
  183.9 2.5 %collective-permute-start.28 = (bf16[2,128,640]{2,1,0:T(8,128)(2,1)S(1)}, bf16[2,128,640]{2,1,0:T(8,128)(2,1)S(1)}, u32[]{:S(2)}, u32[]{:S(2)}) collective-permute-start(bf16[2,128,640]{2,1,0:T(8,128)(2,1)S(1)} %get-tuple-element.26), channel_id=1, source_target_pairs={{0,2},{1,3},{2,0},{3,1},{4,6},{5,7},{6,4},{7,5},{8,10},{9,11},{10,... | collective-permute-start | bytes 983048 | tf_op jit(solution)/shard_map/ppermute | solution.py:68
  186.4 2.2 collective-permute-start.29
  190.1 11.8 %collective-permute-done.31 = bf16[128,512]{1,0:T(8,128)(2,1)S(1)} collective-permute-done((bf16[128,512]{1,0:T(8,128)(2,1)S(1)}, bf16[128,512]{1,0:T(8,128)(2,1)S(1)}, u32[]{:S(2)}, u32[]{:S(2)}) %collective-permute-start.31) | collective-permute-done | bytes 131104 | tf_op jit(solution)/shard_map/ppermute | solution.py:68
  201.9 4.2 %collective-permute-done.32 = bf16[128,512]{1,0:T(8,128)(2,1)S(1)} collective-permute-done((bf16[128,512]{1,0:T(8,128)(2,1)S(1)}, bf16[128,512]{1,0:T(8,128)(2,1)S(1)}, u32[]{:S(2)}, u32[]{:S(2)}) %collective-permute-start.32) | collective-permute-done | bytes 131104 | tf_op jit(solution)/shard_map/ppermute | solution.py:68
  211.2 5.6 %collective-permute-done.33 = bf16[4,128,512]{2,1,0:T(8,128)(2,1)S(1)} collective-permute-done((bf16[4,128,512]{2,1,0:T(8,128)(2,1)S(1)}, bf16[4,128,512]{2,1,0:T(8,128)(2,1)S(1)}, u32[]{:S(2)}, u32[]{:S(2)}) %collective-permute-start.33) | collective-permute-done | bytes 524320 | tf_op jit(solution)/shard_map/ppermute | solution.py:68
  218.5 2.5 %collective-permute-done.34 = bf16[4,2,64,896]{3,2,1,0:T(8,128)(2,1)S(1)} collective-permute-done((bf16[4,2,64,896]{3,2,1,0:T(8,128)(2,1)S(1)}, bf16[4,2,64,896]{3,2,1,0:T(8,128)(2,1)S(1)}, u32[]{:S(2)}, u32[]{:S(2)}) %collective-permute-start.34) | collective-permute-done | bytes 917536 | tf_op jit(solution)/shard_map/ppermute | solution.py:64
  221.4 2.5 %collective-permute-start.36 = (bf16[2,64,896]{2,1,0:T(8,128)(2,1)S(1)}, bf16[2,64,896]{2,1,0:T(8,128)(2,1)S(1)}, u32[]{:S(2)}, u32[]{:S(2)}) collective-permute-start(bf16[2,64,896]{2,1,0:T(8,128)(2,1)S(1)} %get-tuple-element.15), channel_id=1, source_target_pairs={{0,32},{8,40},{16,48},{24,56},{32,0},{40,8},{48,16},{56,24},{64,96... | collective-permute-start | bytes 688136 | tf_op jit(solution)/shard_map/ppermute | solution.py:64
  223.8 2.2 collective-permute-start.37
  226.1 3.7 %collective-permute-done.35 = bf16[2,64,896]{2,1,0:T(8,128)(2,1)S(1)} collective-permute-done((bf16[2,64,896]{2,1,0:T(8,128)(2,1)S(1)}, bf16[2,64,896]{2,1,0:T(8,128)(2,1)S(1)}, u32[]{:S(2)}, u32[]{:S(2)}) %collective-permute-start.35) | collective-permute-done | bytes 229408 | tf_op jit(solution)/shard_map/ppermute | solution.py:64
  229.8 4.7 %collective-permute-done.36 = bf16[2,64,896]{2,1,0:T(8,128)(2,1)S(1)} collective-permute-done((bf16[2,64,896]{2,1,0:T(8,128)(2,1)S(1)}, bf16[2,64,896]{2,1,0:T(8,128)(2,1)S(1)}, u32[]{:S(2)}, u32[]{:S(2)}) %collective-permute-start.36) | collective-permute-done | bytes 229408 | tf_op jit(solution)/shard_map/ppermute | solution.py:64
  234.5 2.6 %collective-permute-done.37 = bf16[2,64,896]{2,1,0:T(8,128)(2,1)S(1)} collective-permute-done((bf16[2,64,896]{2,1,0:T(8,128)(2,1)S(1)}, bf16[2,64,896]{2,1,0:T(8,128)(2,1)S(1)}, u32[]{:S(2)}, u32[]{:S(2)}) %collective-permute-start.37) | collective-permute-done | bytes 229408 | tf_op jit(solution)/shard_map/ppermute | solution.py:64
  237.2 1.9 collective-permute-start.38
  239.1 4.5 %collective-permute-done.38 = bf16[64,896]{1,0:T(8,128)(2,1)S(1)} collective-permute-done((bf16[64,896]{1,0:T(8,128)(2,1)S(1)}, bf16[64,896]{1,0:T(8,128)(2,1)S(1)}, u32[]{:S(2)}, u32[]{:S(2)}) %collective-permute-start.38) | collective-permute-done | bytes 114720 | tf_op jit(solution)/shard_map/ppermute | solution.py:64
  (123 shorter events, 44.1 us)
Async XLA Ops:
  0.0 119.0 %copy-start = (bf16[896,1152]{1,0:T(8,128)(2,1)S(1)}, bf16[896,1152]{1,0:T(8,128)(2,1)}, u32[]{:S(2)}) copy-start(bf16[896,1152]{1,0:T(8,128)(2,1)} %param.17) | copy-start | bytes 6193156
  0.9 2.8 %copy-start.2 = (bf16[2,4,1536,256]{3,2,1,0:T(8,128)(2,1)S(1)}, bf16[2,4,1536,256]{3,2,1,0:T(8,128)(2,1)}, u32[]{:S(2)}) copy-start(bf16[2,4,1536,256]{3,2,1,0:T(8,128)(2,1)} %param.11) | copy-start | bytes 18874372
  3.7 2.8 %copy-start.3 = (bf16[2,4,1536,256]{3,2,1,0:T(8,128)(2,1)S(1)}, bf16[2,4,1536,256]{3,2,1,0:T(8,128)(2,1)}, u32[]{:S(2)}) copy-start(bf16[2,4,1536,256]{3,2,1,0:T(8,128)(2,1)} %param.12) | copy-start | bytes 18874372
  32.5 5.8 %collective-permute-start = (bf16[16,8,512]{2,1,0:T(8,128)(2,1)S(1)}, bf16[16,8,512]{2,1,0:T(8,128)(2,1)S(1)}, u32[]{:S(2)}, u32[]{:S(2)}) collective-permute-start(bf16[16,8,512]{2,1,0:T(8,128)(2,1)S(1)} %get-tuple-element.34), channel_id=1, source_target_pairs={{0,4},{1,5},{2,6},{3,7},{4,0},{5,1},{6,2},{7,3},{8,12},{9,13},{10,... | collective-permute-start | bytes 393224 | tf_op jit(solution)/shard_map/ppermute | solution.py:68
  33.6 9.3 %collective-permute-start.4 = (bf16[16,8,512]{2,1,0:T(8,128)(2,1)S(1)}, bf16[16,8,512]{2,1,0:T(8,128)(2,1)S(1)}, u32[]{:S(2)}, u32[]{:S(2)}) collective-permute-start(bf16[16,8,512]{2,1,0:T(8,128)(2,1)S(1)} %get-tuple-element.33), channel_id=1, source_target_pairs={{0,1},{1,0},{2,3},{3,2},{4,5},{5,4},{6,7},{7,6},{8,9},{9,8},{10,11... | collective-permute-start | bytes 393224 | tf_op jit(solution)/shard_map/ppermute | solution.py:68
  35.2 10.1 %collective-permute-start.5 = (bf16[16,8,512]{2,1,0:T(8,128)(2,1)S(1)}, bf16[16,8,512]{2,1,0:T(8,128)(2,1)S(1)}, u32[]{:S(2)}, u32[]{:S(2)}) collective-permute-start(bf16[16,8,512]{2,1,0:T(8,128)(2,1)S(1)} %get-tuple-element.33), channel_id=1, source_target_pairs={{0,2},{1,3},{2,0},{3,1},{4,6},{5,7},{6,4},{7,5},{8,10},{9,11},{10,... | collective-permute-start | bytes 393224 | tf_op jit(solution)/shard_map/ppermute | solution.py:68
  38.1 8.1 %collective-permute-start.6 = (bf16[16,8,512]{2,1,0:T(8,128)(2,1)S(1)}, bf16[16,8,512]{2,1,0:T(8,128)(2,1)S(1)}, u32[]{:S(2)}, u32[]{:S(2)}) collective-permute-start(bf16[16,8,512]{2,1,0:T(8,128)(2,1)S(1)} %get-tuple-element.33), channel_id=1, source_target_pairs={{0,3},{1,2},{2,1},{3,0},{4,7},{5,6},{6,5},{7,4},{8,11},{9,10},{10,... | collective-permute-start | bytes 393224 | tf_op jit(solution)/shard_map/ppermute | solution.py:68
  38.3 10.0 %collective-permute-start.1 = (bf16[2,16,8,512]{3,2,1,0:T(8,128)(2,1)S(1)}, bf16[2,16,8,512]{3,2,1,0:T(8,128)(2,1)}, u32[]{:S(2)}, u32[]{:S(2)}) collective-permute-start(bf16[2,16,8,512]{3,2,1,0:T(8,128)(2,1)S(1)} %get-tuple-element.36), channel_id=1, source_target_pairs={{0,1},{1,0},{2,3},{3,2},{4,5},{5,4},{6,7},{7,6},{8,9},{9,8},{10,11... | collective-permute-start | bytes 786440 | tf_op jit(solution)/shard_map/ppermute | solution.py:68
  39.4 15.8 %collective-permute-start.2 = (bf16[2,16,8,512]{3,2,1,0:T(8,128)(2,1)S(1)}, bf16[2,16,8,512]{3,2,1,0:T(8,128)(2,1)}, u32[]{:S(2)}, u32[]{:S(2)}) collective-permute-start(bf16[2,16,8,512]{3,2,1,0:T(8,128)(2,1)S(1)} %get-tuple-element.36), channel_id=1, source_target_pairs={{0,2},{1,3},{2,0},{3,1},{4,6},{5,7},{6,4},{7,5},{8,10},{9,11},{10,... | collective-permute-start | bytes 786440 | tf_op jit(solution)/shard_map/ppermute | solution.py:68
  42.9 14.1 %collective-permute-start.3 = (bf16[2,16,8,512]{3,2,1,0:T(8,128)(2,1)S(1)}, bf16[2,16,8,512]{3,2,1,0:T(8,128)(2,1)}, u32[]{:S(2)}, u32[]{:S(2)}) collective-permute-start(bf16[2,16,8,512]{3,2,1,0:T(8,128)(2,1)S(1)} %get-tuple-element.36), channel_id=1, source_target_pairs={{0,3},{1,2},{2,1},{3,0},{4,7},{5,6},{6,5},{7,4},{8,11},{9,10},{10,... | collective-permute-start | bytes 786440 | tf_op jit(solution)/shard_map/ppermute | solution.py:68
  47.1 12.9 %collective-permute-start.7 = (bf16[4,16,8,512]{3,2,1,0:T(8,128)(2,1)}, bf16[4,16,8,512]{3,2,1,0:T(8,128)(2,1)}, u32[]{:S(2)}, u32[]{:S(2)}) collective-permute-start(bf16[4,16,8,512]{3,2,1,0:T(8,128)(2,1)} %get-tuple-element.24), channel_id=1, source_target_pairs={{0,4},{1,5},{2,6},{3,7},{4,0},{5,1},{6,2},{7,3},{8,12},{9,13},{10,... | collective-permute-start | bytes 1572872 | tf_op jit(solution)/shard_map/ppermute | solution.py:68
  57.0 1.7 copy-start.6
  64.8 5.2 %collective-permute-start.8 = (bf16[8,64,896]{2,1,0:T(8,128)(2,1)}, bf16[8,64,896]{2,1,0:T(8,128)(2,1)S(1)}, u32[]{:S(2)}, u32[]{:S(2)}) collective-permute-start(bf16[8,64,896]{2,1,0:T(8,128)(2,1)} %dynamic-slice_bitcast_fusion), channel_id=1, source_target_pairs={{0,8},{8,0},{16,24},{24,16},{32,40},{40,32},{48,56},{56,48},{64,72... | collective-permute-start | bytes 2752520 | tf_op jit(solution)/shard_map/ppermute | solution.py:64
  71.4 16.8 %copy-start.9 = (bf16[896]{0:T(1024)(128)(2,1)S(1)}, bf16[896]{0:T(1024)(128)(2,1)}, u32[]{:S(2)}) copy-start(bf16[896]{0:T(1024)(128)(2,1)} %param.15) | copy-start | bytes 5380
  71.5 10.0 %collective-permute-start.10 = (bf16[2,64,896]{2,1,0:T(8,128)(2,1)S(1)}, bf16[2,64,896]{2,1,0:T(8,128)(2,1)S(1)}, u32[]{:S(2)}, u32[]{:S(2)}) collective-permute-start(bf16[2,64,896]{2,1,0:T(8,128)(2,1)S(1)} %get-tuple-element.20), channel_id=1, source_target_pairs={{0,32},{8,40},{16,48},{24,56},{32,0},{40,8},{48,16},{56,24},{64,96... | collective-permute-start | bytes 688136 | tf_op jit(solution)/shard_map/ppermute | solution.py:64
  73.9 12.2 %collective-permute-start.11 = (bf16[2,64,896]{2,1,0:T(8,128)(2,1)S(1)}, bf16[2,64,896]{2,1,0:T(8,128)(2,1)S(1)}, u32[]{:S(2)}, u32[]{:S(2)}) collective-permute-start(bf16[2,64,896]{2,1,0:T(8,128)(2,1)S(1)} %get-tuple-element.19), channel_id=1, source_target_pairs={{0,48},{8,56},{16,32},{24,40},{32,16},{40,24},{48,0},{56,8},{64,11... | collective-permute-start | bytes 688136 | tf_op jit(solution)/shard_map/ppermute | solution.py:64
  75.9 10.2 %collective-permute-start.9 = (bf16[2,64,896]{2,1,0:T(8,128)(2,1)S(1)}, bf16[2,64,896]{2,1,0:T(8,128)(2,1)S(1)}, u32[]{:S(2)}, u32[]{:S(2)}) collective-permute-start(bf16[2,64,896]{2,1,0:T(8,128)(2,1)S(1)} %get-tuple-element.18), channel_id=1, source_target_pairs={{0,16},{8,24},{16,0},{24,8},{32,48},{40,56},{48,32},{56,40},{64,80... | collective-permute-start | bytes 688136 | tf_op jit(solution)/shard_map/ppermute | solution.py:64
  86.2 6.7 %collective-permute-start.12 = (bf16[64,896]{1,0:T(8,128)(2,1)S(1)}, bf16[64,896]{1,0:T(8,128)(2,1)S(1)}, u32[]{:S(2)}, u32[]{:S(2)}) collective-permute-start(bf16[64,896]{1,0:T(8,128)(2,1)S(1)} %dynamic-slice_bitcast_fusion.4), channel_id=1, source_target_pairs={{0,64},{8,72},{16,80},{24,88},{32,96},{40,104},{48,112},{56,120},{... | collective-permute-start | bytes 344072 | tf_op jit(solution)/shard_map/ppermute | solution.py:64
  92.9 6.4 %collective-permute-start.13 = (bf16[64,896]{1,0:T(8,128)(2,1)S(1)}, bf16[64,896]{1,0:T(8,128)(2,1)S(1)}, u32[]{:S(2)}, u32[]{:S(2)}) collective-permute-start(bf16[64,896]{1,0:T(8,128)(2,1)S(1)} %multiply_convert_fusion), channel_id=1, source_target_pairs={{0,64},{8,72},{16,80},{24,88},{32,96},{40,104},{48,112},{56,120},{... | collective-permute-start | bytes 344072 | tf_op jit(solution)/shard_map/ppermute | solution.py:64
  99.3 8.1 %collective-permute-start.14 = (bf16[2,64,896]{2,1,0:T(8,128)(2,1)S(1)}, bf16[2,64,896]{2,1,0:T(8,128)(2,1)S(1)}, u32[]{:S(2)}, u32[]{:S(2)}) collective-permute-start(bf16[2,64,896]{2,1,0:T(8,128)(2,1)S(1)} %get-tuple-element.38), channel_id=1, source_target_pairs={{0,16},{8,24},{16,0},{24,8},{32,48},{40,56},{48,32},{56,40},{64,80... | collective-permute-start | bytes 688136 | tf_op jit(solution)/shard_map/ppermute | solution.py:64
  100.4 11.2 %collective-permute-start.15 = (bf16[2,64,896]{2,1,0:T(8,128)(2,1)S(1)}, bf16[2,64,896]{2,1,0:T(8,128)(2,1)S(1)}, u32[]{:S(2)}, u32[]{:S(2)}) collective-permute-start(bf16[2,64,896]{2,1,0:T(8,128)(2,1)S(1)} %get-tuple-element.38), channel_id=1, source_target_pairs={{0,32},{8,40},{16,48},{24,56},{32,0},{40,8},{48,16},{56,24},{64,96... | collective-permute-start | bytes 688136 | tf_op jit(solution)/shard_map/ppermute | solution.py:64
  103.1 10.9 %collective-permute-start.16 = (bf16[2,64,896]{2,1,0:T(8,128)(2,1)S(1)}, bf16[2,64,896]{2,1,0:T(8,128)(2,1)S(1)}, u32[]{:S(2)}, u32[]{:S(2)}) collective-permute-start(bf16[2,64,896]{2,1,0:T(8,128)(2,1)S(1)} %get-tuple-element.38), channel_id=1, source_target_pairs={{0,48},{8,56},{16,32},{24,40},{32,16},{40,24},{48,0},{56,8},{64,11... | collective-permute-start | bytes 688136 | tf_op jit(solution)/shard_map/ppermute | solution.py:64
  114.2 2.7 %collective-permute-start.17 = (bf16[4,2,64,896]{3,2,1,0:T(8,128)(2,1)S(1)}, bf16[4,2,64,896]{3,2,1,0:T(8,128)(2,1)S(1)}, u32[]{:S(2)}, u32[]{:S(2)}) collective-permute-start(bf16[4,2,64,896]{3,2,1,0:T(8,128)(2,1)S(1)} %get-tuple-element.17), channel_id=1, source_target_pairs={{0,8},{8,0},{16,24},{24,16},{32,40},{40,32},{48,56},{56,48},{64,72... | collective-permute-start | bytes 2752520 | tf_op jit(solution)/shard_map/ppermute | solution.py:64
  123.9 4.9 %copy-start.7 = (bf16[2,4,2,64,896]{4,3,2,1,0:T(8,128)(2,1)S(1)}, bf16[2,4,2,64,896]{4,3,2,1,0:T(8,128)(2,1)}, u32[]{:S(2)}) copy-start(bf16[2,4,2,64,896]{4,3,2,1,0:T(8,128)(2,1)} %pad_maximum_fusion.1) | copy-start | bytes 5505028
  124.0 4.9 %copy-start.10 = (bf16[896,1152]{1,0:T(8,128)(2,1)S(1)}, bf16[896,1152]{1,0:T(8,128)(2,1)}, u32[]{:S(2)}) copy-start(bf16[896,1152]{1,0:T(8,128)(2,1)} %param.18) | copy-start | bytes 6193156
  124.1 17.7 %collective-permute-start.18 = (bf16[2,128,1280]{2,1,0:T(8,128)(2,1)S(1)}, bf16[2,128,1280]{2,1,0:T(8,128)(2,1)S(1)}, u32[]{:S(2)}, u32[]{:S(2)}) collective-permute-start(bf16[2,128,1280]{2,1,0:T(8,128)(2,1)S(1)} %get-tuple-element.5), channel_id=1, source_target_pairs={{0,1},{1,0},{2,3},{3,2},{4,5},{5,4},{6,7},{7,6},{8,9},{9,8},{10,11... | collective-permute-start | bytes 1966088 | tf_op jit(solution)/shard_map/ppermute | solution.py:68
  124.2 30.9 %collective-permute-start.19 = (bf16[2,128,1280]{2,1,0:T(8,128)(2,1)S(1)}, bf16[2,128,1280]{2,1,0:T(8,128)(2,1)S(1)}, u32[]{:S(2)}, u32[]{:S(2)}) collective-permute-start(bf16[2,128,1280]{2,1,0:T(8,128)(2,1)S(1)} %get-tuple-element.7), channel_id=1, source_target_pairs={{0,2},{1,3},{2,0},{3,1},{4,6},{5,7},{6,4},{7,5},{8,10},{9,11},{10,... | collective-permute-start | bytes 1966088 | tf_op jit(solution)/shard_map/ppermute | solution.py:68
  126.3 31.5 %collective-permute-start.20 = (bf16[2,128,1280]{2,1,0:T(8,128)(2,1)S(1)}, bf16[2,128,1280]{2,1,0:T(8,128)(2,1)S(1)}, u32[]{:S(2)}, u32[]{:S(2)}) collective-permute-start(bf16[2,128,1280]{2,1,0:T(8,128)(2,1)S(1)} %get-tuple-element.6), channel_id=1, source_target_pairs={{0,3},{1,2},{2,1},{3,0},{4,7},{5,6},{6,5},{7,4},{8,11},{9,10},{10,... | collective-permute-start | bytes 1966088 | tf_op jit(solution)/shard_map/ppermute | solution.py:68
  132.3 27.4 %collective-permute-start.22 = (bf16[4,128,1152]{2,1,0:T(8,128)(2,1)S(1)}, bf16[4,128,1152]{2,1,0:T(8,128)(2,1)S(1)}, u32[]{:S(2)}, u32[]{:S(2)}) collective-permute-start(bf16[4,128,1152]{2,1,0:T(8,128)(2,1)S(1)} %slice_bitcast_fusion), channel_id=1, source_target_pairs={{0,4},{1,5},{2,6},{3,7},{4,0},{5,1},{6,2},{7,3},{8,12},{9,13},{10,... | collective-permute-start | bytes 3538952 | tf_op jit(solution)/shard_map/ppermute | solution.py:68
  158.1 8.5 %collective-permute-start.21 = (bf16[128,1280]{1,0:T(8,128)(2,1)S(1)}, bf16[128,1280]{1,0:T(8,128)(2,1)S(1)}, u32[]{:S(2)}, u32[]{:S(2)}) collective-permute-start(bf16[128,1280]{1,0:T(8,128)(2,1)S(1)} %slice_bitcast_fusion.6), channel_id=1, source_target_pairs={{0,4},{1,5},{2,6},{3,7},{4,0},{5,1},{6,2},{7,3},{8,12},{9,13},{10,... | collective-permute-start | bytes 983048 | tf_op jit(solution)/shard_map/ppermute | solution.py:68
  160.1 10.0 %collective-permute-start.23 = (bf16[128,1152]{1,0:T(8,128)(2,1)S(1)}, bf16[128,1152]{1,0:T(8,128)(2,1)S(1)}, u32[]{:S(2)}, u32[]{:S(2)}) collective-permute-start(bf16[128,1152]{1,0:T(8,128)(2,1)S(1)} %get-tuple-element.10), channel_id=1, source_target_pairs={{0,1},{1,0},{2,3},{3,2},{4,5},{5,4},{6,7},{7,6},{8,9},{9,8},{10,11... | collective-permute-start | bytes 884744 | tf_op jit(solution)/shard_map/ppermute | solution.py:68
  160.2 15.2 %collective-permute-start.24 = (bf16[128,1152]{1,0:T(8,128)(2,1)S(1)}, bf16[128,1152]{1,0:T(8,128)(2,1)S(1)}, u32[]{:S(2)}, u32[]{:S(2)}) collective-permute-start(bf16[128,1152]{1,0:T(8,128)(2,1)S(1)} %get-tuple-element.12), channel_id=1, source_target_pairs={{0,2},{1,3},{2,0},{3,1},{4,6},{5,7},{6,4},{7,5},{8,10},{9,11},{10,... | collective-permute-start | bytes 884744 | tf_op jit(solution)/shard_map/ppermute | solution.py:68
  163.7 14.3 %collective-permute-start.25 = (bf16[128,1152]{1,0:T(8,128)(2,1)S(1)}, bf16[128,1152]{1,0:T(8,128)(2,1)S(1)}, u32[]{:S(2)}, u32[]{:S(2)}) collective-permute-start(bf16[128,1152]{1,0:T(8,128)(2,1)S(1)} %get-tuple-element.11), channel_id=1, source_target_pairs={{0,3},{1,2},{2,1},{3,0},{4,7},{5,6},{6,5},{7,4},{8,11},{9,10},{10,... | collective-permute-start | bytes 884744 | tf_op jit(solution)/shard_map/ppermute | solution.py:68
  178.3 5.4 %collective-permute-start.26 = (bf16[128,640]{1,0:T(8,128)(2,1)S(1)}, bf16[128,640]{1,0:T(8,128)(2,1)S(1)}, u32[]{:S(2)}, u32[]{:S(2)}) collective-permute-start(bf16[128,640]{1,0:T(8,128)(2,1)S(1)} %get-tuple-element.30), channel_id=1, source_target_pairs={{0,4},{1,5},{2,6},{3,7},{4,0},{5,1},{6,2},{7,3},{8,12},{9,13},{10,... | collective-permute-start | bytes 491528 | tf_op jit(solution)/shard_map/ppermute | solution.py:68
  179.5 9.1 %collective-permute-start.30 = (bf16[128,512]{1,0:T(8,128)(2,1)S(1)}, bf16[128,512]{1,0:T(8,128)(2,1)S(1)}, u32[]{:S(2)}, u32[]{:S(2)}) collective-permute-start(bf16[128,512]{1,0:T(8,128)(2,1)S(1)} %get-tuple-element.28), channel_id=1, source_target_pairs={{0,1},{1,0},{2,3},{3,2},{4,5},{5,4},{6,7},{7,6},{8,9},{9,8},{10,11... | collective-permute-start | bytes 393224 | tf_op jit(solution)/shard_map/ppermute | solution.py:68
  183.8 23.7 %collective-permute-start.27 = (bf16[2,128,640]{2,1,0:T(8,128)(2,1)S(1)}, bf16[2,128,640]{2,1,0:T(8,128)(2,1)S(1)}, u32[]{:S(2)}, u32[]{:S(2)}) collective-permute-start(bf16[2,128,640]{2,1,0:T(8,128)(2,1)S(1)} %get-tuple-element.26), channel_id=1, source_target_pairs={{0,1},{1,0},{2,3},{3,2},{4,5},{5,4},{6,7},{7,6},{8,9},{9,8},{10,11... | collective-permute-start | bytes 983048 | tf_op jit(solution)/shard_map/ppermute | solution.py:68
  183.9 23.6 %collective-permute-start.28 = (bf16[2,128,640]{2,1,0:T(8,128)(2,1)S(1)}, bf16[2,128,640]{2,1,0:T(8,128)(2,1)S(1)}, u32[]{:S(2)}, u32[]{:S(2)}) collective-permute-start(bf16[2,128,640]{2,1,0:T(8,128)(2,1)S(1)} %get-tuple-element.26), channel_id=1, source_target_pairs={{0,2},{1,3},{2,0},{3,1},{4,6},{5,7},{6,4},{7,5},{8,10},{9,11},{10,... | collective-permute-start | bytes 983048 | tf_op jit(solution)/shard_map/ppermute | solution.py:68
  186.4 21.1 %collective-permute-start.29 = (bf16[2,128,640]{2,1,0:T(8,128)(2,1)S(1)}, bf16[2,128,640]{2,1,0:T(8,128)(2,1)S(1)}, u32[]{:S(2)}, u32[]{:S(2)}) collective-permute-start(bf16[2,128,640]{2,1,0:T(8,128)(2,1)S(1)} %get-tuple-element.26), channel_id=1, source_target_pairs={{0,3},{1,2},{2,1},{3,0},{4,7},{5,6},{6,5},{7,4},{8,11},{9,10},{10,... | collective-permute-start | bytes 983048 | tf_op jit(solution)/shard_map/ppermute | solution.py:68
  188.6 13.3 %collective-permute-start.31 = (bf16[128,512]{1,0:T(8,128)(2,1)S(1)}, bf16[128,512]{1,0:T(8,128)(2,1)S(1)}, u32[]{:S(2)}, u32[]{:S(2)}) collective-permute-start(bf16[128,512]{1,0:T(8,128)(2,1)S(1)} %get-tuple-element.28), channel_id=1, source_target_pairs={{0,2},{1,3},{2,0},{3,1},{4,6},{5,7},{6,4},{7,5},{8,10},{9,11},{10,... | collective-permute-start | bytes 393224 | tf_op jit(solution)/shard_map/ppermute | solution.py:68
  188.6 17.5 %collective-permute-start.32 = (bf16[128,512]{1,0:T(8,128)(2,1)S(1)}, bf16[128,512]{1,0:T(8,128)(2,1)S(1)}, u32[]{:S(2)}, u32[]{:S(2)}) collective-permute-start(bf16[128,512]{1,0:T(8,128)(2,1)S(1)} %get-tuple-element.28), channel_id=1, source_target_pairs={{0,3},{1,2},{2,1},{3,0},{4,7},{5,6},{6,5},{7,4},{8,11},{9,10},{10,... | collective-permute-start | bytes 393224 | tf_op jit(solution)/shard_map/ppermute | solution.py:68
  206.2 10.6 %collective-permute-start.33 = (bf16[4,128,512]{2,1,0:T(8,128)(2,1)S(1)}, bf16[4,128,512]{2,1,0:T(8,128)(2,1)S(1)}, u32[]{:S(2)}, u32[]{:S(2)}) collective-permute-start(bf16[4,128,512]{2,1,0:T(8,128)(2,1)S(1)} %get-tuple-element.22), channel_id=1, source_target_pairs={{0,4},{1,5},{2,6},{3,7},{4,0},{5,1},{6,2},{7,3},{8,12},{9,13},{10,... | collective-permute-start | bytes 1572872 | tf_op jit(solution)/shard_map/ppermute | solution.py:68
  207.8 1.6 copy-start.8
  218.4 2.6 %collective-permute-start.34 = (bf16[4,2,64,896]{3,2,1,0:T(8,128)(2,1)S(1)}, bf16[4,2,64,896]{3,2,1,0:T(8,128)(2,1)S(1)}, u32[]{:S(2)}, u32[]{:S(2)}) collective-permute-start(bf16[4,2,64,896]{3,2,1,0:T(8,128)(2,1)S(1)} %bitcast.214), channel_id=1, source_target_pairs={{0,8},{8,0},{16,24},{24,16},{32,40},{40,32},{48,56},{56,48},{64,72... | collective-permute-start | bytes 2752520 | tf_op jit(solution)/shard_map/ppermute | solution.py:64
  221.2 23.4 %copy-start.1 = (bf16[896,1152]{1,0:T(8,128)(2,1)S(1)}, bf16[896,1152]{1,0:T(8,128)(2,1)}, u32[]{:S(2)}) copy-start(bf16[896,1152]{1,0:T(8,128)(2,1)} %param.17) | copy-start | bytes 6193156
  221.3 8.5 %collective-permute-start.35 = (bf16[2,64,896]{2,1,0:T(8,128)(2,1)S(1)}, bf16[2,64,896]{2,1,0:T(8,128)(2,1)S(1)}, u32[]{:S(2)}, u32[]{:S(2)}) collective-permute-start(bf16[2,64,896]{2,1,0:T(8,128)(2,1)S(1)} %get-tuple-element.13), channel_id=1, source_target_pairs={{0,16},{8,24},{16,0},{24,8},{32,48},{40,56},{48,32},{56,40},{64,80... | collective-permute-start | bytes 688136 | tf_op jit(solution)/shard_map/ppermute | solution.py:64
  221.4 13.1 %collective-permute-start.36 = (bf16[2,64,896]{2,1,0:T(8,128)(2,1)S(1)}, bf16[2,64,896]{2,1,0:T(8,128)(2,1)S(1)}, u32[]{:S(2)}, u32[]{:S(2)}) collective-permute-start(bf16[2,64,896]{2,1,0:T(8,128)(2,1)S(1)} %get-tuple-element.15), channel_id=1, source_target_pairs={{0,32},{8,40},{16,48},{24,56},{32,0},{40,8},{48,16},{56,24},{64,96... | collective-permute-start | bytes 688136 | tf_op jit(solution)/shard_map/ppermute | solution.py:64
  223.8 13.2 %collective-permute-start.37 = (bf16[2,64,896]{2,1,0:T(8,128)(2,1)S(1)}, bf16[2,64,896]{2,1,0:T(8,128)(2,1)S(1)}, u32[]{:S(2)}, u32[]{:S(2)}) collective-permute-start(bf16[2,64,896]{2,1,0:T(8,128)(2,1)S(1)} %get-tuple-element.14), channel_id=1, source_target_pairs={{0,48},{8,56},{16,32},{24,40},{32,16},{40,24},{48,0},{56,8},{64,11... | collective-permute-start | bytes 688136 | tf_op jit(solution)/shard_map/ppermute | solution.py:64
  237.2 6.4 %collective-permute-start.38 = (bf16[64,896]{1,0:T(8,128)(2,1)S(1)}, bf16[64,896]{1,0:T(8,128)(2,1)S(1)}, u32[]{:S(2)}, u32[]{:S(2)}) collective-permute-start(bf16[64,896]{1,0:T(8,128)(2,1)S(1)} %slice_bitcast_fusion.16), channel_id=1, source_target_pairs={{0,64},{8,72},{16,80},{24,88},{32,96},{40,104},{48,112},{56,120},{... | collective-permute-start | bytes 344072 | tf_op jit(solution)/shard_map/ppermute | solution.py:64
  (2 other events, 2.2 us)

commit v2 on v1

v2 whole, which is shorter than its diff:
```python
import functools
import math

import jax
import jax.numpy as jnp
from jax import lax
from jax.experimental import pallas as pl
from jax.experimental.pallas import tpu as pltpu
from jax.sharding import PartitionSpec as P

D = 7168
QB = 128
N_ATTN = 16
N_FFN = 8
NQ = 8
NEG = -1e30
BF = jnp.bfloat16
F32 = jnp.float32
MIB = 2**20
PLANES = [[2 * q + c for q in range(NQ)] for c in range(2)]
ORDER = ((1, 3, 4), (3, 4, 1), (4, 1, 3))
NP = len(ORDER)


def attend_kernel(len_ref, q_ref, k_ref, v_ref, o_ref):
    s = pl.program_id(0)
    q = q_ref[0]
    scores = lax.dot_general(
        q, k_ref[0], (((1,), (1,)), ((), ())), preferred_element_type=F32
    ) * (1.0 / math.sqrt(q.shape[1]))
    offsets = lax.broadcasted_iota(jnp.int32, scores.shape, 1)
    scores = jnp.where(offsets < len_ref[s], scores, NEG)
    peak = jnp.max(scores, axis=1, keepdims=True)
    weights = jnp.exp(scores - peak)
    totals = jnp.sum(weights, axis=1, keepdims=True)
    out = jnp.dot(weights.astype(BF), v_ref[0], preferred_element_type=F32) / totals
    for b in range(out.shape[1] // QB):
        block = out[:, b * QB : (b + 1) * QB]
        scale = (jnp.max(jnp.abs(block), axis=1, keepdims=True) + 1e-06).astype(BF).astype(F32)
        levels = jnp.clip(jnp.floor(127.0 * block / scale + 0.5), -127.0, 127.0)
        o_ref[0, :, b * QB : (b + 1) * QB] = (levels * scale / 127.0).astype(BF)


def attend(q, k, v, lengths):
    n, h, hd = q.shape
    l = k.shape[1]
    return pl.pallas_call(
        attend_kernel,
        out_shape=jax.ShapeDtypeStruct((n, h, hd), BF),
        grid_spec=pltpu.PrefetchScalarGridSpec(
            num_scalar_prefetch=1,
            grid=(n,),
            in_specs=[
                pl.BlockSpec((1, h, hd), lambda i, _: (i, 0, 0)),
                pl.BlockSpec((1, l, hd), lambda i, _: (i, 0, 0)),
                pl.BlockSpec((1, l, hd), lambda i, _: (i, 0, 0)),
            ],
            out_specs=pl.BlockSpec((1, h, hd), lambda i, _: (i, 0, 0)),
        ),
        compiler_params=pltpu.CompilerParams(vmem_limit_bytes=58 * MIB),
        cost_estimate=pl.CostEstimate(
            flops=4 * n * h * l * hd, bytes_accessed=4 * n * l * hd, transcendentals=n * h * l
        ),
    )(lengths, q, k, v)


def ax(x, k):
    return lax.ppermute(x, "attn", [(i, i ^ k) for i in range(N_ATTN)])


def fx(x, k):
    return lax.ppermute(x, "ffn", [(i, i ^ k) for i in range(N_FFN)])


def over_chips(x):
    return lax.all_to_all(x, "attn", 0, 0, axis_index_groups=PLANES)


def flip_bits(x, axis, index):
    s = x.shape
    y = x.reshape(s[:axis] + (2, 2, 2) + s[axis + 1 :])
    for b in range(3):
        bit = (index >> (2 - b)) & 1
        y = jnp.where(bit == 1, jnp.flip(y, axis + b), y)
    return y.reshape(s)


def pair_rows(acc, first, second):
    return jnp.concatenate([acc[first : first + 8], acc[second : second + 8]], axis=0).astype(BF)


def column_chunks(width, step=256):
    return [(s, min(step, width - s)) for s in range(0, width, step)]


def project_kernel(core_ref, b0, r1, r2, r3, b1, t1, own_ref, sib_ref, o_ref, x_ref):
    for k, ref in enumerate((b0, r1, r2, r3)):
        for z in range(2):
            j = z * 4 + k
            x_ref[j * 32 : j * 32 + 32, :] = ref[z]
    for z, ref in enumerate((b1, t1)):
        for k in range(4):
            j = z * 4 + k
            x_ref[256 + j * 32 : 256 + j * 32 + 32, :] = ref[k]
    depth = own_ref.shape[0]
    core = core_ref[0]
    mine = x_ref[:, pl.ds(pl.multiple_of(core * depth, depth), depth)]
    other = x_ref[:, pl.ds(pl.multiple_of((1 - core) * depth, depth), depth)]
    for start, size in column_chunks(o_ref.shape[2]):
        cols = slice(start, start + size)
        acc = jnp.dot(mine, own_ref[:, cols], preferred_element_type=F32) + jnp.dot(
            other, sib_ref[:, cols], preferred_element_type=F32
        )
        for q in range(NQ):
            base = (q // 4) * 256 + (q % 4) * 8
            for t in range(4):
                o_ref[q, t * 16 : t * 16 + 16, cols] = pair_rows(
                    acc, base + 2 * t * 32, base + (2 * t + 1) * 32
                )


def vmem_specs(count):
    return [pl.BlockSpec(memory_space=pltpu.VMEM)] * count


def project(core, pieces, own, sib):
    depth, width = own.shape
    rows = NQ * 64
    return pl.pallas_call(
        project_kernel,
        out_shape=jax.ShapeDtypeStruct((NQ, 64, width), BF),
        in_specs=[pl.BlockSpec(memory_space=pltpu.SMEM)] + vmem_specs(8),
        out_specs=pl.BlockSpec(memory_space=pltpu.VMEM),
        scratch_shapes=[pltpu.VMEM((rows, 2 * depth), BF)],
        compiler_params=pltpu.CompilerParams(vmem_limit_bytes=24 * MIB),
        cost_estimate=pl.CostEstimate(
            flops=4 * rows * depth * width, bytes_accessed=6 * 2**20, transcendentals=0
        ),
    )(core.reshape(1), *pieces, own, sib)


def hidden_kernel(order, with_square, full_ref, gain_ref, g0, u0, g1, u1, send_ref, keep_ref):
    step = g0.shape[1]
    full = full_ref[...]

    def put(acc, cols):
        for b0 in range(2):
            ref = send_ref if b0 else keep_ref
            for b1 in range(2):
                for b2 in range(2):
                    j = (b0 * order[0]) ^ (b1 * order[1]) ^ (b2 * order[2])
                    for t in range(4):
                        ref[b1, b2, t * 16 : t * 16 + 16, cols] = pair_rows(
                            acc, 2 * t * 64 + j * 8, (2 * t + 1) * 64 + j * 8
                        )

    for i, w in enumerate((g0, u0, g1, u1)):
        acc = jnp.dot(full, w[...], preferred_element_type=F32)
        put(acc, slice(i * step, (i + 1) * step))
    if with_square:
        ratio = full.astype(F32) / gain_ref[...].astype(F32)
        square = jnp.sum(ratio * ratio, axis=1, keepdims=True)
        put(jnp.broadcast_to(square, (full.shape[0], 128)), slice(4 * step, 4 * step + 128))


def hidden(part, full, gain, weights):
    rows, width = full.shape
    hid = weights[0].shape[1]
    step = hid // NP
    with_square = part == NP - 1
    cols = 4 * step + (128 if with_square else 0)
    shape = jax.ShapeDtypeStruct((2, 2, rows // N_FFN, cols), BF)
    whole = pl.BlockSpec((2, 2, rows // N_FFN, cols), lambda i: (0, 0, 0, 0))
    return pl.pallas_call(
        functools.partial(hidden_kernel, ORDER[part], with_square),
        out_shape=(shape, shape),
        grid=(1,),
        in_specs=[
            pl.BlockSpec((rows, width), lambda i: (0, 0)),
            pl.BlockSpec((1, width), lambda i: (0, 0)),
        ]
        + [pl.BlockSpec((width, step), lambda i: (0, part))] * 4,
        out_specs=(whole, whole),
        compiler_params=pltpu.CompilerParams(vmem_limit_bytes=24 * MIB),
        cost_estimate=pl.CostEstimate(
            flops=2 * rows * width * cols, bytes_accessed=4 * 2**20, transcendentals=0
        ),
    )(full, gain, *weights)


def down_kernel(s0, r0, s1, r1, s2, r2, own_ref, sib_ref, o_ref, x_ref):
    hid = own_ref.shape[0]
    step = hid // NP
    for p, pair in enumerate(((s0, r0), (s1, r1), (s2, r2))):
        o = ORDER[p]
        for b0 in range(2):
            for b1 in range(2):
                for b2 in range(2):
                    j = (b0 * o[0]) ^ (b1 * o[1]) ^ (b2 * o[2])
                    rows = slice(j * 64, j * 64 + 64)
                    x_ref[rows, p * step : (p + 1) * step] = pair[b0][b1, b2, :, :step]
                    x_ref[rows, hid + p * step : hid + (p + 1) * step] = pair[b0][b1, b2, :, step:]
    mine, other = x_ref[:, :hid], x_ref[:, hid:]
    for start, size in column_chunks(o_ref.shape[2]):
        cols = slice(start, start + size)
        acc = jnp.dot(mine, own_ref[:, cols], preferred_element_type=F32) + jnp.dot(
            other, sib_ref[:, cols], preferred_element_type=F32
        )
        for q in range(NQ):
            for t in range(4):
                o_ref[q, t * 16 : t * 16 + 16, cols] = pair_rows(
                    acc, 2 * t * 64 + q * 8, (2 * t + 1) * 64 + q * 8
                )


def down(pieces, own, sib):
    hid, width = own.shape
    rows = NQ * 64
    return pl.pallas_call(
        down_kernel,
        out_shape=jax.ShapeDtypeStruct((NQ, 64, width), BF),
        in_specs=vmem_specs(8),
        out_specs=pl.BlockSpec(memory_space=pltpu.VMEM),
        scratch_shapes=[pltpu.VMEM((rows, 2 * hid), BF)],
        compiler_params=pltpu.CompilerParams(vmem_limit_bytes=24 * MIB),
        cost_estimate=pl.CostEstimate(
            flops=4 * rows * hid * width, bytes_accessed=6 * 2**20, transcendentals=0
        ),
    )(*pieces, own, sib)


def scatter_ffn(sends, keeps):
    f = lambda t: t.astype(F32)
    r1 = [fx(s, o[0]) for s, o in zip(sends, ORDER)]
    s2 = [(f(k[1]) + f(r[1])).astype(BF) for k, r in zip(keeps, r1)]
    r2 = [fx(s, o[1]) for s, o in zip(s2, ORDER)]
    s3 = [(f(k[0, 1]) + f(r[0, 1]) + f(q[1])).astype(BF) for k, r, q in zip(keeps, r1, r2)]
    r3 = [fx(s, o[2]) for s, o in zip(s3, ORDER)]
    return [
        f(k[0, 0]) + f(r[0, 0]) + f(q[0]) + f(t) for k, r, q, t in zip(keeps, r1, r2, r3)
    ]


def gather_ffn(parts):
    s = [jnp.stack([x, fx(x, o[2])]) for x, o in zip(parts, ORDER)]
    s = [jnp.stack([x, fx(x, o[1])]) for x, o in zip(s, ORDER)]
    return [t for x, o in zip(s, ORDER) for t in (x, fx(x, o[0]))]


def local(
    queries,
    cache_keys,
    cache_values,
    lengths,
    residual,
    norm_gain,
    out_weight,
    gate_weight,
    up_weight,
    down_weight,
):
    nm, r = queries.shape[:2]
    n = nm * r
    a = lax.axis_index("attn")
    f = lax.axis_index("ffn")
    core = a % 2
    w = residual.shape[2]
    rows = N_FFN * n

    out_sib = ax(out_weight, 1)
    gate_sib = ax(gate_weight, 1)
    up_sib = ax(up_weight, 1)
    down_sib = ax(down_weight, 1)

    out = attend(
        queries.reshape(n, *queries.shape[2:]),
        cache_keys.reshape(n, *cache_keys.shape[2:]),
        cache_values.reshape(n, *cache_values.shape[2:]),
        lengths.reshape(n),
    )
    got = over_chips(out.reshape(n, NQ, -1).transpose(1, 0, 2)).reshape(NQ * n, -1)

    x0, x1 = got[: rows // 2], got[rows // 2 :]
    b1 = jnp.stack([x1] + [fx(x1, k) for k in range(1, 4)])
    b0 = jnp.stack([x0, fx(x0, 4)])
    pieces = [b0] + [fx(b0, k) for k in range(1, 4)] + [b1, fx(b1, 4)]
    part = project(core, pieces, out_weight, out_sib)
    projected = jnp.sum(over_chips(part).astype(F32), axis=0)

    res = lax.dynamic_slice_in_dim(residual.reshape(nm, N_ATTN, N_FFN, r, w), a, 1, 1)[:, 0]
    res = flip_bits(res, 1, f).transpose(1, 0, 2, 3).reshape(rows, w)
    stream = res.astype(F32) + projected
    scaled = (stream * norm_gain.astype(F32)).astype(BF)
    full = over_chips(jnp.broadcast_to(scaled[None], (NQ, rows, w))).reshape(NQ * rows, w)

    weights = (gate_weight, up_weight, gate_sib, up_sib)
    gain = norm_gain.reshape(1, w)
    sends, keeps = zip(*[hidden(p, full, gain, weights) for p in range(NP)])
    sums = scatter_ffn(sends, keeps)
    step = gate_weight.shape[1] // NP
    inv = lax.rsqrt(sums[-1][:, 4 * step : 4 * step + 1] / D + 1e-06)
    acts = []
    for t in sums:
        g0, u0, g1, u1 = [t[:, i * step : (i + 1) * step] * inv for i in range(4)]
        acts.append(
            jnp.concatenate([jax.nn.silu(g0) * u0, jax.nn.silu(g1) * u1], axis=1).astype(BF)
        )
    part = down(gather_ffn(acts), down_weight, down_sib)
    final = stream + jnp.sum(over_chips(part).astype(F32), axis=0)
    final = final.astype(BF).reshape(N_FFN, nm, r, w)
    return flip_bits(final, 0, f).transpose(1, 0, 2, 3).reshape(nm, N_FFN * r, w)


def solution(mesh):
    in_specs = (
        P(None, ("attn", "ffn"), None, None),
        P(None, ("attn", "ffn"), None, None),
        P(None, ("attn", "ffn"), None, None),
        P(None, ("attn", "ffn")),
        P(None, None, "ffn"),
        P("ffn"),
        P("attn", "ffn"),
        P("ffn", "attn"),
        P("ffn", "attn"),
        P("attn", "ffn"),
    )
    out_specs = P(None, "attn", "ffn")
    return jax.shard_map(local, mesh=mesh, in_specs=in_specs, out_specs=out_specs, check_vma=False)
```

time: 245 us -> 211 us (0.86)
  waiting for transfers between devices: 125 us -> 101 us
  Pallas kernels: 7.7 us -> 31.6 us
  matrix products: 12.8 us -> 0 us
  starting transfers between devices: 52 us -> 43.2 us
  other arithmetic: 9.78 us -> 3.13 us
  local copies, waits for them, and re-layouts: 19.7 us -> 13.4 us
    ppermute x15 -> x4, waiting for transfers between devices: 49.6 us -> 0.01 us  [ax(): return lax.ppermute(x, 'attn', [(i, i ^ k) for i in range(N_ATTN)])]
    all_to_all x0 -> x3, waiting for transfers between devices: none -> 41.5 us  [over_chips(): return lax.all_to_all(x, 'attn', 0, 0, axis_index_groups=PLANES)]
    pallas_call x0 -> x5, Pallas kernels: none -> 19.9 us  [the longest x3 11.1 us: hidden(): pl.pallas_call(functools.partial(hidden_kernel, ORDER[part], with_square)...]
    ppermute x15 -> x4, starting transfers between devices: 19.9 us -> 0.36 us  [ax(): return lax.ppermute(x, 'attn', [(i, i ^ k) for i in range(N_ATTN)])]
    ppermute x24 -> x26, waiting for transfers between devices: 75.5 us -> 59.8 us  [fx(): return lax.ppermute(x, 'ffn', [(i, i ^ k) for i in range(N_FFN)])]
    dot_general x6 -> x0, matrix products: 12.8 us -> none  [the longest x1 4.32 us: half(): gate = jnp.dot(full, wg, preferred_element_type=F32).astype(BF)]
    all_to_all x0 -> x3, starting transfers between devices: none -> 10.8 us  [over_chips(): return lax.all_to_all(x, 'attn', 0, 0, axis_index_groups=PLANES)]
    unnamed x22 -> x10, local copies, waits for them, and re-layouts: 9.48 us -> 3.09 us
  transfers between devices with their start and end apart: 39 -> 33, of which waited for: 30 -> 23; matrix products, arithmetic and copies ran while one was open for 6% -> 6% of each run, Pallas kernels for 0% -> 12%
where the time goes in v2:
time: 211 us; the launch traced here: 210 us
  waiting for transfers between devices  101 us (48%)
  starting transfers between devices  43.2 us (20%)
  Pallas kernels  31.6 us (15%)
  blocking collectives  16.9 us (8%)
  local copies, waits for them, and re-layouts  13.4 us (6%)
  other arithmetic  3.13 us (1%)
    ppermute x26, waiting for transfers between devices, fx(): return lax.ppermute(x, 'ffn', [(i, i ^ k) for i in range(N_FFN)])  59.8 us
    all_to_all x3, waiting for transfers between devices, over_chips(): return lax.all_to_all(x, 'attn', 0, 0, axis_index_groups=PLANES)  41.5 us
    ppermute x26, starting transfers between devices, fx(): return lax.ppermute(x, 'ffn', [(i, i ^ k) for i in range(N_FFN)])  32 us
    all_to_all x1, blocking collectives, over_chips(): return lax.all_to_all(x, 'attn', 0, 0, axis_index_groups=PLANES)  16.9 us
    pallas_call x1, Pallas kernels, attend(): pl.pallas_call(attend_kernel, out_shape=jax.ShapeDtypeStruct((n, h, hd),...  11.6 us
    pallas_call x3, Pallas kernels, hidden(): pl.pallas_call(functools.partial(hidden_kernel, ORDER[part], with_square)...  11.1 us
    all_to_all x3, starting transfers between devices, over_chips(): return lax.all_to_all(x, 'attn', 0, 0, axis_index_groups=PLANES)  10.8 us
    pallas_call x1, Pallas kernels, project(): pl.pallas_call(project_kernel, out_shape=jax.ShapeDtypeStruct((NQ, 64, wi...  5.14 us
  transfers between devices with their start and end apart: 33, of which 23 were waited for; matrix products, arithmetic and copies ran while one was open for 6% of the time, Pallas kernels for 12%

profile of v2, /device:TPU:0, one launch (start us, length us, event | category | flops | bytes accessed | tf_op | source)
XLA Modules:
  0.0 210.0 jit_solution(16701393144507454657)
XLA Ops:
  0.0 1.3 reshape.213.len_ref
  1.3 11.6 %shard_map.100 = bf16[8,64,256]{2,1,0:T(8,128)(2,1)} custom-call(s32[8]{0:T(128)} %reshape.213.len_ref, bf16[8,64,256]{2,1,0:T(8,128)(2,1)} %bitcast.113, bf16[8,1536,256]{2,1,0:T(8,128)(2,1)} %bitcast.100, bf16[8,1536,256]{2,1,0:T(8,128)(2,1)} %bitcast.101), custom_call_target="tpu_custom_call" | custom-call | flops 805306368 | bytes 12582912 | tf_op jit(solution)/shard_map/pallas_call | solution.py:47
  14.2 16.9 %all_to_all.20 = bf16[8,8,2048]{2,1,0:T(8,128)(2,1)S(1)} all-to-all(bf16[8,8,2048]{2,1,0:T(8,128)(2,1)S(1)} %bitcast.103), channel_id=1, replica_groups={{0,16,32,48,64,80,96,112},{8,24,40,56,72,88,104,120},{1,17,33,49,65,81,..., dimensions={0} | all-to-all | bytes 524288 | tf_op jit(solution)/shard_map/all_to_all | solution.py:76
  31.1 1.7 collective-permute-start.4
  32.8 2.9 %collective-permute-start.5 = (bf16[32,2048]{1,0:T(8,128)(2,1)S(1)}, bf16[32,2048]{1,0:T(8,128)(2,1)S(1)}, u32[]{:S(2)}, u32[]{:S(2)}) collective-permute-start(bf16[32,2048]{1,0:T(8,128)(2,1)S(1)} %get-tuple-element.25), channel_id=1, source_target_pairs={{0,2},{1,3},{2,0},{3,1},{4,6},{5,7},{6,4},{7,5},{8,10},{9,11},{10,... | collective-permute-start | bytes 393224 | tf_op jit(solution)/shard_map/ppermute | solution.py:72
  36.9 4.7 %collective-permute-done.5 = bf16[32,2048]{1,0:T(8,128)(2,1)S(1)} collective-permute-done((bf16[32,2048]{1,0:T(8,128)(2,1)S(1)}, bf16[32,2048]{1,0:T(8,128)(2,1)S(1)}, u32[]{:S(2)}, u32[]{:S(2)}) %collective-permute-start.5) | collective-permute-done | bytes 131104 | tf_op jit(solution)/shard_map/ppermute | solution.py:72
  41.7 2.0 collective-permute-done.6
  43.7 1.1 collective-permute-start.7
  45.0 2.1 %collective-permute-start.2 = (bf16[2,32,2048]{2,1,0:T(8,128)(2,1)S(1)}, bf16[2,32,2048]{2,1,0:T(8,128)(2,1)}, u32[]{:S(2)}, u32[]{:S(2)}) collective-permute-start(bf16[2,32,2048]{2,1,0:T(8,128)(2,1)S(1)} %pad_maximum_fusion.4.b0), channel_id=1, source_target_pairs={{0,2},{1,3},{2,0},{3,1},{4,6},{5,7},{6,4},{7,5},{8,10},{9,11},{10,... | collective-permute-start | bytes 786440 | tf_op jit(solution)/shard_map/ppermute | solution.py:72
  47.1 2.6 %collective-permute-start.3 = (bf16[2,32,2048]{2,1,0:T(8,128)(2,1)S(1)}, bf16[2,32,2048]{2,1,0:T(8,128)(2,1)}, u32[]{:S(2)}, u32[]{:S(2)}) collective-permute-start(bf16[2,32,2048]{2,1,0:T(8,128)(2,1)S(1)} %pad_maximum_fusion.4.b0), channel_id=1, source_target_pairs={{0,3},{1,2},{2,1},{3,0},{4,7},{5,6},{6,5},{7,4},{8,11},{9,10},{10,... | collective-permute-start | bytes 786440 | tf_op jit(solution)/shard_map/ppermute | solution.py:72
  49.7 4.1 %reshape.211 = bf16[2,16,8,4,896]{4,3,2,1,0:T(4,128)(2,1)} reshape(bf16[2,512,896]{2,1,0:T(8,128)(2,1)} %param.14) | data formatting | bytes 3670016 | tf_op jit(solution)/shard_map/reshape | solution.py:290
  54.8 3.7 %collective-permute-done.2.r2 = bf16[2,32,2048]{2,1,0:T(8,128)(2,1)} collective-permute-done((bf16[2,32,2048]{2,1,0:T(8,128)(2,1)S(1)}, bf16[2,32,2048]{2,1,0:T(8,128)(2,1)}, u32[]{:S(2)}, u32[]{:S(2)}) %collective-permute-start.2) | collective-permute-done | bytes 262176 | tf_op jit(solution)/shard_map/ppermute | solution.py:72
  58.5 2.6 %collective-permute-done.3.r3 = bf16[2,32,2048]{2,1,0:T(8,128)(2,1)} collective-permute-done((bf16[2,32,2048]{2,1,0:T(8,128)(2,1)S(1)}, bf16[2,32,2048]{2,1,0:T(8,128)(2,1)}, u32[]{:S(2)}, u32[]{:S(2)}) %collective-permute-start.3) | collective-permute-done | bytes 262176 | tf_op jit(solution)/shard_map/ppermute | solution.py:72
  61.1 1.5 copy-done.3
  62.6 5.1 %shard_map.101 = bf16[8,64,896]{2,1,0:T(8,128)(2,1)} custom-call(s32[1]{0:T(128)} %bitcast.4.core_ref, bf16[2,32,2048]{2,1,0:T(8,128)(2,1)S(1)} %pad_maximum_fusion.4.b0, bf16[2,32,2048]{2,1,0:T(8,128)(2,1)} %collective-permute-done.1.r1, bf16[2,32,2048]{2,1,0:T(8,128)(2,1)} %collective-permute-done.2.r2, bf16[2,32,2048]{2,1,0:T(8,128)(2,1)} %collective-permute-done.3.r3, ...), custom_call_target="tpu_custom_call" | custom-call | flops 1879048192 | bytes 6291456 | tf_op jit(solution)/shard_map/pallas_call | solution.py:129
  67.7 3.7 %all-to-all-start.1 = ((bf16[8,64,896]{2,1,0:T(8,128)(2,1)}), bf16[8,64,896]{2,1,0:T(8,128)(2,1)S(1)}, u32[]{:S(2)}, u32[]{:S(2)}) async-start(bf16[8,64,896]{2,1,0:T(8,128)(2,1)} %shard_map.101), calls=%async_computation.1 | async-start | bytes 1835008 | tf_op jit(solution)/shard_map/all_to_all | solution.py:76
  72.4 13.5 %all-to-all-done.1 = bf16[8,64,896]{2,1,0:T(8,128)(2,1)S(1)} async-done(((bf16[8,64,896]{2,1,0:T(8,128)(2,1)}), bf16[8,64,896]{2,1,0:T(8,128)(2,1)S(1)}, u32[]{:S(2)}, u32[]{:S(2)}) %all-to-all-start.1) | async-done | bytes 917536 | tf_op jit(solution)/shard_map/all_to_all | solution.py:76
  87.0 1.1 broadcast_in_dim.2
  88.1 3.6 %all-to-all-start.2 = ((bf16[8,64,896]{2,1,0:T(8,128)(2,1)}), bf16[8,64,896]{2,1,0:T(8,128)(2,1)S(1)}, u32[]{:S(2)}, u32[]{:S(2)}) async-start(bf16[8,64,896]{2,1,0:T(8,128)(2,1)} %broadcast_in_dim.2), calls=%async_computation.2 | async-start | bytes 1835008 | tf_op jit(solution)/shard_map/all_to_all | solution.py:76
  91.7 15.8 %all-to-all-done.2 = bf16[8,64,896]{2,1,0:T(8,128)(2,1)S(1)} async-done(((bf16[8,64,896]{2,1,0:T(8,128)(2,1)}), bf16[8,64,896]{2,1,0:T(8,128)(2,1)S(1)}, u32[]{:S(2)}, u32[]{:S(2)}) %all-to-all-start.2) | async-done | bytes 917536 | tf_op jit(solution)/shard_map/all_to_all | solution.py:76
  107.5 1.6 copy-done.1
  109.1 3.6 %shard_map.104 = (bf16[2,2,64,1536]{3,2,1,0:T(8,128)(2,1)S(1)}, bf16[2,2,64,1536]{3,2,1,0:T(8,128)(2,1)S(1)}) custom-call(bf16[512,896]{1,0:T(8,128)(2,1)S(1)} %bitcast.97, bf16[1,896]{1,0:T(2,128)(2,1)S(1)} %reshape.219.gain_ref, bf16[896,1152]{1,0:T(8,128)(2,1)S(1)} %copy-done, bf16[896,1152]{1,0:T(8,128)(2,1)S(1)} %copy-done.1, ...), custom_call_target="tpu_custom_call" | custom-call | flops 1409286144 | bytes 4194304 | tf_op jit(solution)/shard_map/pallas_call | solution.py:174
  112.8 2.2 %collective-permute-start.20 = (bf16[2,2,64,1536]{3,2,1,0:T(8,128)(2,1)S(1)}, bf16[2,2,64,1536]{3,2,1,0:T(8,128)(2,1)S(1)}, u32[]{:S(2)}, u32[]{:S(2)}) collective-permute-start(bf16[2,2,64,1536]{3,2,1,0:T(8,128)(2,1)S(1)} %get-tuple-element.16), channel_id=1, source_target_pairs={{0,3},{1,2},{2,1},{3,0},{4,7},{5,6},{6,5},{7,4},{8,11},{9,10},{10,... | collective-permute-start | bytes 2359304 | tf_op jit(solution)/shard_map/ppermute | solution.py:72
  115.0 3.7 %shard_map.102 = (bf16[2,2,64,1536]{3,2,1,0:T(8,128)(2,1)S(1)}, bf16[2,2,64,1536]{3,2,1,0:T(8,128)(2,1)S(1)}) custom-call(bf16[512,896]{1,0:T(8,128)(2,1)S(1)} %bitcast.98, bf16[1,896]{1,0:T(2,128)(2,1)S(1)} %reshape.219.gain_ref, bf16[896,1152]{1,0:T(8,128)(2,1)S(1)} %copy-done, bf16[896,1152]{1,0:T(8,128)(2,1)S(1)} %copy-done.1, ...), custom_call_target="tpu_custom_call" | custom-call | flops 1409286144 | bytes 4194304 | tf_op jit(solution)/shard_map/pallas_call | solution.py:174
  119.0 3.8 %shard_map.103 = (bf16[2,2,64,1664]{3,2,1,0:T(8,128)(2,1)S(1)}, bf16[2,2,64,1664]{3,2,1,0:T(8,128)(2,1)S(1)}) custom-call(bf16[512,896]{1,0:T(8,128)(2,1)S(1)} %bitcast.99, bf16[1,896]{1,0:T(2,128)(2,1)S(1)} %reshape.219.gain_ref, bf16[896,1152]{1,0:T(8,128)(2,1)S(1)} %copy-done, bf16[896,1152]{1,0:T(8,128)(2,1)S(1)} %copy-done.1, ...), custom_call_target="tpu_custom_call" | custom-call | flops 1526726656 | bytes 4194304 | tf_op jit(solution)/shard_map/pallas_call | solution.py:174
  123.9 9.3 %collective-permute-done.20 = bf16[2,2,64,1536]{3,2,1,0:T(8,128)(2,1)S(1)} collective-permute-done((bf16[2,2,64,1536]{3,2,1,0:T(8,128)(2,1)S(1)}, bf16[2,2,64,1536]{3,2,1,0:T(8,128)(2,1)S(1)}, u32[]{:S(2)}, u32[]{:S(2)}) %collective-permute-start.20) | collective-permute-done | bytes 786464 | tf_op jit(solution)/shard_map/ppermute | solution.py:72
  134.4 3.2 %collective-permute-done.11 = bf16[2,2,64,1536]{3,2,1,0:T(8,128)(2,1)S(1)} collective-permute-done((bf16[2,2,64,1536]{3,2,1,0:T(8,128)(2,1)S(1)}, bf16[2,2,64,1536]{3,2,1,0:T(8,128)(2,1)S(1)}, u32[]{:S(2)}, u32[]{:S(2)}) %collective-permute-start.11) | collective-permute-done | bytes 786464 | tf_op jit(solution)/shard_map/ppermute | solution.py:72
  137.7 1.2 collective-permute-start.12
  138.9 5.7 %collective-permute-done.14 = bf16[2,2,64,1664]{3,2,1,0:T(8,128)(2,1)S(1)} collective-permute-done((bf16[2,2,64,1664]{3,2,1,0:T(8,128)(2,1)S(1)}, bf16[2,2,64,1664]{3,2,1,0:T(8,128)(2,1)S(1)}, u32[]{:S(2)}, u32[]{:S(2)}) %collective-permute-start.14) | collective-permute-done | bytes 852000 | tf_op jit(solution)/shard_map/ppermute | solution.py:72
  144.7 1.8 collective-permute-start.15
  146.5 6.1 %collective-permute-done.21 = bf16[2,64,1536]{2,1,0:T(8,128)(2,1)S(1)} collective-permute-done((bf16[2,64,1536]{2,1,0:T(8,128)(2,1)S(1)}, bf16[2,64,1536]{2,1,0:T(8,128)(2,1)S(1)}, u32[]{:S(2)}, u32[]{:S(2)}) %collective-permute-start.21) | collective-permute-done | bytes 393248 | tf_op jit(solution)/shard_map/ppermute | solution.py:72
  152.7 1.8 collective-permute-start.22
  154.6 1.1 collective-permute-start.13
  156.6 1.2 collective-permute-start.16
  157.8 2.3 %collective-permute-done.22 = bf16[64,1536]{1,0:T(8,128)(2,1)S(1)} collective-permute-done((bf16[64,1536]{1,0:T(8,128)(2,1)S(1)}, bf16[64,1536]{1,0:T(8,128)(2,1)S(1)}, u32[]{:S(2)}, u32[]{:S(2)}) %collective-permute-start.22) | collective-permute-done | bytes 196640 | tf_op jit(solution)/shard_map/ppermute | solution.py:72
  161.0 2.7 %collective-permute-done.16 = bf16[64,1664]{1,0:T(8,128)(2,1)S(1)} collective-permute-done((bf16[64,1664]{1,0:T(8,128)(2,1)S(1)}, bf16[64,1664]{1,0:T(8,128)(2,1)S(1)}, u32[]{:S(2)}, u32[]{:S(2)}) %collective-permute-start.16) | collective-permute-done | bytes 213024 | tf_op jit(solution)/shard_map/ppermute | solution.py:72
  164.2 1.2 collective-permute-start.26
  166.6 3.5 %collective-permute-done.26 = bf16[64,768]{1,0:T(8,128)(2,1)S(1)} collective-permute-done((bf16[64,768]{1,0:T(8,128)(2,1)S(1)}, bf16[64,768]{1,0:T(8,128)(2,1)S(1)}, u32[]{:S(2)}, u32[]{:S(2)}) %collective-permute-start.26) | collective-permute-done | bytes 98336 | tf_op jit(solution)/shard_map/ppermute | solution.py:72
  172.3 2.1 %collective-permute-start.18 = (bf16[2,64,768]{2,1,0:T(8,128)(2,1)S(1)}, bf16[2,64,768]{2,1,0:T(8,128)(2,1)S(1)}, u32[]{:S(2)}, u32[]{:S(2)}) collective-permute-start(bf16[2,64,768]{2,1,0:T(8,128)(2,1)S(1)} %get-tuple-element.32), channel_id=1, source_target_pairs={{0,3},{1,2},{2,1},{3,0},{4,7},{5,6},{6,5},{7,4},{8,11},{9,10},{10,... | collective-permute-start | bytes 589832 | tf_op jit(solution)/shard_map/ppermute | solution.py:72
  174.4 1.5 collective-permute-done.27
  176.0 1.1 collective-permute-start.28
  177.1 2.0 collective-permute-done.24
  179.1 2.1 collective-permute-start.25
  181.5 3.7 %collective-permute-done.28.r2 = bf16[2,2,64,768]{3,2,1,0:T(8,128)(2,1)S(1)} collective-permute-done((bf16[2,2,64,768]{3,2,1,0:T(8,128)(2,1)S(1)}, bf16[2,2,64,768]{3,2,1,0:T(8,128)(2,1)S(1)}, u32[]{:S(2)}, u32[]{:S(2)}) %collective-permute-start.28) | collective-permute-done | bytes 393248 | tf_op jit(solution)/shard_map/ppermute | solution.py:72
  185.2 3.0 %collective-permute-done.25.r1 = bf16[2,2,64,768]{3,2,1,0:T(8,128)(2,1)S(1)} collective-permute-done((bf16[2,2,64,768]{3,2,1,0:T(8,128)(2,1)S(1)}, bf16[2,2,64,768]{3,2,1,0:T(8,128)(2,1)S(1)}, u32[]{:S(2)}, u32[]{:S(2)}) %collective-permute-start.25) | collective-permute-done | bytes 393248 | tf_op jit(solution)/shard_map/ppermute | solution.py:72
  189.2 3.8 %shard_map.105 = bf16[8,64,896]{2,1,0:T(8,128)(2,1)} custom-call(bf16[2,2,64,768]{3,2,1,0:T(8,128)(2,1)S(1)} %pad_maximum_fusion.1.s0, bf16[2,2,64,768]{3,2,1,0:T(8,128)(2,1)S(1)} %collective-permute-done.19.r0, bf16[2,2,64,768]{3,2,1,0:T(8,128)(2,1)S(1)} %pad_maximum_fusion.2.s1, bf16[2,2,64,768]{3,2,1,0:T(8,128)(2,1)S(1)} %collective-permute-done.25.r1, ...), custom_call_target="tpu_custom_call" | custom-call | flops 2113929216 | bytes 6291456 | tf_op jit(solution)/shard_map/pallas_call | solution.py:219
  193.0 3.6 %all-to-all-start.3 = ((bf16[8,64,896]{2,1,0:T(8,128)(2,1)}), bf16[8,64,896]{2,1,0:T(8,128)(2,1)S(1)}, u32[]{:S(2)}, u32[]{:S(2)}) async-start(bf16[8,64,896]{2,1,0:T(8,128)(2,1)} %shard_map.105), calls=%async_computation.3 | async-start | bytes 1835008 | tf_op jit(solution)/shard_map/all_to_all | solution.py:76
  196.6 12.2 %all-to-all-done.3 = bf16[8,64,896]{2,1,0:T(8,128)(2,1)S(1)} async-done(((bf16[8,64,896]{2,1,0:T(8,128)(2,1)}), bf16[8,64,896]{2,1,0:T(8,128)(2,1)S(1)}, u32[]{:S(2)}, u32[]{:S(2)}) %all-to-all-start.3) | async-done | bytes 917536 | tf_op jit(solution)/shard_map/all_to_all | solution.py:76
  (83 shorter events, 17.0 us)
Async XLA Ops:
  0.0 61.1 %collective-permute-start.8 = (bf16[1024,896]{1,0:T(8,128)(2,1)}, bf16[1024,896]{1,0:T(8,128)(2,1)}, u32[]{:S(2)}, u32[]{:S(2)}) collective-permute-start(bf16[1024,896]{1,0:T(8,128)(2,1)} %own_ref.2), channel_id=1, source_target_pairs={{0,8},{8,0},{16,24},{24,16},{32,40},{40,32},{48,56},{56,48},{64,72... | collective-permute-start | bytes 5505032 | tf_op jit(solution)/shard_map/ppermute | solution.py:68
  31.1 5.8 %collective-permute-start.4 = (bf16[32,2048]{1,0:T(8,128)(2,1)S(1)}, bf16[32,2048]{1,0:T(8,128)(2,1)S(1)}, u32[]{:S(2)}, u32[]{:S(2)}) collective-permute-start(bf16[32,2048]{1,0:T(8,128)(2,1)S(1)} %get-tuple-element.25), channel_id=1, source_target_pairs={{0,1},{1,0},{2,3},{3,2},{4,5},{5,4},{6,7},{7,6},{8,9},{9,8},{10,11... | collective-permute-start | bytes 393224 | tf_op jit(solution)/shard_map/ppermute | solution.py:72
  32.8 8.9 %collective-permute-start.5 = (bf16[32,2048]{1,0:T(8,128)(2,1)S(1)}, bf16[32,2048]{1,0:T(8,128)(2,1)S(1)}, u32[]{:S(2)}, u32[]{:S(2)}) collective-permute-start(bf16[32,2048]{1,0:T(8,128)(2,1)S(1)} %get-tuple-element.25), channel_id=1, source_target_pairs={{0,2},{1,3},{2,0},{3,1},{4,6},{5,7},{6,4},{7,5},{8,10},{9,11},{10,... | collective-permute-start | bytes 393224 | tf_op jit(solution)/shard_map/ppermute | solution.py:72
  35.7 8.0 %collective-permute-start.6 = (bf16[32,2048]{1,0:T(8,128)(2,1)S(1)}, bf16[32,2048]{1,0:T(8,128)(2,1)S(1)}, u32[]{:S(2)}, u32[]{:S(2)}) collective-permute-start(bf16[32,2048]{1,0:T(8,128)(2,1)S(1)} %get-tuple-element.25), channel_id=1, source_target_pairs={{0,3},{1,2},{2,1},{3,0},{4,7},{5,6},{6,5},{7,4},{8,11},{9,10},{10,... | collective-permute-start | bytes 393224 | tf_op jit(solution)/shard_map/ppermute | solution.py:72
  35.9 8.9 %collective-permute-start = (bf16[32,2048]{1,0:T(8,128)(2,1)S(1)}, bf16[32,2048]{1,0:T(8,128)(2,1)S(1)}, u32[]{:S(2)}, u32[]{:S(2)}) collective-permute-start(bf16[32,2048]{1,0:T(8,128)(2,1)S(1)} %get-tuple-element.24), channel_id=1, source_target_pairs={{0,4},{1,5},{2,6},{3,7},{4,0},{5,1},{6,2},{7,3},{8,12},{9,13},{10,... | collective-permute-start | bytes 393224 | tf_op jit(solution)/shard_map/ppermute | solution.py:72
  43.7 17.3 %collective-permute-start.7 = (bf16[4,32,2048]{2,1,0:T(8,128)(2,1)S(1)}, bf16[4,32,2048]{2,1,0:T(8,128)(2,1)S(1)}, u32[]{:S(2)}, u32[]{:S(2)}) collective-permute-start(bf16[4,32,2048]{2,1,0:T(8,128)(2,1)S(1)} %pad_maximum_fusion.b1), channel_id=1, source_target_pairs={{0,4},{1,5},{2,6},{3,7},{4,0},{5,1},{6,2},{7,3},{8,12},{9,13},{10,... | collective-permute-start | bytes 1572872 | tf_op jit(solution)/shard_map/ppermute | solution.py:72
  44.9 13.6 %copy-start = (bf16[896,1152]{1,0:T(8,128)(2,1)S(1)}, bf16[896,1152]{1,0:T(8,128)(2,1)}, u32[]{:S(2)}) copy-start(bf16[896,1152]{1,0:T(8,128)(2,1)} %g0.5) | copy-start | bytes 6193156
  44.9 9.8 %collective-permute-start.1 = (bf16[2,32,2048]{2,1,0:T(8,128)(2,1)S(1)}, bf16[2,32,2048]{2,1,0:T(8,128)(2,1)}, u32[]{:S(2)}, u32[]{:S(2)}) collective-permute-start(bf16[2,32,2048]{2,1,0:T(8,128)(2,1)S(1)} %pad_maximum_fusion.4.b0), channel_id=1, source_target_pairs={{0,1},{1,0},{2,3},{3,2},{4,5},{5,4},{6,7},{7,6},{8,9},{9,8},{10,11... | collective-permute-start | bytes 786440 | tf_op jit(solution)/shard_map/ppermute | solution.py:72
  45.0 13.5 %collective-permute-start.2 = (bf16[2,32,2048]{2,1,0:T(8,128)(2,1)S(1)}, bf16[2,32,2048]{2,1,0:T(8,128)(2,1)}, u32[]{:S(2)}, u32[]{:S(2)}) collective-permute-start(bf16[2,32,2048]{2,1,0:T(8,128)(2,1)S(1)} %pad_maximum_fusion.4.b0), channel_id=1, source_target_pairs={{0,2},{1,3},{2,0},{3,1},{4,6},{5,7},{6,4},{7,5},{8,10},{9,11},{10,... | collective-permute-start | bytes 786440 | tf_op jit(solution)/shard_map/ppermute | solution.py:72
  47.1 14.0 %collective-permute-start.3 = (bf16[2,32,2048]{2,1,0:T(8,128)(2,1)S(1)}, bf16[2,32,2048]{2,1,0:T(8,128)(2,1)}, u32[]{:S(2)}, u32[]{:S(2)}) collective-permute-start(bf16[2,32,2048]{2,1,0:T(8,128)(2,1)S(1)} %pad_maximum_fusion.4.b0), channel_id=1, source_target_pairs={{0,3},{1,2},{2,1},{3,0},{4,7},{5,6},{6,5},{7,4},{8,11},{9,10},{10,... | collective-permute-start | bytes 786440 | tf_op jit(solution)/shard_map/ppermute | solution.py:72
  54.7 37.0 %collective-permute-start.10 = (bf16[896,1152]{1,0:T(8,128)(2,1)}, bf16[896,1152]{1,0:T(8,128)(2,1)}, u32[]{:S(2)}, u32[]{:S(2)}) collective-permute-start(bf16[896,1152]{1,0:T(8,128)(2,1)} %u0.5), channel_id=1, source_target_pairs={{0,8},{8,0},{16,24},{24,16},{32,40},{40,32},{48,56},{56,48},{64,72... | collective-permute-start | bytes 6193160 | tf_op jit(solution)/shard_map/ppermute | solution.py:68
  58.5 33.2 %collective-permute-start.9 = (bf16[896,1152]{1,0:T(8,128)(2,1)S(1)}, bf16[896,1152]{1,0:T(8,128)(2,1)}, u32[]{:S(2)}, u32[]{:S(2)}) collective-permute-start(bf16[896,1152]{1,0:T(8,128)(2,1)S(1)} %copy-done), channel_id=1, source_target_pairs={{0,8},{8,0},{16,24},{24,16},{32,40},{40,32},{48,56},{56,48},{64,72... | collective-permute-start | bytes 6193160 | tf_op jit(solution)/shard_map/ppermute | solution.py:68
  61.1 1.5 copy-start.3
  67.7 4.7 %copy-start.4 = (bf16[896]{0:T(1024)(128)(2,1)S(1)}, bf16[896]{0:T(1024)(128)(2,1)}, u32[]{:S(2)}) copy-start(bf16[896]{0:T(1024)(128)(2,1)} %param.15) | copy-start | bytes 5380
  67.7 18.2 %all-to-all-start.1 = ((bf16[8,64,896]{2,1,0:T(8,128)(2,1)}), bf16[8,64,896]{2,1,0:T(8,128)(2,1)S(1)}, u32[]{:S(2)}, u32[]{:S(2)}) async-start(bf16[8,64,896]{2,1,0:T(8,128)(2,1)} %shard_map.101), calls=%async_computation.1 | async-start | bytes 1835008 | tf_op jit(solution)/shard_map/all_to_all | solution.py:76
  88.1 19.4 %all-to-all-start.2 = ((bf16[8,64,896]{2,1,0:T(8,128)(2,1)}), bf16[8,64,896]{2,1,0:T(8,128)(2,1)S(1)}, u32[]{:S(2)}, u32[]{:S(2)}) async-start(bf16[8,64,896]{2,1,0:T(8,128)(2,1)} %broadcast_in_dim.2), calls=%async_computation.2 | async-start | bytes 1835008 | tf_op jit(solution)/shard_map/all_to_all | solution.py:76
  107.5 1.6 copy-start.1
  112.8 6.0 %copy-start.2 = (bf16[1152,896]{1,0:T(8,128)(2,1)S(1)}, bf16[1152,896]{1,0:T(8,128)(2,1)}, u32[]{:S(2)}) copy-start(bf16[1152,896]{1,0:T(8,128)(2,1)} %own_ref.3) | copy-start | bytes 6193156
  112.8 20.4 %collective-permute-start.20 = (bf16[2,2,64,1536]{3,2,1,0:T(8,128)(2,1)S(1)}, bf16[2,2,64,1536]{3,2,1,0:T(8,128)(2,1)S(1)}, u32[]{:S(2)}, u32[]{:S(2)}) collective-permute-start(bf16[2,2,64,1536]{3,2,1,0:T(8,128)(2,1)S(1)} %get-tuple-element.16), channel_id=1, source_target_pairs={{0,3},{1,2},{2,1},{3,0},{4,7},{5,6},{6,5},{7,4},{8,11},{9,10},{10,... | collective-permute-start | bytes 2359304 | tf_op jit(solution)/shard_map/ppermute | solution.py:72
  118.7 18.9 %collective-permute-start.11 = (bf16[2,2,64,1536]{3,2,1,0:T(8,128)(2,1)S(1)}, bf16[2,2,64,1536]{3,2,1,0:T(8,128)(2,1)S(1)}, u32[]{:S(2)}, u32[]{:S(2)}) collective-permute-start(bf16[2,2,64,1536]{3,2,1,0:T(8,128)(2,1)S(1)} %get-tuple-element.12), channel_id=1, source_target_pairs={{0,1},{1,0},{2,3},{3,2},{4,5},{5,4},{6,7},{7,6},{8,9},{9,8},{10,11... | collective-permute-start | bytes 2359304 | tf_op jit(solution)/shard_map/ppermute | solution.py:72
  118.8 62.7 %collective-permute-start.29 = (bf16[1152,896]{1,0:T(8,128)(2,1)S(1)}, bf16[1152,896]{1,0:T(8,128)(2,1)S(1)}, u32[]{:S(2)}, u32[]{:S(2)}) collective-permute-start(bf16[1152,896]{1,0:T(8,128)(2,1)S(1)} %copy-done.2), channel_id=1, source_target_pairs={{0,8},{8,0},{16,24},{24,16},{32,40},{40,32},{48,56},{56,48},{64,72... | collective-permute-start | bytes 6193160 | tf_op jit(solution)/shard_map/ppermute | solution.py:68
  122.8 21.8 %collective-permute-start.14 = (bf16[2,2,64,1664]{3,2,1,0:T(8,128)(2,1)S(1)}, bf16[2,2,64,1664]{3,2,1,0:T(8,128)(2,1)S(1)}, u32[]{:S(2)}, u32[]{:S(2)}) collective-permute-start(bf16[2,2,64,1664]{3,2,1,0:T(8,128)(2,1)S(1)} %get-tuple-element.14), channel_id=1, source_target_pairs={{0,4},{1,5},{2,6},{3,7},{4,0},{5,1},{6,2},{7,3},{8,12},{9,13},{10,... | collective-permute-start | bytes 2555912 | tf_op jit(solution)/shard_map/ppermute | solution.py:72
  133.3 19.3 %collective-permute-start.21 = (bf16[2,64,1536]{2,1,0:T(8,128)(2,1)S(1)}, bf16[2,64,1536]{2,1,0:T(8,128)(2,1)S(1)}, u32[]{:S(2)}, u32[]{:S(2)}) collective-permute-start(bf16[2,64,1536]{2,1,0:T(8,128)(2,1)S(1)} %fusion.4), channel_id=1, source_target_pairs={{0,4},{1,5},{2,6},{3,7},{4,0},{5,1},{6,2},{7,3},{8,12},{9,13},{10,... | collective-permute-start | bytes 1179656 | tf_op jit(solution)/shard_map/ppermute | solution.py:72
  137.7 16.9 %collective-permute-start.12 = (bf16[2,64,1536]{2,1,0:T(8,128)(2,1)S(1)}, bf16[2,64,1536]{2,1,0:T(8,128)(2,1)S(1)}, u32[]{:S(2)}, u32[]{:S(2)}) collective-permute-start(bf16[2,64,1536]{2,1,0:T(8,128)(2,1)S(1)} %fusion.3), channel_id=1, source_target_pairs={{0,3},{1,2},{2,1},{3,0},{4,7},{5,6},{6,5},{7,4},{8,11},{9,10},{10,... | collective-permute-start | bytes 1179656 | tf_op jit(solution)/shard_map/ppermute | solution.py:72
  144.7 11.8 %collective-permute-start.15 = (bf16[2,64,1664]{2,1,0:T(8,128)(2,1)S(1)}, bf16[2,64,1664]{2,1,0:T(8,128)(2,1)S(1)}, u32[]{:S(2)}, u32[]{:S(2)}) collective-permute-start(bf16[2,64,1664]{2,1,0:T(8,128)(2,1)S(1)} %fusion), channel_id=1, source_target_pairs={{0,1},{1,0},{2,3},{3,2},{4,5},{5,4},{6,7},{7,6},{8,9},{9,8},{10,11... | collective-permute-start | bytes 1277960 | tf_op jit(solution)/shard_map/ppermute | solution.py:72
  152.7 7.3 %collective-permute-start.22 = (bf16[64,1536]{1,0:T(8,128)(2,1)S(1)}, bf16[64,1536]{1,0:T(8,128)(2,1)S(1)}, u32[]{:S(2)}, u32[]{:S(2)}) collective-permute-start(bf16[64,1536]{1,0:T(8,128)(2,1)S(1)} %fusion.5), channel_id=1, source_target_pairs={{0,1},{1,0},{2,3},{3,2},{4,5},{5,4},{6,7},{7,6},{8,9},{9,8},{10,11... | collective-permute-start | bytes 589832 | tf_op jit(solution)/shard_map/ppermute | solution.py:72
  154.6 6.3 %collective-permute-start.13 = (bf16[64,1536]{1,0:T(8,128)(2,1)S(1)}, bf16[64,1536]{1,0:T(8,128)(2,1)S(1)}, u32[]{:S(2)}, u32[]{:S(2)}) collective-permute-start(bf16[64,1536]{1,0:T(8,128)(2,1)S(1)} %fusion.7), channel_id=1, source_target_pairs={{0,4},{1,5},{2,6},{3,7},{4,0},{5,1},{6,2},{7,3},{8,12},{9,13},{10,... | collective-permute-start | bytes 589832 | tf_op jit(solution)/shard_map/ppermute | solution.py:72
  156.6 7.1 %collective-permute-start.16 = (bf16[64,1664]{1,0:T(8,128)(2,1)S(1)}, bf16[64,1664]{1,0:T(8,128)(2,1)S(1)}, u32[]{:S(2)}, u32[]{:S(2)}) collective-permute-start(bf16[64,1664]{1,0:T(8,128)(2,1)S(1)} %fusion.1), channel_id=1, source_target_pairs={{0,3},{1,2},{2,1},{3,0},{4,7},{5,6},{6,5},{7,4},{8,11},{9,10},{10,... | collective-permute-start | bytes 638984 | tf_op jit(solution)/shard_map/ppermute | solution.py:72
  164.2 5.9 %collective-permute-start.26 = (bf16[64,768]{1,0:T(8,128)(2,1)S(1)}, bf16[64,768]{1,0:T(8,128)(2,1)S(1)}, u32[]{:S(2)}, u32[]{:S(2)}) collective-permute-start(bf16[64,768]{1,0:T(8,128)(2,1)S(1)} %pad_maximum_fusion.10), channel_id=1, source_target_pairs={{0,3},{1,2},{2,1},{3,0},{4,7},{5,6},{6,5},{7,4},{8,11},{9,10},{10,... | collective-permute-start | bytes 294920 | tf_op jit(solution)/shard_map/ppermute | solution.py:72
  165.4 5.7 %collective-permute-start.23 = (bf16[64,768]{1,0:T(8,128)(2,1)S(1)}, bf16[64,768]{1,0:T(8,128)(2,1)S(1)}, u32[]{:S(2)}, u32[]{:S(2)}) collective-permute-start(bf16[64,768]{1,0:T(8,128)(2,1)S(1)} %pad_maximum_fusion.9), channel_id=1, source_target_pairs={{0,1},{1,0},{2,3},{3,2},{4,5},{5,4},{6,7},{7,6},{8,9},{9,8},{10,11... | collective-permute-start | bytes 294920 | tf_op jit(solution)/shard_map/ppermute | solution.py:72
  165.5 6.7 %collective-permute-start.17 = (bf16[64,768]{1,0:T(8,128)(2,1)S(1)}, bf16[64,768]{1,0:T(8,128)(2,1)S(1)}, u32[]{:S(2)}, u32[]{:S(2)}) collective-permute-start(bf16[64,768]{1,0:T(8,128)(2,1)S(1)} %pad_maximum_fusion.8), channel_id=1, source_target_pairs={{0,4},{1,5},{2,6},{3,7},{4,0},{5,1},{6,2},{7,3},{8,12},{9,13},{10,... | collective-permute-start | bytes 294920 | tf_op jit(solution)/shard_map/ppermute | solution.py:72
  170.2 5.7 %collective-permute-start.27 = (bf16[2,64,768]{2,1,0:T(8,128)(2,1)S(1)}, bf16[2,64,768]{2,1,0:T(8,128)(2,1)S(1)}, u32[]{:S(2)}, u32[]{:S(2)}) collective-permute-start(bf16[2,64,768]{2,1,0:T(8,128)(2,1)S(1)} %get-tuple-element.28), channel_id=1, source_target_pairs={{0,1},{1,0},{2,3},{3,2},{4,5},{5,4},{6,7},{7,6},{8,9},{9,8},{10,11... | collective-permute-start | bytes 589832 | tf_op jit(solution)/shard_map/ppermute | solution.py:72
  171.2 7.9 %collective-permute-start.24 = (bf16[2,64,768]{2,1,0:T(8,128)(2,1)S(1)}, bf16[2,64,768]{2,1,0:T(8,128)(2,1)S(1)}, u32[]{:S(2)}, u32[]{:S(2)}) collective-permute-start(bf16[2,64,768]{2,1,0:T(8,128)(2,1)S(1)} %get-tuple-element.30), channel_id=1, source_target_pairs={{0,4},{1,5},{2,6},{3,7},{4,0},{5,1},{6,2},{7,3},{8,12},{9,13},{10,... | collective-permute-start | bytes 589832 | tf_op jit(solution)/shard_map/ppermute | solution.py:72
  172.3 9.0 %collective-permute-start.18 = (bf16[2,64,768]{2,1,0:T(8,128)(2,1)S(1)}, bf16[2,64,768]{2,1,0:T(8,128)(2,1)S(1)}, u32[]{:S(2)}, u32[]{:S(2)}) collective-permute-start(bf16[2,64,768]{2,1,0:T(8,128)(2,1)S(1)} %get-tuple-element.32), channel_id=1, source_target_pairs={{0,3},{1,2},{2,1},{3,0},{4,7},{5,6},{6,5},{7,4},{8,11},{9,10},{10,... | collective-permute-start | bytes 589832 | tf_op jit(solution)/shard_map/ppermute | solution.py:72
  176.0 9.2 %collective-permute-start.28 = (bf16[2,2,64,768]{3,2,1,0:T(8,128)(2,1)S(1)}, bf16[2,2,64,768]{3,2,1,0:T(8,128)(2,1)S(1)}, u32[]{:S(2)}, u32[]{:S(2)}) collective-permute-start(bf16[2,2,64,768]{3,2,1,0:T(8,128)(2,1)S(1)} %pad_maximum_fusion.3.s2), channel_id=1, source_target_pairs={{0,4},{1,5},{2,6},{3,7},{4,0},{5,1},{6,2},{7,3},{8,12},{9,13},{10,... | collective-permute-start | bytes 1179656 | tf_op jit(solution)/shard_map/ppermute | solution.py:72
  179.1 9.1 %collective-permute-start.25 = (bf16[2,2,64,768]{3,2,1,0:T(8,128)(2,1)S(1)}, bf16[2,2,64,768]{3,2,1,0:T(8,128)(2,1)S(1)}, u32[]{:S(2)}, u32[]{:S(2)}) collective-permute-start(bf16[2,2,64,768]{3,2,1,0:T(8,128)(2,1)S(1)} %pad_maximum_fusion.2.s1), channel_id=1, source_target_pairs={{0,3},{1,2},{2,1},{3,0},{4,7},{5,6},{6,5},{7,4},{8,11},{9,10},{10,... | collective-permute-start | bytes 1179656 | tf_op jit(solution)/shard_map/ppermute | solution.py:72
  181.4 7.9 %collective-permute-start.19 = (bf16[2,2,64,768]{3,2,1,0:T(8,128)(2,1)S(1)}, bf16[2,2,64,768]{3,2,1,0:T(8,128)(2,1)S(1)}, u32[]{:S(2)}, u32[]{:S(2)}) collective-permute-start(bf16[2,2,64,768]{3,2,1,0:T(8,128)(2,1)S(1)} %pad_maximum_fusion.1.s0), channel_id=1, source_target_pairs={{0,1},{1,0},{2,3},{3,2},{4,5},{5,4},{6,7},{7,6},{8,9},{9,8},{10,11... | collective-permute-start | bytes 1179656 | tf_op jit(solution)/shard_map/ppermute | solution.py:72
  193.0 15.8 %all-to-all-start.3 = ((bf16[8,64,896]{2,1,0:T(8,128)(2,1)}), bf16[8,64,896]{2,1,0:T(8,128)(2,1)S(1)}, u32[]{:S(2)}, u32[]{:S(2)}) async-start(bf16[8,64,896]{2,1,0:T(8,128)(2,1)} %shard_map.105), calls=%async_computation.3 | async-start | bytes 1835008 | tf_op jit(solution)/shard_map/all_to_all | solution.py:76

commit v3 on v2

v3 whole, which is shorter than its diff:
```python
import functools
import math

import jax
import jax.numpy as jnp
from jax import lax
from jax.experimental import pallas as pl
from jax.experimental.pallas import tpu as pltpu
from jax.sharding import PartitionSpec as P

D = 7168
QB = 128
N_ATTN = 16
N_FFN = 8
NQ = 8
NEG = -1e30
BF = jnp.bfloat16
F32 = jnp.float32
MIB = 2**20
PLANES = [[2 * q + c for q in range(NQ)] for c in range(2)]
ORDER = ((1, 3, 4), (3, 4, 1), (4, 1, 3))
NP = len(ORDER)


def attend_kernel(len_ref, q_ref, k_hbm, v_hbm, o_ref, k_ref, v_ref, k_sem, v_sem):
    nm, r, h, hd = q_ref.shape
    l = k_ref.shape[1]
    for i in range(nm * r):
        m, t = divmod(i, r)
        pltpu.make_async_copy(k_hbm.at[m, t], k_ref.at[i], k_sem.at[i]).start()
        pltpu.make_async_copy(v_hbm.at[m, t], v_ref.at[i], v_sem.at[i]).start()
    offsets = lax.broadcasted_iota(jnp.int32, (h, l), 1)

    @pl.loop(0, nm * r // 2)
    def _(step):
        outs = []
        for u in range(2):
            i = step * 2 + u
            m, t = i // r, i % r
            pltpu.make_async_copy(k_hbm.at[m, t], k_ref.at[i], k_sem.at[i]).wait()
            pltpu.make_async_copy(v_hbm.at[m, t], v_ref.at[i], v_sem.at[i]).wait()
        for u in range(2):
            i = step * 2 + u
            m, t = i // r, i % r
            scores = lax.dot_general(
                q_ref[m, t], k_ref[i], (((1,), (1,)), ((), ())), preferred_element_type=F32
            ) * (1.0 / math.sqrt(hd))
            scores = jnp.where(offsets < len_ref[m, t], scores, NEG)
            weights = jnp.exp(scores - jnp.max(scores, axis=1, keepdims=True))
            totals = jnp.sum(weights, axis=1, keepdims=True)
            outs.append(
                jnp.dot(weights.astype(BF), v_ref[i], preferred_element_type=F32) / totals
            )
        for u in range(2):
            for b in range(hd // QB):
                cols = slice(b * QB, (b + 1) * QB)
                block = outs[u][:, cols]
                peak = jnp.max(jnp.abs(block), axis=1, keepdims=True)
                scale = (peak + 1e-06).astype(BF).astype(F32)
                levels = jnp.clip(jnp.floor(127.0 * block / scale + 0.5), -127.0, 127.0)
                o_ref[step * 2 + u, :, cols] = (levels * scale / 127.0).astype(BF)


def attend(q, k, v, lengths):
    nm, r, h, hd = q.shape
    n, l = nm * r, k.shape[2]
    return pl.pallas_call(
        attend_kernel,
        out_shape=jax.ShapeDtypeStruct((n, h, hd), BF),
        in_specs=[
            pl.BlockSpec(memory_space=pltpu.SMEM),
            pl.BlockSpec(memory_space=pltpu.VMEM),
            pl.BlockSpec(memory_space=pl.ANY),
            pl.BlockSpec(memory_space=pl.ANY),
        ],
        out_specs=pl.BlockSpec(memory_space=pltpu.VMEM),
        scratch_shapes=[
            pltpu.VMEM((n, l, hd), BF),
            pltpu.VMEM((n, l, hd), BF),
            pltpu.SemaphoreType.DMA((n,)),
            pltpu.SemaphoreType.DMA((n,)),
        ],
        compiler_params=pltpu.CompilerParams(vmem_limit_bytes=58 * MIB),
        cost_estimate=pl.CostEstimate(
            flops=4 * n * h * l * hd, bytes_accessed=4 * n * l * hd, transcendentals=n * h * l
        ),
    )(lengths, q, k, v)


def ax(x, k):
    return lax.ppermute(x, "attn", [(i, i ^ k) for i in range(N_ATTN)])


def fx(x, k):
    return lax.ppermute(x, "ffn", [(i, i ^ k) for i in range(N_FFN)])


def over_chips(x):
    return lax.all_to_all(x, "attn", 0, 0, axis_index_groups=PLANES)


def vmem_specs(count):
    return [pl.BlockSpec(memory_space=pltpu.VMEM)] * count


def any_specs(count):
    return [pl.BlockSpec(memory_space=pl.ANY)] * count


SMEM = pl.BlockSpec(memory_space=pltpu.SMEM)


def column_chunks(width, step=256):
    return [(s, min(step, width - s)) for s in range(0, width, step)]


def rows_at(start, size):
    return pl.ds(pl.multiple_of(start, size), size)


def spread(at_ref, x_ref, groups, put):
    f = at_ref[1]
    per = x_ref.shape[0] // N_FFN
    for p, (near, far) in enumerate(zip(groups[0::2], groups[1::2])):
        o = ORDER[p]
        for b0, ref in enumerate((near, far)):
            for b1 in range(2):
                for b2 in range(2):
                    j = (b0 * o[0]) ^ (b1 * o[1]) ^ (b2 * o[2])
                    put(rows_at((f ^ j) * per, per), p, ref[b1, b2])


def project_kernel(at_ref, s0, r0, s1, r1, s2, r2, own_hbm, sib_hbm, o_ref, x_ref, w_ref, sem):
    copies = [
        pltpu.make_async_copy(src, w_ref.at[i], sem.at[i])
        for i, src in enumerate((own_hbm, sib_hbm))
    ]
    for copy in copies:
        copy.start()

    def put(rows, p, piece):
        x_ref[rows, PROJECT_CUTS[p] : PROJECT_CUTS[p + 1]] = piece

    spread(at_ref, x_ref, (s0, r0, s1, r1, s2, r2), put)
    for copy in copies:
        copy.wait()
    core = at_ref[0]
    depth = w_ref.shape[1]
    mine = x_ref[:, rows_at(core * depth, depth)]
    other = x_ref[:, rows_at((1 - core) * depth, depth)]
    for start, size in column_chunks(o_ref.shape[2]):
        cols = slice(start, start + size)
        acc = jnp.dot(mine, w_ref[0, :, cols], preferred_element_type=F32) + jnp.dot(
            other, w_ref[1, :, cols], preferred_element_type=F32
        )
        for q in range(NQ):
            for t in range(4):
                first = 2 * t * 64 + q * 8
                o_ref[q, t * 16 : t * 16 + 16, cols] = jnp.concatenate(
                    [acc[first : first + 8], acc[first + 64 : first + 72]], axis=0
                ).astype(BF)


def project(at, pieces, own, sib):
    depth, width = own.shape
    rows = NQ * 64
    return pl.pallas_call(
        project_kernel,
        out_shape=jax.ShapeDtypeStruct((NQ, 64, width), BF),
        in_specs=[SMEM] + vmem_specs(6) + any_specs(2),
        out_specs=pl.BlockSpec(memory_space=pltpu.VMEM),
        scratch_shapes=[
            pltpu.VMEM((rows, 2 * depth), BF),
            pltpu.VMEM((2, depth, width), BF),
            pltpu.SemaphoreType.DMA((2,)),
        ],
        compiler_params=pltpu.CompilerParams(vmem_limit_bytes=LIMIT),
        cost_estimate=pl.CostEstimate(
            flops=4 * rows * depth * width, bytes_accessed=6 * MIB, transcendentals=0
        ),
    )(at, *pieces, own, sib)


def stream_kernel(got_ref, res_ref, gain_ref, stream_ref, scaled_ref):
    total = res_ref[...].astype(F32)
    for i in range(NQ):
        total = total + got_ref[i].astype(F32)
    stream_ref[...] = total
    scaled_ref[...] = (total * gain_ref[...].astype(F32)).astype(BF)


def residual_stream(got, res, gain):
    _, rows, width = got.shape
    return pl.pallas_call(
        stream_kernel,
        out_shape=(
            jax.ShapeDtypeStruct((rows, width), F32),
            jax.ShapeDtypeStruct((rows, width), BF),
        ),
        in_specs=vmem_specs(3),
        out_specs=tuple(vmem_specs(2)),
        compiler_params=pltpu.CompilerParams(vmem_limit_bytes=16 * MIB),
    )(got, res, gain)


def hidden_kernel(at_ref, p0, p1, p2, p3, gain_ref, g0, u0, g1, u1, *refs):
    outs, (x_ref, w_ref, sem) = refs[:-3], refs[-3:]
    step = w_ref.shape[2]
    weights, copies = (g0, u0, g1, u1), []
    for part in range(NP):
        for w, third in HIDDEN_BLOCKS[part]:
            i = len(copies)
            src = weights[w].at[:, pl.ds(third * step, step)]
            copies.append(pltpu.make_async_copy(src, w_ref.at[i], sem.at[i]))
            copies[-1].start()
    f, q = at_ref[1], at_ref[2]
    for k, ref in enumerate((p0, p1, p2, p3)):
        for z in range(2):
            x_ref[rows_at((f ^ q ^ (z * 4 + k)) * 64, 64), :] = ref[z]
    full = x_ref[...]

    def put(acc, part, cols):
        o = ORDER[part]
        for b0 in range(2):
            ref = outs[2 * part + 1 - b0]
            for b1 in range(2):
                for b2 in range(2):
                    j = (b0 * o[0]) ^ (b1 * o[1]) ^ (b2 * o[2])
                    ref[b1, b2, :, cols] = acc[j * 64 : j * 64 + 64].astype(BF)

    ratio = full.astype(F32) / gain_ref[...].astype(F32)
    square = jnp.sum(ratio * ratio, axis=1, keepdims=True)
    put(jnp.broadcast_to(square, (full.shape[0], 128)), SQUARE_PART, slice(4 * step, 4 * step + 128))
    for i, copy in enumerate(copies):
        copy.wait()
        acc = jnp.dot(full, w_ref[i], preferred_element_type=F32)
        put(acc, i // 4, slice((i % 4) * step, (i % 4 + 1) * step))


HIDDEN_BLOCKS = (
    ((0, 0), (1, 0), (0, 1), (1, 1)),
    ((0, 2), (1, 2), (2, 0), (3, 0)),
    ((2, 1), (3, 1), (2, 2), (3, 2)),
)
SQUARE_PART = 2
PROJECT_CUTS = (0, 768, 1408, 2048)
LIMIT = 48 * MIB


def hidden(at, pieces, gain, weights):
    width, hid = weights[0].shape
    step, rows = hid // NP, NQ * 64
    shapes = []
    for part in range(NP):
        cols = 4 * step + (128 if part == SQUARE_PART else 0)
        shapes += [jax.ShapeDtypeStruct((2, 2, 64, cols), BF)] * 2
    outs = pl.pallas_call(
        hidden_kernel,
        out_shape=tuple(shapes),
        in_specs=[SMEM] + vmem_specs(5) + any_specs(4),
        out_specs=tuple(vmem_specs(2 * NP)),
        scratch_shapes=[
            pltpu.VMEM((rows, width), BF),
            pltpu.VMEM((4 * NP, width, step), BF),
            pltpu.SemaphoreType.DMA((4 * NP,)),
        ],
        compiler_params=pltpu.CompilerParams(vmem_limit_bytes=LIMIT),
        cost_estimate=pl.CostEstimate(
            flops=8 * rows * width * hid, bytes_accessed=14 * MIB, transcendentals=0
        ),
    )(at, *pieces, gain, *weights)
    return outs[0::2], outs[1::2]


def down_kernel(at_ref, s0, r0, s1, r1, s2, r2, own_hbm, sib_hbm, o_ref, x_ref, w_ref, sem):
    copies = [
        pltpu.make_async_copy(src, w_ref.at[i], sem.at[i])
        for i, src in enumerate((own_hbm, sib_hbm))
    ]
    for copy in copies:
        copy.start()
    step = s0.shape[3]

    def put(rows, p, piece):
        x_ref[rows, p * step : (p + 1) * step] = piece

    spread(at_ref, x_ref, (s0, r0, s1, r1, s2, r2), put)
    for copy in copies:
        copy.wait()
    hid = w_ref.shape[1]
    mine, other = x_ref[:, :hid], x_ref[:, hid:]
    for start, size in column_chunks(o_ref.shape[1]):
        cols = slice(start, start + size)
        acc = jnp.dot(mine, w_ref[0, :, cols], preferred_element_type=F32) + jnp.dot(
            other, w_ref[1, :, cols], preferred_element_type=F32
        )
        o_ref[:, cols] = acc.astype(BF)


def down(at, pieces, own, sib):
    hid, width = own.shape
    rows = NQ * 64
    return pl.pallas_call(
        down_kernel,
        out_shape=jax.ShapeDtypeStruct((rows, width), BF),
        in_specs=[SMEM] + vmem_specs(6) + any_specs(2),
        out_specs=pl.BlockSpec(memory_space=pltpu.VMEM),
        scratch_shapes=[
            pltpu.VMEM((rows, 2 * hid), BF),
            pltpu.VMEM((2, hid, width), BF),
            pltpu.SemaphoreType.DMA((2,)),
        ],
        compiler_params=pltpu.CompilerParams(vmem_limit_bytes=LIMIT),
        cost_estimate=pl.CostEstimate(
            flops=4 * rows * hid * width, bytes_accessed=6 * MIB, transcendentals=0
        ),
    )(at, *pieces, own, sib)


def scatter_ffn(sends, keeps):
    f = lambda t: t.astype(F32)
    r1 = [fx(s, o[0]) for s, o in zip(sends, ORDER)]
    s2 = [(f(k[1]) + f(r[1])).astype(BF) for k, r in zip(keeps, r1)]
    r2 = [fx(s, o[1]) for s, o in zip(s2, ORDER)]
    s3 = [(f(k[0, 1]) + f(r[0, 1]) + f(q[1])).astype(BF) for k, r, q in zip(keeps, r1, r2)]
    r3 = [fx(s, o[2]) for s, o in zip(s3, ORDER)]
    return [
        f(k[0, 0]) + f(r[0, 0]) + f(q[0]) + f(t) for k, r, q, t in zip(keeps, r1, r2, r3)
    ]


def gather_ffn(parts):
    s = [jnp.stack([x, fx(x, o[2])]) for x, o in zip(parts, ORDER)]
    s = [jnp.stack([x, fx(x, o[1])]) for x, o in zip(s, ORDER)]
    return [t for x, o in zip(s, ORDER) for t in (x, fx(x, o[0]))]


def local(
    queries,
    cache_keys,
    cache_values,
    lengths,
    residual,
    norm_gain,
    out_weight,
    gate_weight,
    up_weight,
    down_weight,
):
    nm, r = queries.shape[:2]
    n = nm * r
    a = lax.axis_index("attn")
    f = lax.axis_index("ffn")
    at = jnp.stack([a % 2, f, a // 2]).astype(jnp.int32)
    w = residual.shape[2]
    rows = N_FFN * n

    out_sib = ax(out_weight, 1)
    gate_sib = ax(gate_weight, 1)
    up_sib = ax(up_weight, 1)
    down_sib = ax(down_weight, 1)

    res = lax.dynamic_slice_in_dim(residual, a * (N_FFN * r), N_FFN * r, 1)
    res = res.reshape(nm, N_FFN, r, w).transpose(1, 0, 2, 3).reshape(rows, w)
    gain = norm_gain.reshape(1, w)

    out = attend(queries, cache_keys, cache_values, lengths)
    got = over_chips(out.reshape(n, NQ, -1).transpose(1, 0, 2)).reshape(NQ * n, -1)

    got, out_sib, gate_sib, up_sib, down_sib = lax.optimization_barrier(
        (got, out_sib, gate_sib, up_sib, down_sib)
    )
    pieces = gather_ffn([got[:, x:y] for x, y in zip(PROJECT_CUTS, PROJECT_CUTS[1:])])
    part = project(at, pieces, out_weight, out_sib)
    stream, scaled = residual_stream(over_chips(part), res, gain)

    pair = jnp.stack([scaled, ax(scaled, 8)])
    pieces = [pair] + [ax(pair, 2 * k) for k in range(1, 4)]
    weights = (gate_weight, up_weight, gate_sib, up_sib)
    sends, keeps = hidden(at, pieces, gain, weights)
    sums = scatter_ffn(sends, keeps)
    step = gate_weight.shape[1] // NP
    inv = lax.rsqrt(sums[SQUARE_PART][:, 4 * step : 4 * step + 1] / D + 1e-06)
    acts = []
    for t in sums:
        g0, u0, g1, u1 = [t[:, i * step : (i + 1) * step] * inv for i in range(4)]
        acts.append(
            jnp.concatenate([jax.nn.silu(g0) * u0, jax.nn.silu(g1) * u1], axis=1).astype(BF)
        )
    part = down(at, gather_ffn(acts), down_weight, down_sib).reshape(NQ, rows, w)
    final = stream + jnp.sum(over_chips(part).astype(F32), axis=0)
    final = final.astype(BF).reshape(N_FFN, nm, r, w)
    return final.transpose(1, 0, 2, 3).reshape(nm, N_FFN * r, w)


def solution(mesh):
    in_specs = (
        P(None, ("attn", "ffn"), None, None),
        P(None, ("attn", "ffn"), None, None),
        P(None, ("attn", "ffn"), None, None),
        P(None, ("attn", "ffn")),
        P(None, None, "ffn"),
        P("ffn"),
        P("attn", "ffn"),
        P("ffn", "attn"),
        P("ffn", "attn"),
        P("attn", "ffn"),
    )
    out_specs = P(None, "attn", "ffn")
    return jax.shard_map(local, mesh=mesh, in_specs=in_specs, out_specs=out_specs, check_vma=False)
```

time: 211 us -> 194 us (0.919)
  waiting for transfers between devices: 101 us -> 86.6 us
  blocking collectives: 16.9 us -> 31.3 us
  local copies, waits for them, and re-layouts: 13.4 us -> 4.63 us
  starting transfers between devices: 43.2 us -> 38.1 us
    all_to_all x3 -> x1, waiting for transfers between devices: 41.5 us -> 12.2 us  [over_chips(): return lax.all_to_all(x, 'attn', 0, 0, axis_index_groups=PLANES)]
    all_to_all x1 -> x2, blocking collectives: 16.9 us -> 31.3 us  [over_chips(): return lax.all_to_all(x, 'attn', 0, 0, axis_index_groups=PLANES)]
    ppermute x4 -> x8, waiting for transfers between devices: 0.01 us -> 12.2 us  [ax(): return lax.ppermute(x, 'attn', [(i, i ^ k) for i in range(N_ATTN)])]
    all_to_all x3 -> x1, starting transfers between devices: 10.8 us -> 3.72 us  [over_chips(): return lax.all_to_all(x, 'attn', 0, 0, axis_index_groups=PLANES)]
    ppermute x4 -> x8, starting transfers between devices: 0.36 us -> 5.83 us  [ax(): return lax.ppermute(x, 'attn', [(i, i ^ k) for i in range(N_ATTN)])]
    reshape x3, local copies, waits for them, and re-layouts: 6.06 us -> 0.74 us  [the longest x1 0.68 us: local(): return final.transpose(1, 0, 2, 3).reshape(nm, N_FFN * r, w)]
    ppermute x26 -> x27, starting transfers between devices: 32 us -> 28.6 us  [fx(): return lax.ppermute(x, 'ffn', [(i, i ^ k) for i in range(N_FFN)])]
    ppermute x26 -> x27, waiting for transfers between devices: 59.8 us -> 62.2 us  [fx(): return lax.ppermute(x, 'ffn', [(i, i ^ k) for i in range(N_FFN)])]
  transfers between devices with their start and end apart: 33 -> 36, of which waited for: 23 -> 21; matrix products, arithmetic and copies ran while one was open for 6% -> 1% of each run, Pallas kernels for 12% -> 5%
where the time goes in v3:
time: 194 us
  waiting for transfers between devices  86.6 us (45%)
  starting transfers between devices  38.1 us (20%)
  blocking collectives  31.3 us (16%)
  Pallas kernels  30.8 us (16%)
  local copies, waits for them, and re-layouts  4.63 us (2%)
    ppermute x27, waiting for transfers between devices, fx(): return lax.ppermute(x, 'ffn', [(i, i ^ k) for i in range(N_FFN)])  62.2 us
    all_to_all x2, blocking collectives, over_chips(): return lax.all_to_all(x, 'attn', 0, 0, axis_index_groups=PLANES)  31.3 us
    ppermute x27, starting transfers between devices, fx(): return lax.ppermute(x, 'ffn', [(i, i ^ k) for i in range(N_FFN)])  28.6 us
    ppermute x8, waiting for transfers between devices, ax(): return lax.ppermute(x, 'attn', [(i, i ^ k) for i in range(N_ATTN)])  12.2 us
    all_to_all x1, waiting for transfers between devices, over_chips(): return lax.all_to_all(x, 'attn', 0, 0, axis_index_groups=PLANES)  12.2 us
    pallas_call x1, Pallas kernels, hidden(): pl.pallas_call(hidden_kernel, out_shape=tuple(shapes), in_specs=[SMEM] +...  10.4 us
    pallas_call x1, Pallas kernels, attend(): pl.pallas_call(attend_kernel, out_shape=jax.ShapeDtypeStruct((n, h, hd),...  9.56 us
    ppermute x8, starting transfers between devices, ax(): return lax.ppermute(x, 'attn', [(i, i ^ k) for i in range(N_ATTN)])  5.83 us
  transfers between devices with their start and end apart: 36, of which 21 were waited for; matrix products, arithmetic and copies ran while one was open for 1% of the time, Pallas kernels for 5%

profile of v3, /device:TPU:0, one launch (start us, length us, event | category | flops | bytes accessed | tf_op | source)
XLA Modules:
  0.0 193.7 jit_solution(5159532666899810871)
XLA Ops:
  1.0 9.6 %shard_map.100 = bf16[8,64,256]{2,1,0:T(8,128)(2,1)} custom-call(s32[2,4]{1,0:T(2,128)} %len_ref.1, bf16[2,4,64,256]{3,2,1,0:T(8,128)(2,1)} %q_ref.1, bf16[2,4,1536,256]{3,2,1,0:T(8,128)(2,1)} %k_hbm.1, bf16[2,4,1536,256]{3,2,1,0:T(8,128)(2,1)} %v_hbm.1), custom_call_target="tpu_custom_call" | custom-call | flops 805306368 | bytes 12582912 | tf_op jit(solution)/shard_map/pallas_call | solution.py:67
  10.6 1.1 reshape.159
  11.8 16.5 %all_to_all.15 = bf16[8,8,2048]{2,1,0:T(8,128)(2,1)S(1)} all-to-all(bf16[8,8,2048]{2,1,0:T(8,128)(2,1)S(1)} %bitcast.100), channel_id=1, replica_groups={{0,16,32,48,64,80,96,112},{8,24,40,56,72,88,104,120},{1,17,33,49,65,81,..., dimensions={0} | all-to-all | bytes 524288 | tf_op jit(solution)/shard_map/all_to_all | solution.py:99
  28.4 1.7 collective-permute-start.7
  30.1 2.3 %collective-permute-start.10 = (bf16[64,640]{1,0:T(8,128)(2,1)S(1)}, bf16[64,640]{1,0:T(8,128)(2,1)S(1)}, u32[]{:S(2)}, u32[]{:S(2)}) collective-permute-start(bf16[64,640]{1,0:T(8,128)(2,1)S(1)} %get-tuple-element.39), channel_id=1, source_target_pairs={{0,3},{1,2},{2,1},{3,0},{4,7},{5,6},{6,5},{7,4},{8,11},{9,10},{10,... | collective-permute-start | bytes 245768 | tf_op jit(solution)/shard_map/ppermute | solution.py:95
  32.3 1.0 collective-permute-start.4
  33.4 1.1 collective-permute-start.8
  34.5 2.5 %collective-permute-done.4 = bf16[64,768]{1,0:T(8,128)(2,1)S(1)} collective-permute-done((bf16[64,768]{1,0:T(8,128)(2,1)S(1)}, bf16[64,768]{1,0:T(8,128)(2,1)S(1)}, u32[]{:S(2)}, u32[]{:S(2)}) %collective-permute-start.4) | collective-permute-done | bytes 98336 | tf_op jit(solution)/shard_map/ppermute | solution.py:95
  37.0 2.1 %collective-permute-start.5 = (bf16[2,64,768]{2,1,0:T(8,128)(2,1)S(1)}, bf16[2,64,768]{2,1,0:T(8,128)(2,1)S(1)}, u32[]{:S(2)}, u32[]{:S(2)}) collective-permute-start(bf16[2,64,768]{2,1,0:T(8,128)(2,1)S(1)} %get-tuple-element.50), channel_id=1, source_target_pairs={{0,3},{1,2},{2,1},{3,0},{4,7},{5,6},{6,5},{7,4},{8,11},{9,10},{10,... | collective-permute-start | bytes 589832 | tf_op jit(solution)/shard_map/ppermute | solution.py:95
  39.3 2.2 %collective-permute-start.9 = (bf16[2,2,64,640]{3,2,1,0:T(8,128)(2,1)S(1)}, bf16[2,2,64,640]{3,2,1,0:T(8,128)(2,1)}, u32[]{:S(2)}, u32[]{:S(2)}) collective-permute-start(bf16[2,2,64,640]{3,2,1,0:T(8,128)(2,1)S(1)} %pad_maximum_fusion.4.s1), channel_id=1, source_target_pairs={{0,3},{1,2},{2,1},{3,0},{4,7},{5,6},{6,5},{7,4},{8,11},{9,10},{10,... | collective-permute-start | bytes 983048 | tf_op jit(solution)/shard_map/ppermute | solution.py:95
  41.5 4.2 %collective-permute-done.5 = bf16[2,64,768]{2,1,0:T(8,128)(2,1)S(1)} collective-permute-done((bf16[2,64,768]{2,1,0:T(8,128)(2,1)S(1)}, bf16[2,64,768]{2,1,0:T(8,128)(2,1)S(1)}, u32[]{:S(2)}, u32[]{:S(2)}) %collective-permute-start.5) | collective-permute-done | bytes 196640 | tf_op jit(solution)/shard_map/ppermute | solution.py:95
  46.3 1.1 collective-permute-start.12
  47.5 1.8 collective-permute-done.9.r1
  49.3 4.3 %collective-permute-done.12.r2 = bf16[2,2,64,640]{3,2,1,0:T(8,128)(2,1)} collective-permute-done((bf16[2,2,64,640]{3,2,1,0:T(8,128)(2,1)S(1)}, bf16[2,2,64,640]{3,2,1,0:T(8,128)(2,1)}, u32[]{:S(2)}, u32[]{:S(2)}) %collective-permute-start.12) | collective-permute-done | bytes 327712 | tf_op jit(solution)/shard_map/ppermute | solution.py:95
  53.6 1.5 copy-done.3
  55.1 5.2 %shard_map.101 = bf16[8,64,896]{2,1,0:T(8,128)(2,1)S(1)} custom-call(s32[3]{0:T(128)S(1)} %pad_add_fusion.at_ref, bf16[2,2,64,768]{3,2,1,0:T(8,128)(2,1)S(1)} %pad_maximum_fusion.s0, bf16[2,2,64,768]{3,2,1,0:T(8,128)(2,1)S(1)} %collective-permute-done.6.r0, bf16[2,2,64,640]{3,2,1,0:T(8,128)(2,1)S(1)} %pad_maximum_fusion.4.s1, ...), custom_call_target="tpu_custom_call" | custom-call | flops 1879048192 | bytes 6291456 | tf_op jit(solution)/shard_map/pallas_call | solution.py:167
  60.3 0.9 copy-done.1
  61.2 3.7 %all-to-all-start.1 = ((bf16[8,64,896]{2,1,0:T(8,128)(2,1)}), bf16[8,64,896]{2,1,0:T(8,128)(2,1)S(1)}, u32[]{:S(2)}, u32[]{:S(2)}) async-start(bf16[8,64,896]{2,1,0:T(8,128)(2,1)} %copy-done.1), calls=%async_computation.1 | async-start | bytes 1835008 | tf_op jit(solution)/shard_map/all_to_all | solution.py:99
  65.2 12.2 %all-to-all-done.1.got_ref = bf16[8,64,896]{2,1,0:T(8,128)(2,1)S(1)} async-done(((bf16[8,64,896]{2,1,0:T(8,128)(2,1)}), bf16[8,64,896]{2,1,0:T(8,128)(2,1)S(1)}, u32[]{:S(2)}, u32[]{:S(2)}) %all-to-all-start.1) | async-done | bytes 917536 | tf_op jit(solution)/shard_map/all_to_all | solution.py:99
  78.2 5.7 %collective-permute-done.13 = bf16[64,896]{1,0:T(8,128)(2,1)S(1)} collective-permute-done((bf16[64,896]{1,0:T(8,128)(2,1)S(1)}, bf16[64,896]{1,0:T(8,128)(2,1)S(1)}, u32[]{:S(2)}, u32[]{:S(2)}) %collective-permute-start.13) | collective-permute-done | bytes 114720 | tf_op jit(solution)/shard_map/ppermute | solution.py:91
  83.9 1.0 collective-permute-start.16
  84.9 2.0 %collective-permute-start.15 = (bf16[2,64,896]{2,1,0:T(8,128)(2,1)S(1)}, bf16[2,64,896]{2,1,0:T(8,128)(2,1)S(1)}, u32[]{:S(2)}, u32[]{:S(2)}) collective-permute-start(bf16[2,64,896]{2,1,0:T(8,128)(2,1)S(1)} %pad_maximum_fusion.6.p0), channel_id=1, source_target_pairs={{0,32},{8,40},{16,48},{24,56},{32,0},{40,8},{48,16},{56,24},{64,96... | collective-permute-start | bytes 688136 | tf_op jit(solution)/shard_map/ppermute | solution.py:91
  86.9 1.2 collective-permute-start.14
  88.1 5.6 %collective-permute-done.16.p3 = bf16[2,64,896]{2,1,0:T(8,128)(2,1)S(1)} collective-permute-done((bf16[2,64,896]{2,1,0:T(8,128)(2,1)S(1)}, bf16[2,64,896]{2,1,0:T(8,128)(2,1)S(1)}, u32[]{:S(2)}, u32[]{:S(2)}) %collective-permute-start.16) | collective-permute-done | bytes 229408 | tf_op jit(solution)/shard_map/ppermute | solution.py:91
  93.7 0.9 collective-permute-done.14.p1
  94.6 10.4 %shard_map.103 = (bf16[2,2,64,1536]{3,2,1,0:T(8,128)(2,1)S(1)}, bf16[2,2,64,1536]{3,2,1,0:T(8,128)(2,1)S(1)}, bf16[2,2,64,1536]{3,2,1,0:T(8,128)(2,1)S(1)}, bf16...) custom-call(s32[3]{0:T(128)S(1)} %pad_add_fusion.at_ref, ...), custom_call_target="tpu_custom_call" | custom-call | flops 4227858432 | bytes 14680064 | tf_op jit(solution)/shard_map/pallas_call | solution.py:257
  104.9 1.6 collective-permute-start.17
  106.6 2.1 %collective-permute-start.26 = (bf16[2,2,64,1536]{3,2,1,0:T(8,128)(2,1)S(1)}, bf16[2,2,64,1536]{3,2,1,0:T(8,128)(2,1)S(1)}, u32[]{:S(2)}, u32[]{:S(2)}) collective-permute-start(bf16[2,2,64,1536]{3,2,1,0:T(8,128)(2,1)S(1)} %get-tuple-element.29), channel_id=1, source_target_pairs={{0,3},{1,2},{2,1},{3,0},{4,7},{5,6},{6,5},{7,4},{8,11},{9,10},{10,... | collective-permute-start | bytes 2359304 | tf_op jit(solution)/shard_map/ppermute | solution.py:95
  108.6 1.0 collective-permute-start.20
  109.7 10.2 %collective-permute-done.17 = bf16[2,2,64,1536]{3,2,1,0:T(8,128)(2,1)S(1)} collective-permute-done((bf16[2,2,64,1536]{3,2,1,0:T(8,128)(2,1)S(1)}, bf16[2,2,64,1536]{3,2,1,0:T(8,128)(2,1)S(1)}, u32[]{:S(2)}, u32[]{:S(2)}) %collective-permute-start.17) | collective-permute-done | bytes 786464 | tf_op jit(solution)/shard_map/ppermute | solution.py:95
  120.0 2.5 %collective-permute-start.18 = (bf16[2,64,1536]{2,1,0:T(8,128)(2,1)S(1)}, bf16[2,64,1536]{2,1,0:T(8,128)(2,1)S(1)}, u32[]{:S(2)}, u32[]{:S(2)}) collective-permute-start(bf16[2,64,1536]{2,1,0:T(8,128)(2,1)S(1)} %fusion.3), channel_id=1, source_target_pairs={{0,3},{1,2},{2,1},{3,0},{4,7},{5,6},{6,5},{7,4},{8,11},{9,10},{10,... | collective-permute-start | bytes 1179656 | tf_op jit(solution)/shard_map/ppermute | solution.py:95
  122.6 1.4 collective-permute-done.26
  124.1 0.9 collective-permute-start.27
  125.0 2.5 %collective-permute-done.20 = bf16[2,2,64,1664]{3,2,1,0:T(8,128)(2,1)S(1)} collective-permute-done((bf16[2,2,64,1664]{3,2,1,0:T(8,128)(2,1)S(1)}, bf16[2,2,64,1664]{3,2,1,0:T(8,128)(2,1)S(1)}, u32[]{:S(2)}, u32[]{:S(2)}) %collective-permute-start.20) | collective-permute-done | bytes 852000 | tf_op jit(solution)/shard_map/ppermute | solution.py:95
  127.6 3.7 %collective-permute-done.18 = bf16[2,64,1536]{2,1,0:T(8,128)(2,1)S(1)} collective-permute-done((bf16[2,64,1536]{2,1,0:T(8,128)(2,1)S(1)}, bf16[2,64,1536]{2,1,0:T(8,128)(2,1)S(1)}, u32[]{:S(2)}, u32[]{:S(2)}) %collective-permute-start.18) | collective-permute-done | bytes 393248 | tf_op jit(solution)/shard_map/ppermute | solution.py:95
  132.3 1.5 collective-permute-start.28
  133.8 3.1 %collective-permute-done.21 = bf16[2,64,1664]{2,1,0:T(8,128)(2,1)S(1)} collective-permute-done((bf16[2,64,1664]{2,1,0:T(8,128)(2,1)S(1)}, bf16[2,64,1664]{2,1,0:T(8,128)(2,1)S(1)}, u32[]{:S(2)}, u32[]{:S(2)}) %collective-permute-start.21) | collective-permute-done | bytes 426016 | tf_op jit(solution)/shard_map/ppermute | solution.py:95
  137.0 1.2 collective-permute-done.19
  139.0 6.9 %collective-permute-done.22 = bf16[64,1664]{1,0:T(8,128)(2,1)S(1)} collective-permute-done((bf16[64,1664]{1,0:T(8,128)(2,1)S(1)}, bf16[64,1664]{1,0:T(8,128)(2,1)S(1)}, u32[]{:S(2)}, u32[]{:S(2)}) %collective-permute-start.22) | collective-permute-done | bytes 213024 | tf_op jit(solution)/shard_map/ppermute | solution.py:95
  147.4 6.1 %collective-permute-done.32 = bf16[64,768]{1,0:T(8,128)(2,1)S(1)} collective-permute-done((bf16[64,768]{1,0:T(8,128)(2,1)S(1)}, bf16[64,768]{1,0:T(8,128)(2,1)S(1)}, u32[]{:S(2)}, u32[]{:S(2)}) %collective-permute-start.32) | collective-permute-done | bytes 98336 | tf_op jit(solution)/shard_map/ppermute | solution.py:95
  153.6 0.9 collective-permute-start.33
  156.0 3.4 %collective-permute-done.33 = bf16[2,64,768]{2,1,0:T(8,128)(2,1)S(1)} collective-permute-done((bf16[2,64,768]{2,1,0:T(8,128)(2,1)S(1)}, bf16[2,64,768]{2,1,0:T(8,128)(2,1)S(1)}, u32[]{:S(2)}, u32[]{:S(2)}) %collective-permute-start.33) | collective-permute-done | bytes 196640 | tf_op jit(solution)/shard_map/ppermute | solution.py:95
  159.4 1.0 collective-permute-start.34
  160.4 1.1 collective-permute-done.24
  161.7 2.1 %collective-permute-start.31 = (bf16[2,2,64,768]{3,2,1,0:T(8,128)(2,1)S(1)}, bf16[2,2,64,768]{3,2,1,0:T(8,128)(2,1)S(1)}, u32[]{:S(2)}, u32[]{:S(2)}) collective-permute-start(bf16[2,2,64,768]{3,2,1,0:T(8,128)(2,1)S(1)} %pad_maximum_fusion.2.s1), channel_id=1, source_target_pairs={{0,3},{1,2},{2,1},{3,0},{4,7},{5,6},{6,5},{7,4},{8,11},{9,10},{10,... | collective-permute-start | bytes 1179656 | tf_op jit(solution)/shard_map/ppermute | solution.py:95
  163.7 8.7 %collective-permute-done.34.r2 = bf16[2,2,64,768]{3,2,1,0:T(8,128)(2,1)S(1)} collective-permute-done((bf16[2,2,64,768]{3,2,1,0:T(8,128)(2,1)S(1)}, bf16[2,2,64,768]{3,2,1,0:T(8,128)(2,1)S(1)}, u32[]{:S(2)}, u32[]{:S(2)}) %collective-permute-start.34) | collective-permute-done | bytes 393248 | tf_op jit(solution)/shard_map/ppermute | solution.py:95
  172.4 5.5 %shard_map.104 = bf16[512,896]{1,0:T(8,128)(2,1)S(1)} custom-call(s32[3]{0:T(128)S(1)} %pad_add_fusion.at_ref, bf16[2,2,64,768]{3,2,1,0:T(8,128)(2,1)S(1)} %pad_maximum_fusion.1.s0, bf16[2,2,64,768]{3,2,1,0:T(8,128)(2,1)S(1)} %collective-permute-done.25.r0, bf16[2,2,64,768]{3,2,1,0:T(8,128)(2,1)S(1)} %pad_maximum_fusion.2.s1, ...), custom_call_target="tpu_custom_call" | custom-call | flops 2113929216 | bytes 6291456 | tf_op jit(solution)/shard_map/pallas_call | solution.py:303
  178.0 14.8 %all_to_all.16 = bf16[8,64,896]{2,1,0:T(8,128)(2,1)S(1)} all-to-all(bf16[8,64,896]{2,1,0:T(8,128)(2,1)S(1)} %bitcast.98), channel_id=1, replica_groups={{0,16,32,48,64,80,96,112},{8,24,40,56,72,88,104,120},{1,17,33,49,65,81,..., dimensions={0} | all-to-all | bytes 1835008 | tf_op jit(solution)/shard_map/all_to_all | solution.py:99
  (83 shorter events, 9.5 us)
Async XLA Ops:
  0.0 65.0 %copy-start = (bf16[2,512,896]{2,1,0:T(8,128)(2,1)S(1)}, bf16[2,512,896]{2,1,0:T(8,128)(2,1)}, u32[]{:S(2)}) copy-start(bf16[2,512,896]{2,1,0:T(8,128)(2,1)} %param.14) | copy-start | bytes 5505028
  0.0 28.3 %collective-permute-start.1 = (bf16[896,1152]{1,0:T(8,128)(2,1)}, bf16[896,1152]{1,0:T(8,128)(2,1)}, u32[]{:S(2)}, u32[]{:S(2)}) collective-permute-start(bf16[896,1152]{1,0:T(8,128)(2,1)} %g0.1), channel_id=1, source_target_pairs={{0,8},{8,0},{16,24},{24,16},{32,40},{40,32},{48,56},{56,48},{64,72... | collective-permute-start | bytes 6193160 | tf_op jit(solution)/shard_map/ppermute | solution.py:91
  0.0 28.3 %collective-permute-start.2 = (bf16[896,1152]{1,0:T(8,128)(2,1)}, bf16[896,1152]{1,0:T(8,128)(2,1)}, u32[]{:S(2)}, u32[]{:S(2)}) collective-permute-start(bf16[896,1152]{1,0:T(8,128)(2,1)} %u0.1), channel_id=1, source_target_pairs={{0,8},{8,0},{16,24},{24,16},{32,40},{40,32},{48,56},{56,48},{64,72... | collective-permute-start | bytes 6193160 | tf_op jit(solution)/shard_map/ppermute | solution.py:91
  0.5 27.8 %collective-permute-start.3 = (bf16[1152,896]{1,0:T(8,128)(2,1)}, bf16[1152,896]{1,0:T(8,128)(2,1)}, u32[]{:S(2)}, u32[]{:S(2)}) collective-permute-start(bf16[1152,896]{1,0:T(8,128)(2,1)} %own_hbm.3), channel_id=1, source_target_pairs={{0,8},{8,0},{16,24},{24,16},{32,40},{40,32},{48,56},{56,48},{64,72... | collective-permute-start | bytes 6193160 | tf_op jit(solution)/shard_map/ppermute | solution.py:91
  0.5 27.8 %collective-permute-start = (bf16[1024,896]{1,0:T(8,128)(2,1)}, bf16[1024,896]{1,0:T(8,128)(2,1)}, u32[]{:S(2)}, u32[]{:S(2)}) collective-permute-start(bf16[1024,896]{1,0:T(8,128)(2,1)} %own_hbm.2), channel_id=1, source_target_pairs={{0,8},{8,0},{16,24},{24,16},{32,40},{40,32},{48,56},{56,48},{64,72... | collective-permute-start | bytes 5505032 | tf_op jit(solution)/shard_map/ppermute | solution.py:91
  28.4 5.0 %collective-permute-start.7 = (bf16[64,640]{1,0:T(8,128)(2,1)S(1)}, bf16[64,640]{1,0:T(8,128)(2,1)S(1)}, u32[]{:S(2)}, u32[]{:S(2)}) collective-permute-start(bf16[64,640]{1,0:T(8,128)(2,1)S(1)} %get-tuple-element.40), channel_id=1, source_target_pairs={{0,1},{1,0},{2,3},{3,2},{4,5},{5,4},{6,7},{7,6},{8,9},{9,8},{10,11... | collective-permute-start | bytes 245768 | tf_op jit(solution)/shard_map/ppermute | solution.py:95
  30.1 9.0 %collective-permute-start.10 = (bf16[64,640]{1,0:T(8,128)(2,1)S(1)}, bf16[64,640]{1,0:T(8,128)(2,1)S(1)}, u32[]{:S(2)}, u32[]{:S(2)}) collective-permute-start(bf16[64,640]{1,0:T(8,128)(2,1)S(1)} %get-tuple-element.39), channel_id=1, source_target_pairs={{0,3},{1,2},{2,1},{3,0},{4,7},{5,6},{6,5},{7,4},{8,11},{9,10},{10,... | collective-permute-start | bytes 245768 | tf_op jit(solution)/shard_map/ppermute | solution.py:95
  32.3 4.7 %collective-permute-start.4 = (bf16[64,768]{1,0:T(8,128)(2,1)S(1)}, bf16[64,768]{1,0:T(8,128)(2,1)S(1)}, u32[]{:S(2)}, u32[]{:S(2)}) collective-permute-start(bf16[64,768]{1,0:T(8,128)(2,1)S(1)} %get-tuple-element.42), channel_id=1, source_target_pairs={{0,4},{1,5},{2,6},{3,7},{4,0},{5,1},{6,2},{7,3},{8,12},{9,13},{10,... | collective-permute-start | bytes 294920 | tf_op jit(solution)/shard_map/ppermute | solution.py:95
  33.4 5.9 %collective-permute-start.8 = (bf16[2,64,640]{2,1,0:T(8,128)(2,1)S(1)}, bf16[2,64,640]{2,1,0:T(8,128)(2,1)S(1)}, u32[]{:S(2)}, u32[]{:S(2)}) collective-permute-start(bf16[2,64,640]{2,1,0:T(8,128)(2,1)S(1)} %get-tuple-element.54), channel_id=1, source_target_pairs={{0,4},{1,5},{2,6},{3,7},{4,0},{5,1},{6,2},{7,3},{8,12},{9,13},{10,... | collective-permute-start | bytes 491528 | tf_op jit(solution)/shard_map/ppermute | solution.py:95
  37.0 8.7 %collective-permute-start.5 = (bf16[2,64,768]{2,1,0:T(8,128)(2,1)S(1)}, bf16[2,64,768]{2,1,0:T(8,128)(2,1)S(1)}, u32[]{:S(2)}, u32[]{:S(2)}) collective-permute-start(bf16[2,64,768]{2,1,0:T(8,128)(2,1)S(1)} %get-tuple-element.50), channel_id=1, source_target_pairs={{0,3},{1,2},{2,1},{3,0},{4,7},{5,6},{6,5},{7,4},{8,11},{9,10},{10,... | collective-permute-start | bytes 589832 | tf_op jit(solution)/shard_map/ppermute | solution.py:95
  39.2 7.2 %collective-permute-start.11 = (bf16[2,64,640]{2,1,0:T(8,128)(2,1)S(1)}, bf16[2,64,640]{2,1,0:T(8,128)(2,1)S(1)}, u32[]{:S(2)}, u32[]{:S(2)}) collective-permute-start(bf16[2,64,640]{2,1,0:T(8,128)(2,1)S(1)} %get-tuple-element.52), channel_id=1, source_target_pairs={{0,1},{1,0},{2,3},{3,2},{4,5},{5,4},{6,7},{7,6},{8,9},{9,8},{10,11... | collective-permute-start | bytes 491528 | tf_op jit(solution)/shard_map/ppermute | solution.py:95
  39.3 10.0 %collective-permute-start.9 = (bf16[2,2,64,640]{3,2,1,0:T(8,128)(2,1)S(1)}, bf16[2,2,64,640]{3,2,1,0:T(8,128)(2,1)}, u32[]{:S(2)}, u32[]{:S(2)}) collective-permute-start(bf16[2,2,64,640]{3,2,1,0:T(8,128)(2,1)S(1)} %pad_maximum_fusion.4.s1), channel_id=1, source_target_pairs={{0,3},{1,2},{2,1},{3,0},{4,7},{5,6},{6,5},{7,4},{8,11},{9,10},{10,... | collective-permute-start | bytes 983048 | tf_op jit(solution)/shard_map/ppermute | solution.py:95
  45.8 7.9 %collective-permute-start.6 = (bf16[2,2,64,768]{3,2,1,0:T(8,128)(2,1)S(1)}, bf16[2,2,64,768]{3,2,1,0:T(8,128)(2,1)S(1)}, u32[]{:S(2)}, u32[]{:S(2)}) collective-permute-start(bf16[2,2,64,768]{3,2,1,0:T(8,128)(2,1)S(1)} %pad_maximum_fusion.s0), channel_id=1, source_target_pairs={{0,1},{1,0},{2,3},{3,2},{4,5},{5,4},{6,7},{7,6},{8,9},{9,8},{10,11... | collective-permute-start | bytes 1179656 | tf_op jit(solution)/shard_map/ppermute | solution.py:95
  46.3 7.3 %collective-permute-start.12 = (bf16[2,2,64,640]{3,2,1,0:T(8,128)(2,1)S(1)}, bf16[2,2,64,640]{3,2,1,0:T(8,128)(2,1)}, u32[]{:S(2)}, u32[]{:S(2)}) collective-permute-start(bf16[2,2,64,640]{3,2,1,0:T(8,128)(2,1)S(1)} %pad_maximum_fusion.5.s2), channel_id=1, source_target_pairs={{0,4},{1,5},{2,6},{3,7},{4,0},{5,1},{6,2},{7,3},{8,12},{9,13},{10,... | collective-permute-start | bytes 983048 | tf_op jit(solution)/shard_map/ppermute | solution.py:95
  47.5 17.5 %copy-start.4 = (bf16[896]{0:T(1024)(128)(2,1)S(1)}, bf16[896]{0:T(1024)(128)(2,1)}, u32[]{:S(2)}) copy-start(bf16[896]{0:T(1024)(128)(2,1)} %param.15) | copy-start | bytes 5380
  53.6 1.5 copy-start.3
  60.3 0.9 copy-start.1
  61.2 16.1 %all-to-all-start.1 = ((bf16[8,64,896]{2,1,0:T(8,128)(2,1)}), bf16[8,64,896]{2,1,0:T(8,128)(2,1)S(1)}, u32[]{:S(2)}, u32[]{:S(2)}) async-start(bf16[8,64,896]{2,1,0:T(8,128)(2,1)} %copy-done.1), calls=%async_computation.1 | async-start | bytes 1835008 | tf_op jit(solution)/shard_map/all_to_all | solution.py:99
  77.5 6.4 %collective-permute-start.13 = (bf16[64,896]{1,0:T(8,128)(2,1)S(1)}, bf16[64,896]{1,0:T(8,128)(2,1)S(1)}, u32[]{:S(2)}, u32[]{:S(2)}) collective-permute-start(bf16[64,896]{1,0:T(8,128)(2,1)S(1)} %get-tuple-element.21), channel_id=1, source_target_pairs={{0,64},{8,72},{16,80},{24,88},{32,96},{40,104},{48,112},{56,120},{... | collective-permute-start | bytes 344072 | tf_op jit(solution)/shard_map/ppermute | solution.py:91
  83.9 9.8 %collective-permute-start.16 = (bf16[2,64,896]{2,1,0:T(8,128)(2,1)S(1)}, bf16[2,64,896]{2,1,0:T(8,128)(2,1)S(1)}, u32[]{:S(2)}, u32[]{:S(2)}) collective-permute-start(bf16[2,64,896]{2,1,0:T(8,128)(2,1)S(1)} %pad_maximum_fusion.6.p0), channel_id=1, source_target_pairs={{0,48},{8,56},{16,32},{24,40},{32,16},{40,24},{48,0},{56,8},{64,11... | collective-permute-start | bytes 688136 | tf_op jit(solution)/shard_map/ppermute | solution.py:91
  84.9 8.8 %collective-permute-start.15 = (bf16[2,64,896]{2,1,0:T(8,128)(2,1)S(1)}, bf16[2,64,896]{2,1,0:T(8,128)(2,1)S(1)}, u32[]{:S(2)}, u32[]{:S(2)}) collective-permute-start(bf16[2,64,896]{2,1,0:T(8,128)(2,1)S(1)} %pad_maximum_fusion.6.p0), channel_id=1, source_target_pairs={{0,32},{8,40},{16,48},{24,56},{32,0},{40,8},{48,16},{56,24},{64,96... | collective-permute-start | bytes 688136 | tf_op jit(solution)/shard_map/ppermute | solution.py:91
  86.9 7.6 %collective-permute-start.14 = (bf16[2,64,896]{2,1,0:T(8,128)(2,1)S(1)}, bf16[2,64,896]{2,1,0:T(8,128)(2,1)S(1)}, u32[]{:S(2)}, u32[]{:S(2)}) collective-permute-start(bf16[2,64,896]{2,1,0:T(8,128)(2,1)S(1)} %pad_maximum_fusion.6.p0), channel_id=1, source_target_pairs={{0,16},{8,24},{16,0},{24,8},{32,48},{40,56},{48,32},{56,40},{64,80... | collective-permute-start | bytes 688136 | tf_op jit(solution)/shard_map/ppermute | solution.py:91
  104.9 15.0 %collective-permute-start.17 = (bf16[2,2,64,1536]{3,2,1,0:T(8,128)(2,1)S(1)}, bf16[2,2,64,1536]{3,2,1,0:T(8,128)(2,1)S(1)}, u32[]{:S(2)}, u32[]{:S(2)}) collective-permute-start(bf16[2,2,64,1536]{3,2,1,0:T(8,128)(2,1)S(1)} %get-tuple-element.25), channel_id=1, source_target_pairs={{0,1},{1,0},{2,3},{3,2},{4,5},{5,4},{6,7},{7,6},{8,9},{9,8},{10,11... | collective-permute-start | bytes 2359304 | tf_op jit(solution)/shard_map/ppermute | solution.py:95
  106.6 17.4 %collective-permute-start.26 = (bf16[2,2,64,1536]{3,2,1,0:T(8,128)(2,1)S(1)}, bf16[2,2,64,1536]{3,2,1,0:T(8,128)(2,1)S(1)}, u32[]{:S(2)}, u32[]{:S(2)}) collective-permute-start(bf16[2,2,64,1536]{3,2,1,0:T(8,128)(2,1)S(1)} %get-tuple-element.29), channel_id=1, source_target_pairs={{0,3},{1,2},{2,1},{3,0},{4,7},{5,6},{6,5},{7,4},{8,11},{9,10},{10,... | collective-permute-start | bytes 2359304 | tf_op jit(solution)/shard_map/ppermute | solution.py:95
  108.6 18.8 %collective-permute-start.20 = (bf16[2,2,64,1664]{3,2,1,0:T(8,128)(2,1)S(1)}, bf16[2,2,64,1664]{3,2,1,0:T(8,128)(2,1)S(1)}, u32[]{:S(2)}, u32[]{:S(2)}) collective-permute-start(bf16[2,2,64,1664]{3,2,1,0:T(8,128)(2,1)S(1)} %get-tuple-element.27), channel_id=1, source_target_pairs={{0,4},{1,5},{2,6},{3,7},{4,0},{5,1},{6,2},{7,3},{8,12},{9,13},{10,... | collective-permute-start | bytes 2555912 | tf_op jit(solution)/shard_map/ppermute | solution.py:95
  120.0 11.3 %collective-permute-start.18 = (bf16[2,64,1536]{2,1,0:T(8,128)(2,1)S(1)}, bf16[2,64,1536]{2,1,0:T(8,128)(2,1)S(1)}, u32[]{:S(2)}, u32[]{:S(2)}) collective-permute-start(bf16[2,64,1536]{2,1,0:T(8,128)(2,1)S(1)} %fusion.3), channel_id=1, source_target_pairs={{0,3},{1,2},{2,1},{3,0},{4,7},{5,6},{6,5},{7,4},{8,11},{9,10},{10,... | collective-permute-start | bytes 1179656 | tf_op jit(solution)/shard_map/ppermute | solution.py:95
  124.1 8.1 %collective-permute-start.27 = (bf16[2,64,1536]{2,1,0:T(8,128)(2,1)S(1)}, bf16[2,64,1536]{2,1,0:T(8,128)(2,1)S(1)}, u32[]{:S(2)}, u32[]{:S(2)}) collective-permute-start(bf16[2,64,1536]{2,1,0:T(8,128)(2,1)S(1)} %fusion.4), channel_id=1, source_target_pairs={{0,4},{1,5},{2,6},{3,7},{4,0},{5,1},{6,2},{7,3},{8,12},{9,13},{10,... | collective-permute-start | bytes 1179656 | tf_op jit(solution)/shard_map/ppermute | solution.py:95
  127.6 9.3 %collective-permute-start.21 = (bf16[2,64,1664]{2,1,0:T(8,128)(2,1)S(1)}, bf16[2,64,1664]{2,1,0:T(8,128)(2,1)S(1)}, u32[]{:S(2)}, u32[]{:S(2)}) collective-permute-start(bf16[2,64,1664]{2,1,0:T(8,128)(2,1)S(1)} %fusion), channel_id=1, source_target_pairs={{0,1},{1,0},{2,3},{3,2},{4,5},{5,4},{6,7},{7,6},{8,9},{9,8},{10,11... | collective-permute-start | bytes 1277960 | tf_op jit(solution)/shard_map/ppermute | solution.py:95
  131.4 6.8 %collective-permute-start.19 = (bf16[64,1536]{1,0:T(8,128)(2,1)S(1)}, bf16[64,1536]{1,0:T(8,128)(2,1)S(1)}, u32[]{:S(2)}, u32[]{:S(2)}) collective-permute-start(bf16[64,1536]{1,0:T(8,128)(2,1)S(1)} %fusion.7), channel_id=1, source_target_pairs={{0,4},{1,5},{2,6},{3,7},{4,0},{5,1},{6,2},{7,3},{8,12},{9,13},{10,... | collective-permute-start | bytes 589832 | tf_op jit(solution)/shard_map/ppermute | solution.py:95
  132.3 6.7 %collective-permute-start.28 = (bf16[64,1536]{1,0:T(8,128)(2,1)S(1)}, bf16[64,1536]{1,0:T(8,128)(2,1)S(1)}, u32[]{:S(2)}, u32[]{:S(2)}) collective-permute-start(bf16[64,1536]{1,0:T(8,128)(2,1)S(1)} %fusion.5), channel_id=1, source_target_pairs={{0,1},{1,0},{2,3},{3,2},{4,5},{5,4},{6,7},{7,6},{8,9},{9,8},{10,11... | collective-permute-start | bytes 589832 | tf_op jit(solution)/shard_map/ppermute | solution.py:95
  136.9 9.0 %collective-permute-start.22 = (bf16[64,1664]{1,0:T(8,128)(2,1)S(1)}, bf16[64,1664]{1,0:T(8,128)(2,1)S(1)}, u32[]{:S(2)}, u32[]{:S(2)}) collective-permute-start(bf16[64,1664]{1,0:T(8,128)(2,1)S(1)} %fusion.1), channel_id=1, source_target_pairs={{0,3},{1,2},{2,1},{3,0},{4,7},{5,6},{6,5},{7,4},{8,11},{9,10},{10,... | collective-permute-start | bytes 638984 | tf_op jit(solution)/shard_map/ppermute | solution.py:95
  146.4 8.8 %collective-permute-start.29 = (bf16[64,768]{1,0:T(8,128)(2,1)S(1)}, bf16[64,768]{1,0:T(8,128)(2,1)S(1)}, u32[]{:S(2)}, u32[]{:S(2)}) collective-permute-start(bf16[64,768]{1,0:T(8,128)(2,1)S(1)} %pad_maximum_fusion.14), channel_id=1, source_target_pairs={{0,1},{1,0},{2,3},{3,2},{4,5},{5,4},{6,7},{7,6},{8,9},{9,8},{10,11... | collective-permute-start | bytes 294920 | tf_op jit(solution)/shard_map/ppermute | solution.py:95
  146.6 7.0 %collective-permute-start.32 = (bf16[64,768]{1,0:T(8,128)(2,1)S(1)}, bf16[64,768]{1,0:T(8,128)(2,1)S(1)}, u32[]{:S(2)}, u32[]{:S(2)}) collective-permute-start(bf16[64,768]{1,0:T(8,128)(2,1)S(1)} %pad_maximum_fusion.15), channel_id=1, source_target_pairs={{0,3},{1,2},{2,1},{3,0},{4,7},{5,6},{6,5},{7,4},{8,11},{9,10},{10,... | collective-permute-start | bytes 294920 | tf_op jit(solution)/shard_map/ppermute | solution.py:95
  146.7 7.8 %collective-permute-start.23 = (bf16[64,768]{1,0:T(8,128)(2,1)S(1)}, bf16[64,768]{1,0:T(8,128)(2,1)S(1)}, u32[]{:S(2)}, u32[]{:S(2)}) collective-permute-start(bf16[64,768]{1,0:T(8,128)(2,1)S(1)} %pad_maximum_fusion.13), channel_id=1, source_target_pairs={{0,4},{1,5},{2,6},{3,7},{4,0},{5,1},{6,2},{7,3},{8,12},{9,13},{10,... | collective-permute-start | bytes 294920 | tf_op jit(solution)/shard_map/ppermute | solution.py:95
  153.6 18.8 %copy-start.2 = (bf16[1152,896]{1,0:T(8,128)(2,1)S(1)}, bf16[1152,896]{1,0:T(8,128)(2,1)}, u32[]{:S(2)}) copy-start(bf16[1152,896]{1,0:T(8,128)(2,1)} %own_hbm.3) | copy-start | bytes 6193156
  153.6 5.7 %collective-permute-start.33 = (bf16[2,64,768]{2,1,0:T(8,128)(2,1)S(1)}, bf16[2,64,768]{2,1,0:T(8,128)(2,1)S(1)}, u32[]{:S(2)}, u32[]{:S(2)}) collective-permute-start(bf16[2,64,768]{2,1,0:T(8,128)(2,1)S(1)} %get-tuple-element.44), channel_id=1, source_target_pairs={{0,1},{1,0},{2,3},{3,2},{4,5},{5,4},{6,7},{7,6},{8,9},{9,8},{10,11... | collective-permute-start | bytes 589832 | tf_op jit(solution)/shard_map/ppermute | solution.py:95
  154.5 7.0 %collective-permute-start.24 = (bf16[2,64,768]{2,1,0:T(8,128)(2,1)S(1)}, bf16[2,64,768]{2,1,0:T(8,128)(2,1)S(1)}, u32[]{:S(2)}, u32[]{:S(2)}) collective-permute-start(bf16[2,64,768]{2,1,0:T(8,128)(2,1)S(1)} %get-tuple-element.48), channel_id=1, source_target_pairs={{0,3},{1,2},{2,1},{3,0},{4,7},{5,6},{6,5},{7,4},{8,11},{9,10},{10,... | collective-permute-start | bytes 589832 | tf_op jit(solution)/shard_map/ppermute | solution.py:95
  155.2 6.4 %collective-permute-start.30 = (bf16[2,64,768]{2,1,0:T(8,128)(2,1)S(1)}, bf16[2,64,768]{2,1,0:T(8,128)(2,1)S(1)}, u32[]{:S(2)}, u32[]{:S(2)}) collective-permute-start(bf16[2,64,768]{2,1,0:T(8,128)(2,1)S(1)} %get-tuple-element.46), channel_id=1, source_target_pairs={{0,4},{1,5},{2,6},{3,7},{4,0},{5,1},{6,2},{7,3},{8,12},{9,13},{10,... | collective-permute-start | bytes 589832 | tf_op jit(solution)/shard_map/ppermute | solution.py:95
  159.4 13.0 %collective-permute-start.34 = (bf16[2,2,64,768]{3,2,1,0:T(8,128)(2,1)S(1)}, bf16[2,2,64,768]{3,2,1,0:T(8,128)(2,1)S(1)}, u32[]{:S(2)}, u32[]{:S(2)}) collective-permute-start(bf16[2,2,64,768]{3,2,1,0:T(8,128)(2,1)S(1)} %pad_maximum_fusion.3.s2), channel_id=1, source_target_pairs={{0,4},{1,5},{2,6},{3,7},{4,0},{5,1},{6,2},{7,3},{8,12},{9,13},{10,... | collective-permute-start | bytes 1179656 | tf_op jit(solution)/shard_map/ppermute | solution.py:95
  161.5 10.9 %collective-permute-start.25 = (bf16[2,2,64,768]{3,2,1,0:T(8,128)(2,1)S(1)}, bf16[2,2,64,768]{3,2,1,0:T(8,128)(2,1)S(1)}, u32[]{:S(2)}, u32[]{:S(2)}) collective-permute-start(bf16[2,2,64,768]{3,2,1,0:T(8,128)(2,1)S(1)} %pad_maximum_fusion.1.s0), channel_id=1, source_target_pairs={{0,1},{1,0},{2,3},{3,2},{4,5},{5,4},{6,7},{7,6},{8,9},{9,8},{10,11... | collective-permute-start | bytes 1179656 | tf_op jit(solution)/shard_map/ppermute | solution.py:95
  161.7 10.7 %collective-permute-start.31 = (bf16[2,2,64,768]{3,2,1,0:T(8,128)(2,1)S(1)}, bf16[2,2,64,768]{3,2,1,0:T(8,128)(2,1)S(1)}, u32[]{:S(2)}, u32[]{:S(2)}) collective-permute-start(bf16[2,2,64,768]{3,2,1,0:T(8,128)(2,1)S(1)} %pad_maximum_fusion.2.s1), channel_id=1, source_target_pairs={{0,3},{1,2},{2,1},{3,0},{4,7},{5,6},{6,5},{7,4},{8,11},{9,10},{10,... | collective-permute-start | bytes 1179656 | tf_op jit(solution)/shard_map/ppermute | solution.py:95

commit v4 on v3

--- a/solution.py
+++ b/solution.py
@@ -70,8 +70,8 @@
         in_specs=[
             pl.BlockSpec(memory_space=pltpu.SMEM),
             pl.BlockSpec(memory_space=pltpu.VMEM),
-            pl.BlockSpec(memory_space=pl.ANY),
-            pl.BlockSpec(memory_space=pl.ANY),
+            pl.BlockSpec(memory_space=pltpu.HBM),
+            pl.BlockSpec(memory_space=pltpu.HBM),
         ],
         out_specs=pl.BlockSpec(memory_space=pltpu.VMEM),
         scratch_shapes=[
@@ -103,10 +103,6 @@
     return [pl.BlockSpec(memory_space=pltpu.VMEM)] * count
 
 
-def any_specs(count):
-    return [pl.BlockSpec(memory_space=pl.ANY)] * count
-
-
 SMEM = pl.BlockSpec(memory_space=pltpu.SMEM)
 
 
@@ -130,28 +126,17 @@
                     put(rows_at((f ^ j) * per, per), p, ref[b1, b2])
 
 
-def project_kernel(at_ref, s0, r0, s1, r1, s2, r2, own_hbm, sib_hbm, o_ref, x_ref, w_ref, sem):
-    copies = [
-        pltpu.make_async_copy(src, w_ref.at[i], sem.at[i])
-        for i, src in enumerate((own_hbm, sib_hbm))
-    ]
-    for copy in copies:
-        copy.start()
-
+def project_kernel(at_ref, s0, r0, s1, r1, s2, r2, low_ref, high_ref, o_ref, x_ref):
     def put(rows, p, piece):
         x_ref[rows, PROJECT_CUTS[p] : PROJECT_CUTS[p + 1]] = piece
 
     spread(at_ref, x_ref, (s0, r0, s1, r1, s2, r2), put)
-    for copy in copies:
-        copy.wait()
-    core = at_ref[0]
-    depth = w_ref.shape[1]
-    mine = x_ref[:, rows_at(core * depth, depth)]
-    other = x_ref[:, rows_at((1 - core) * depth, depth)]
+    depth = low_ref.shape[0]
+    low, high = x_ref[:, :depth], x_ref[:, depth:]
     for start, size in column_chunks(o_ref.shape[2]):
         cols = slice(start, start + size)
-        acc = jnp.dot(mine, w_ref[0, :, cols], preferred_element_type=F32) + jnp.dot(
-            other, w_ref[1, :, cols], preferred_element_type=F32
+        acc = jnp.dot(low, low_ref[:, cols], preferred_element_type=F32) + jnp.dot(
+            high, high_ref[:, cols], preferred_element_type=F32
         )
         for q in range(NQ):
             for t in range(4):
@@ -161,24 +146,20 @@
                 ).astype(BF)
 
 
-def project(at, pieces, own, sib):
-    depth, width = own.shape
+def project(at, pieces, low, high):
+    depth, width = low.shape
     rows = NQ * 64
     return pl.pallas_call(
         project_kernel,
         out_shape=jax.ShapeDtypeStruct((NQ, 64, width), BF),
-        in_specs=[SMEM] + vmem_specs(6) + any_specs(2),
+        in_specs=[SMEM] + vmem_specs(8),
         out_specs=pl.BlockSpec(memory_space=pltpu.VMEM),
-        scratch_shapes=[
-            pltpu.VMEM((rows, 2 * depth), BF),
-            pltpu.VMEM((2, depth, width), BF),
-            pltpu.SemaphoreType.DMA((2,)),
-        ],
-        compiler_params=pltpu.CompilerParams(vmem_limit_bytes=LIMIT),
+        scratch_shapes=[pltpu.VMEM((rows, 2 * depth), BF)],
+        compiler_params=pltpu.CompilerParams(vmem_limit_bytes=24 * MIB),
         cost_estimate=pl.CostEstimate(
             flops=4 * rows * depth * width, bytes_accessed=6 * MIB, transcendentals=0
         ),
-    )(at, *pieces, own, sib)
+    )(at, *pieces, low, high)
 
 
 def stream_kernel(got_ref, res_ref, gain_ref, stream_ref, scaled_ref):
@@ -204,23 +185,17 @@
 
 
 def hidden_kernel(at_ref, p0, p1, p2, p3, gain_ref, g0, u0, g1, u1, *refs):
-    outs, (x_ref, w_ref, sem) = refs[:-3], refs[-3:]
-    step = w_ref.shape[2]
-    weights, copies = (g0, u0, g1, u1), []
-    for part in range(NP):
-        for w, third in HIDDEN_BLOCKS[part]:
-            i = len(copies)
-            src = weights[w].at[:, pl.ds(third * step, step)]
-            copies.append(pltpu.make_async_copy(src, w_ref.at[i], sem.at[i]))
-            copies[-1].start()
+    outs, x_ref = refs[:-1], refs[-1]
+    step = g0.shape[1] // NP
     f, q = at_ref[1], at_ref[2]
     for k, ref in enumerate((p0, p1, p2, p3)):
         for z in range(2):
             x_ref[rows_at((f ^ q ^ (z * 4 + k)) * 64, 64), :] = ref[z]
     full = x_ref[...]
 
-    def put(acc, part, cols):
+    def put(acc, part, start):
         o = ORDER[part]
+        cols = slice(start, start + acc.shape[1])
         for b0 in range(2):
             ref = outs[2 * part + 1 - b0]
             for b1 in range(2):
@@ -230,21 +205,15 @@
 
     ratio = full.astype(F32) / gain_ref[...].astype(F32)
     square = jnp.sum(ratio * ratio, axis=1, keepdims=True)
-    put(jnp.broadcast_to(square, (full.shape[0], 128)), SQUARE_PART, slice(4 * step, 4 * step + 128))
-    for i, copy in enumerate(copies):
-        copy.wait()
-        acc = jnp.dot(full, w_ref[i], preferred_element_type=F32)
-        put(acc, i // 4, slice((i % 4) * step, (i % 4 + 1) * step))
-
-
-HIDDEN_BLOCKS = (
-    ((0, 0), (1, 0), (0, 1), (1, 1)),
-    ((0, 2), (1, 2), (2, 0), (3, 0)),
-    ((2, 1), (3, 1), (2, 2), (3, 2)),
-)
+    put(jnp.broadcast_to(square, (full.shape[0], 128)), SQUARE_PART, 4 * step)
+    for i, w in enumerate((g0, u0, g1, u1)):
+        acc = jnp.dot(full, w[...], preferred_element_type=F32)
+        for part in range(NP):
+            put(acc[:, part * step : (part + 1) * step], part, i * step)
+
+
 SQUARE_PART = 2
 PROJECT_CUTS = (0, 768, 1408, 2048)
-LIMIT = 48 * MIB
 
 
 def hidden(at, pieces, gain, weights):
@@ -257,14 +226,10 @@
     outs = pl.pallas_call(
         hidden_kernel,
         out_shape=tuple(shapes),
-        in_specs=[SMEM] + vmem_specs(5) + any_specs(4),
+        in_specs=[SMEM] + vmem_specs(9),
         out_specs=tuple(vmem_specs(2 * NP)),
-        scratch_shapes=[
-            pltpu.VMEM((rows, width), BF),
-            pltpu.VMEM((4 * NP, width, step), BF),
-            pltpu.SemaphoreType.DMA((4 * NP,)),
-        ],
-        compiler_params=pltpu.CompilerParams(vmem_limit_bytes=LIMIT),
+        scratch_shapes=[pltpu.VMEM((rows, width), BF)],
+        compiler_params=pltpu.CompilerParams(vmem_limit_bytes=24 * MIB),
         cost_estimate=pl.CostEstimate(
             flops=8 * rows * width * hid, bytes_accessed=14 * MIB, transcendentals=0
         ),
@@ -272,49 +237,64 @@
     return outs[0::2], outs[1::2]
 
 
-def down_kernel(at_ref, s0, r0, s1, r1, s2, r2, own_hbm, sib_hbm, o_ref, x_ref, w_ref, sem):
-    copies = [
-        pltpu.make_async_copy(src, w_ref.at[i], sem.at[i])
-        for i, src in enumerate((own_hbm, sib_hbm))
-    ]
-    for copy in copies:
-        copy.start()
-    step = s0.shape[3]
+def down_kernel(at_ref, s0, r0, s1, r1, s2, r2, low_ref, high_ref, o_ref, x_ref):
+    hid = low_ref.shape[0]
+    step = hid // NP
 
     def put(rows, p, piece):
-        x_ref[rows, p * step : (p + 1) * step] = piece
+        x_ref[rows, p * step : (p + 1) * step] = piece[:, :step]
+        x_ref[rows, hid + p * step : hid + (p + 1) * step] = piece[:, step:]
 
     spread(at_ref, x_ref, (s0, r0, s1, r1, s2, r2), put)
-    for copy in copies:
-        copy.wait()
-    hid = w_ref.shape[1]
-    mine, other = x_ref[:, :hid], x_ref[:, hid:]
+    low, high = x_ref[:, :hid], x_ref[:, hid:]
     for start, size in column_chunks(o_ref.shape[1]):
         cols = slice(start, start + size)
-        acc = jnp.dot(mine, w_ref[0, :, cols], preferred_element_type=F32) + jnp.dot(
-            other, w_ref[1, :, cols], preferred_element_type=F32
+        acc = jnp.dot(low, low_ref[:, cols], preferred_element_type=F32) + jnp.dot(
+            high, high_ref[:, cols], preferred_element_type=F32
         )
         o_ref[:, cols] = acc.astype(BF)
 
 
-def down(at, pieces, own, sib):
-    hid, width = own.shape
-    rows = NQ * 64
+def down(at, pieces, low, high):
+    hid, width = low.shape
+    rows = NQ * pieces[0].shape[2]
     return pl.pallas_call(
         down_kernel,
         out_shape=jax.ShapeDtypeStruct((rows, width), BF),
-        in_specs=[SMEM] + vmem_specs(6) + any_specs(2),
+        in_specs=[SMEM] + vmem_specs(8),
         out_specs=pl.BlockSpec(memory_space=pltpu.VMEM),
-        scratch_shapes=[
-            pltpu.VMEM((rows, 2 * hid), BF),
-            pltpu.VMEM((2, hid, width), BF),
-            pltpu.SemaphoreType.DMA((2,)),
-        ],
-        compiler_params=pltpu.CompilerParams(vmem_limit_bytes=LIMIT),
+        scratch_shapes=[pltpu.VMEM((rows, 2 * hid), BF)],
+        compiler_params=pltpu.CompilerParams(vmem_limit_bytes=24 * MIB),
         cost_estimate=pl.CostEstimate(
             flops=4 * rows * hid * width, bytes_accessed=6 * MIB, transcendentals=0
         ),
-    )(at, *pieces, own, sib)
+    )(at, *pieces, low, high)
+
+
+def last_kernel(got_ref, stream_ref, o_ref):
+    total = stream_ref[...]
+    for i in range(NQ):
+        total = total + got_ref[i].astype(F32)
+    nm = o_ref.shape[0]
+    r = o_ref.shape[1] // N_FFN
+    for m in range(nm):
+        rows = [total[(j * nm + m) * r : (j * nm + m + 1) * r] for j in range(N_FFN)]
+        o_ref[m] = jnp.concatenate(rows, axis=0).astype(BF)
+
+
+def last(got, stream, nm):
+    rows, width = stream.shape
+    return pl.pallas_call(
+        last_kernel,
+        out_shape=jax.ShapeDtypeStruct((nm, rows // nm, width), BF),
+        in_specs=vmem_specs(2),
+        out_specs=pl.BlockSpec(memory_space=pltpu.VMEM),
+        compiler_params=pltpu.CompilerParams(vmem_limit_bytes=16 * MIB),
+    )(got, stream)
+
+
+def by_core(a, own, sib):
+    return jnp.where(a % 2 == 0, own, sib), jnp.where(a % 2 == 0, sib, own)
 
 
 def scatter_ffn(sends, keeps):
@@ -371,13 +351,14 @@
         (got, out_sib, gate_sib, up_sib, down_sib)
     )
     pieces = gather_ffn([got[:, x:y] for x, y in zip(PROJECT_CUTS, PROJECT_CUTS[1:])])
-    part = project(at, pieces, out_weight, out_sib)
+    part = project(at, pieces, *by_core(a, out_weight, out_sib))
     stream, scaled = residual_stream(over_chips(part), res, gain)
 
     pair = jnp.stack([scaled, ax(scaled, 8)])
     pieces = [pair] + [ax(pair, 2 * k) for k in range(1, 4)]
-    weights = (gate_weight, up_weight, gate_sib, up_sib)
-    sends, keeps = hidden(at, pieces, gain, weights)
+    gate0, gate1 = by_core(a, gate_weight, gate_sib)
+    up0, up1 = by_core(a, up_weight, up_sib)
+    sends, keeps = hidden(at, pieces, gain, (gate0, up0, gate1, up1))
     sums = scatter_ffn(sends, keeps)
     step = gate_weight.shape[1] // NP
     inv = lax.rsqrt(sums[SQUARE_PART][:, 4 * step : 4 * step + 1] / D + 1e-06)
@@ -387,10 +368,8 @@
         acts.append(
             jnp.concatenate([jax.nn.silu(g0) * u0, jax.nn.silu(g1) * u1], axis=1).astype(BF)
         )
-    part = down(at, gather_ffn(acts), down_weight, down_sib).reshape(NQ, rows, w)
-    final = stream + jnp.sum(over_chips(part).astype(F32), axis=0)
-    final = final.astype(BF).reshape(N_FFN, nm, r, w)
-    return final.transpose(1, 0, 2, 3).reshape(nm, N_FFN * r, w)
+    part = down(at, gather_ffn(acts), *by_core(a, down_weight, down_sib)).reshape(NQ, rows, w)
+    return last(over_chips(part), stream, nm)
 
 
 def solution(mesh):

time: 194 us -> 183 us (0.943)
  blocking collectives: 31.3 us -> 15 us
  Pallas kernels: 30.8 us -> 23.2 us
  other arithmetic: 1.86 us -> 9.31 us
  starting transfers between devices: 38.1 us -> 41.5 us
  waiting for transfers between devices: 86.6 us -> 89.4 us
    all_to_all x2 -> x1, blocking collectives: 31.3 us -> 15 us  [over_chips(): return lax.all_to_all(x, 'attn', 0, 0, axis_index_groups=PLANES)]
    all_to_all x1 -> x2, waiting for transfers between devices: 12.2 us -> 20.9 us  [over_chips(): return lax.all_to_all(x, 'attn', 0, 0, axis_index_groups=PLANES)]
    all_to_all x1 -> x2, starting transfers between devices: 3.72 us -> 11.4 us  [over_chips(): return lax.all_to_all(x, 'attn', 0, 0, axis_index_groups=PLANES)]
    select_n x0 -> x3, other arithmetic: none -> 7.59 us  [by_core(): return (jnp.where(a % 2 == 0, own, sib), jnp.where(a % 2 == 0, sib, own))]
    ppermute x27, starting transfers between devices: 28.6 us -> 23.8 us  [fx(): return lax.ppermute(x, 'ffn', [(i, i ^ k) for i in range(N_FFN)])]
    pallas_call x1, Pallas kernels: 10.4 us -> 6.15 us  [hidden(): pl.pallas_call(hidden_kernel, out_shape=tuple(shapes), in_specs=[SMEM] +...]
    ppermute x27, waiting for transfers between devices: 62.2 us -> 59.1 us  [fx(): return lax.ppermute(x, 'ffn', [(i, i ^ k) for i in range(N_FFN)])]
    ppermute x8, waiting for transfers between devices: 12.2 us -> 9.35 us  [ax(): return lax.ppermute(x, 'attn', [(i, i ^ k) for i in range(N_ATTN)])]
  transfers between devices with their start and end apart: 36 -> 37, of which waited for: 21 -> 22; matrix products, arithmetic and copies ran while one was open for 1% -> 6% of each run, Pallas kernels for 5% -> 5%
where the time goes in v4:
time: 183 us; the launch traced here: 182 us
  waiting for transfers between devices  89.4 us (49%)
  starting transfers between devices  41.5 us (23%)
  Pallas kernels  23.2 us (13%)
  blocking collectives  15 us (8%)
  other arithmetic  9.31 us (5%)
  local copies, waits for them, and re-layouts  3.14 us (2%)
    ppermute x27, waiting for transfers between devices, fx(): return lax.ppermute(x, 'ffn', [(i, i ^ k) for i in range(N_FFN)])  59.1 us
    ppermute x27, starting transfers between devices, fx(): return lax.ppermute(x, 'ffn', [(i, i ^ k) for i in range(N_FFN)])  23.8 us
    all_to_all x2, waiting for transfers between devices, over_chips(): return lax.all_to_all(x, 'attn', 0, 0, axis_index_groups=PLANES)  20.9 us
    all_to_all x1, blocking collectives, over_chips(): return lax.all_to_all(x, 'attn', 0, 0, axis_index_groups=PLANES)  15 us
    all_to_all x2, starting transfers between devices, over_chips(): return lax.all_to_all(x, 'attn', 0, 0, axis_index_groups=PLANES)  11.4 us
    pallas_call x1, Pallas kernels, attend(): pl.pallas_call(attend_kernel, out_shape=jax.ShapeDtypeStruct((n, h, hd),...  9.56 us
    ppermute x8, waiting for transfers between devices, ax(): return lax.ppermute(x, 'attn', [(i, i ^ k) for i in range(N_ATTN)])  9.35 us
    select_n x3, other arithmetic, by_core(): return (jnp.where(a % 2 == 0, own, sib), jnp.where(a % 2 == 0, sib, own))  7.59 us
  transfers between devices with their start and end apart: 37, of which 22 were waited for; matrix products, arithmetic and copies ran while one was open for 6% of the time, Pallas kernels for 5%

profile of v4, /device:TPU:0, one launch (start us, length us, event | category | flops | bytes accessed | tf_op | source)
XLA Modules:
  0.0 182.0 jit_solution(13582232039850354060)
XLA Ops:
  1.0 9.6 %shard_map.100 = bf16[8,64,256]{2,1,0:T(8,128)(2,1)} custom-call(s32[2,4]{1,0:T(2,128)} %len_ref.1, bf16[2,4,64,256]{3,2,1,0:T(8,128)(2,1)} %q_ref.1, bf16[2,4,1536,256]{3,2,1,0:T(8,128)(2,1)} %k_hbm.1, bf16[2,4,1536,256]{3,2,1,0:T(8,128)(2,1)} %v_hbm.1), custom_call_target="tpu_custom_call" | custom-call | flops 805306368 | bytes 12582912 | tf_op jit(solution)/shard_map/pallas_call | solution.py:67
  10.6 1.1 reshape.153
  12.5 7.7 %all-to-all-start = ((bf16[8,8,2048]{2,1,0:T(8,128)(2,1)}), bf16[8,8,2048]{2,1,0:T(8,128)(2,1)S(1)}, u32[]{:S(2)}, u32[]{:S(2)}) async-start(bf16[8,8,2048]{2,1,0:T(8,128)(2,1)} %bitcast.96), calls=%async_computation | async-start | bytes 524288 | tf_op jit(solution)/shard_map/all_to_all | solution.py:99
  20.3 8.9 %all-to-all-done = bf16[8,8,2048]{2,1,0:T(8,128)(2,1)S(1)} async-done(((bf16[8,8,2048]{2,1,0:T(8,128)(2,1)}), bf16[8,8,2048]{2,1,0:T(8,128)(2,1)S(1)}, u32[]{:S(2)}, u32[]{:S(2)}) %all-to-all-start) | async-done | bytes 262176 | tf_op jit(solution)/shard_map/all_to_all | solution.py:99
  29.3 3.1 %collective-permute-start.10 = (bf16[64,640]{1,0:T(8,128)(2,1)S(1)}, bf16[64,640]{1,0:T(8,128)(2,1)S(1)}, u32[]{:S(2)}, u32[]{:S(2)}) collective-permute-start(bf16[64,640]{1,0:T(8,128)(2,1)S(1)} %get-tuple-element.47), channel_id=1, source_target_pairs={{0,3},{1,2},{2,1},{3,0},{4,7},{5,6},{6,5},{7,4},{8,11},{9,10},{10,... | collective-permute-start | bytes 245768 | tf_op jit(solution)/shard_map/ppermute | solution.py:95
  33.7 1.4 collective-permute-done.10
  35.7 2.1 %collective-permute-done.7 = bf16[64,640]{1,0:T(8,128)(2,1)S(1)} collective-permute-done((bf16[64,640]{1,0:T(8,128)(2,1)S(1)}, bf16[64,640]{1,0:T(8,128)(2,1)S(1)}, u32[]{:S(2)}, u32[]{:S(2)}) %collective-permute-start.7) | collective-permute-done | bytes 81952 | tf_op jit(solution)/shard_map/ppermute | solution.py:95
  37.8 1.1 collective-permute-start.8
  39.5 1.0 collective-permute-done.11
  40.5 1.1 collective-permute-start.12
  41.6 3.3 %collective-permute-done.8 = bf16[2,64,640]{2,1,0:T(8,128)(2,1)S(1)} collective-permute-done((bf16[2,64,640]{2,1,0:T(8,128)(2,1)S(1)}, bf16[2,64,640]{2,1,0:T(8,128)(2,1)S(1)}, u32[]{:S(2)}, u32[]{:S(2)}) %collective-permute-start.8) | collective-permute-done | bytes 163872 | tf_op jit(solution)/shard_map/ppermute | solution.py:95
  45.1 2.9 %collective-permute-done.5 = bf16[2,64,768]{2,1,0:T(8,128)(2,1)S(1)} collective-permute-done((bf16[2,64,768]{2,1,0:T(8,128)(2,1)S(1)}, bf16[2,64,768]{2,1,0:T(8,128)(2,1)S(1)}, u32[]{:S(2)}, u32[]{:S(2)}) %collective-permute-start.5) | collective-permute-done | bytes 196640 | tf_op jit(solution)/shard_map/ppermute | solution.py:95
  48.1 1.9 %broadcast_select_fusion.6 = (bf16[1024,896]{1,0:T(8,128)(2,1)S(1)}, bf16[1024,896]{1,0:T(8,128)(2,1)S(1)}) fusion(bf16[1024,896]{1,0:T(8,128)(2,1)} %collective-permute-done, bf16[1024,896]{1,0:T(8,128)(2,1)S(1)} %copy-done.4, pred[]{:T(512)S(6)} %eq.20), kind=kLoop, calls=%fused_computation.6 | loop fusion | flops 1835008 | bytes 7340033 | tf_op jit(solution)/shard_map/jit(_where)/select_n | solution.py:297
  50.0 3.3 %collective-permute-done.9.r1 = bf16[2,2,64,640]{3,2,1,0:T(8,128)(2,1)S(1)} collective-permute-done((bf16[2,2,64,640]{3,2,1,0:T(8,128)(2,1)S(1)}, bf16[2,2,64,640]{3,2,1,0:T(8,128)(2,1)S(1)}, u32[]{:S(2)}, u32[]{:S(2)}) %collective-permute-start.9) | collective-permute-done | bytes 327712 | tf_op jit(solution)/shard_map/ppermute | solution.py:95
  53.3 2.5 %collective-permute-done.6.r0 = bf16[2,2,64,768]{3,2,1,0:T(8,128)(2,1)S(1)} collective-permute-done((bf16[2,2,64,768]{3,2,1,0:T(8,128)(2,1)S(1)}, bf16[2,2,64,768]{3,2,1,0:T(8,128)(2,1)S(1)}, u32[]{:S(2)}, u32[]{:S(2)}) %collective-permute-start.6) | collective-permute-done | bytes 393248 | tf_op jit(solution)/shard_map/ppermute | solution.py:95
  55.9 3.0 %shard_map.101 = bf16[8,64,896]{2,1,0:T(8,128)(2,1)S(1)} custom-call(s32[3]{0:T(128)S(1)} %pad_add_fusion.at_ref, bf16[2,2,64,768]{3,2,1,0:T(8,128)(2,1)S(1)} %pad_maximum_fusion.s0, bf16[2,2,64,768]{3,2,1,0:T(8,128)(2,1)S(1)} %collective-permute-done.6.r0, bf16[2,2,64,640]{3,2,1,0:T(8,128)(2,1)S(1)} %pad_maximum_fusion.4.s1, ...), custom_call_target="tpu_custom_call" | custom-call | flops 1879048192 | bytes 6291456 | tf_op jit(solution)/shard_map/pallas_call | solution.py:152
  59.8 3.7 %all-to-all-start.1 = ((bf16[8,64,896]{2,1,0:T(8,128)(2,1)}), bf16[8,64,896]{2,1,0:T(8,128)(2,1)S(1)}, u32[]{:S(2)}, u32[]{:S(2)}) async-start(bf16[8,64,896]{2,1,0:T(8,128)(2,1)} %copy-done.2), calls=%async_computation.1 | async-start | bytes 1835008 | tf_op jit(solution)/shard_map/all_to_all | solution.py:99
  63.8 12.0 %all-to-all-done.1.got_ref = bf16[8,64,896]{2,1,0:T(8,128)(2,1)S(1)} async-done(((bf16[8,64,896]{2,1,0:T(8,128)(2,1)}), bf16[8,64,896]{2,1,0:T(8,128)(2,1)S(1)}, u32[]{:S(2)}, u32[]{:S(2)}) %all-to-all-start.1) | async-done | bytes 917536 | tf_op jit(solution)/shard_map/all_to_all | solution.py:99
  76.5 5.8 %collective-permute-done.13 = bf16[64,896]{1,0:T(8,128)(2,1)S(1)} collective-permute-done((bf16[64,896]{1,0:T(8,128)(2,1)S(1)}, bf16[64,896]{1,0:T(8,128)(2,1)S(1)}, u32[]{:S(2)}, u32[]{:S(2)}) %collective-permute-start.13) | collective-permute-done | bytes 114720 | tf_op jit(solution)/shard_map/ppermute | solution.py:91
  82.3 1.0 collective-permute-start.14
  83.4 2.2 %collective-permute-start.15 = (bf16[2,64,896]{2,1,0:T(8,128)(2,1)S(1)}, bf16[2,64,896]{2,1,0:T(8,128)(2,1)S(1)}, u32[]{:S(2)}, u32[]{:S(2)}) collective-permute-start(bf16[2,64,896]{2,1,0:T(8,128)(2,1)S(1)} %pad_maximum_fusion.6.p0), channel_id=1, source_target_pairs={{0,32},{8,40},{16,48},{24,56},{32,0},{40,8},{48,16},{56,24},{64,96... | collective-permute-start | bytes 688136 | tf_op jit(solution)/shard_map/ppermute | solution.py:91
  85.5 1.6 collective-permute-start.16
  87.1 3.8 %broadcast_select_fusion.2 = (bf16[896,1152]{1,0:T(8,128)(2,1)S(1)}, bf16[896,1152]{1,0:T(8,128)(2,1)S(1)}, bf16[896,1152]{1,0:T(8,128)(2,1)S(1)}, bf16[896,1152]{1,0:T(8,128)(2,1)S(1)}) fusion(bf16[896,1152]{1,0:T(8,128)(2,1)} %collective-permute-done.2, bf16[896,1152]{1,0:T(8,128)(2,1)} %param.18, pred[]{:T(512)S(6)} %eq.20, bf16[896,1152]{1,0:T(8,128)(2,1)} %param.17, ...), kind=kLoop, calls=%fused_computation.2 | loop fusion | flops 4128768 | bytes 16515073 | tf_op jit(solution)/shard_map/jit(_where)/select_n | solution.py:297
  90.9 1.2 collective-permute-done.15.p2
  92.1 2.4 %collective-permute-done.16.p3 = bf16[2,64,896]{2,1,0:T(8,128)(2,1)S(1)} collective-permute-done((bf16[2,64,896]{2,1,0:T(8,128)(2,1)S(1)}, bf16[2,64,896]{2,1,0:T(8,128)(2,1)S(1)}, u32[]{:S(2)}, u32[]{:S(2)}) %collective-permute-start.16) | collective-permute-done | bytes 229408 | tf_op jit(solution)/shard_map/ppermute | solution.py:91
  94.5 6.2 %shard_map.103 = (bf16[2,2,64,1536]{3,2,1,0:T(8,128)(2,1)S(1)}, bf16[2,2,64,1536]{3,2,1,0:T(8,128)(2,1)S(1)}, bf16[2,2,64,1536]{3,2,1,0:T(8,128)(2,1)S(1)}, bf16...) custom-call(s32[3]{0:T(128)S(1)} %pad_add_fusion.at_ref, ...), custom_call_target="tpu_custom_call" | custom-call | flops 4227858432 | bytes 14680064 | tf_op jit(solution)/shard_map/pallas_call | solution.py:226
  100.8 1.1 collective-permute-start.20
  101.9 15.8 %collective-permute-done.26 = bf16[2,2,64,1536]{3,2,1,0:T(8,128)(2,1)S(1)} collective-permute-done((bf16[2,2,64,1536]{3,2,1,0:T(8,128)(2,1)S(1)}, bf16[2,2,64,1536]{3,2,1,0:T(8,128)(2,1)S(1)}, u32[]{:S(2)}, u32[]{:S(2)}) %collective-permute-start.26) | collective-permute-done | bytes 786464 | tf_op jit(solution)/shard_map/ppermute | solution.py:95
  117.7 1.1 collective-permute-start.27
  120.2 6.8 %collective-permute-done.27 = bf16[2,64,1536]{2,1,0:T(8,128)(2,1)S(1)} collective-permute-done((bf16[2,64,1536]{2,1,0:T(8,128)(2,1)S(1)}, bf16[2,64,1536]{2,1,0:T(8,128)(2,1)S(1)}, u32[]{:S(2)}, u32[]{:S(2)}) %collective-permute-start.27) | collective-permute-done | bytes 393248 | tf_op jit(solution)/shard_map/ppermute | solution.py:95
  127.2 2.1 %collective-permute-done.18 = bf16[2,64,1536]{2,1,0:T(8,128)(2,1)S(1)} collective-permute-done((bf16[2,64,1536]{2,1,0:T(8,128)(2,1)S(1)}, bf16[2,64,1536]{2,1,0:T(8,128)(2,1)S(1)}, u32[]{:S(2)}, u32[]{:S(2)}) %collective-permute-start.18) | collective-permute-done | bytes 393248 | tf_op jit(solution)/shard_map/ppermute | solution.py:95
  129.4 1.1 collective-permute-start.19
  130.5 1.9 %collective-permute-start.22 = (bf16[64,1664]{1,0:T(8,128)(2,1)S(1)}, bf16[64,1664]{1,0:T(8,128)(2,1)S(1)}, u32[]{:S(2)}, u32[]{:S(2)}) collective-permute-start(bf16[64,1664]{1,0:T(8,128)(2,1)S(1)} %fusion.1), channel_id=1, source_target_pairs={{0,3},{1,2},{2,1},{3,0},{4,7},{5,6},{6,5},{7,4},{8,11},{9,10},{10,... | collective-permute-start | bytes 638984 | tf_op jit(solution)/shard_map/ppermute | solution.py:95
  132.4 1.1 collective-permute-done.28
  133.6 1.8 collective-permute-done.19
  135.5 2.2 %collective-permute-done.22 = bf16[64,1664]{1,0:T(8,128)(2,1)S(1)} collective-permute-done((bf16[64,1664]{1,0:T(8,128)(2,1)S(1)}, bf16[64,1664]{1,0:T(8,128)(2,1)S(1)}, u32[]{:S(2)}, u32[]{:S(2)}) %collective-permute-start.22) | collective-permute-done | bytes 213024 | tf_op jit(solution)/shard_map/ppermute | solution.py:95
  138.2 2.0 %collective-permute-start.32 = (bf16[64,768]{1,0:T(8,128)(2,1)S(1)}, bf16[64,768]{1,0:T(8,128)(2,1)S(1)}, u32[]{:S(2)}, u32[]{:S(2)}) collective-permute-start(bf16[64,768]{1,0:T(8,128)(2,1)S(1)} %pad_maximum_fusion.15), channel_id=1, source_target_pairs={{0,3},{1,2},{2,1},{3,0},{4,7},{5,6},{6,5},{7,4},{8,11},{9,10},{10,... | collective-permute-start | bytes 294920 | tf_op jit(solution)/shard_map/ppermute | solution.py:95
  140.3 1.1 collective-permute-start.23
  141.4 3.7 %collective-permute-done.32 = bf16[64,768]{1,0:T(8,128)(2,1)S(1)} collective-permute-done((bf16[64,768]{1,0:T(8,128)(2,1)S(1)}, bf16[64,768]{1,0:T(8,128)(2,1)S(1)}, u32[]{:S(2)}, u32[]{:S(2)}) %collective-permute-start.32) | collective-permute-done | bytes 98336 | tf_op jit(solution)/shard_map/ppermute | solution.py:95
  145.9 1.1 collective-permute-start.30
  147.1 1.4 collective-permute-start.24
  148.4 2.5 %collective-permute-done.33 = bf16[2,64,768]{2,1,0:T(8,128)(2,1)S(1)} collective-permute-done((bf16[2,64,768]{2,1,0:T(8,128)(2,1)S(1)}, bf16[2,64,768]{2,1,0:T(8,128)(2,1)S(1)}, u32[]{:S(2)}, u32[]{:S(2)}) %collective-permute-start.33) | collective-permute-done | bytes 196640 | tf_op jit(solution)/shard_map/ppermute | solution.py:95
  151.0 1.1 collective-permute-start.34
  152.2 1.9 %collective-permute-start.31 = (bf16[2,2,64,768]{3,2,1,0:T(8,128)(2,1)S(1)}, bf16[2,2,64,768]{3,2,1,0:T(8,128)(2,1)S(1)}, u32[]{:S(2)}, u32[]{:S(2)}) collective-permute-start(bf16[2,2,64,768]{3,2,1,0:T(8,128)(2,1)S(1)} %pad_maximum_fusion.2.s1), channel_id=1, source_target_pairs={{0,3},{1,2},{2,1},{3,0},{4,7},{5,6},{6,5},{7,4},{8,11},{9,10},{10,... | collective-permute-start | bytes 1179656 | tf_op jit(solution)/shard_map/ppermute | solution.py:95
  154.8 2.0 %broadcast_select_fusion = (bf16[1152,896]{1,0:T(8,128)(2,1)S(1)}, bf16[1152,896]{1,0:T(8,128)(2,1)S(1)}) fusion(bf16[1152,896]{1,0:T(8,128)(2,1)} %collective-permute-done.3, bf16[1152,896]{1,0:T(8,128)(2,1)S(1)} %copy-done.3, pred[]{:T(512)S(6)} %eq.20), kind=kLoop, calls=%fused_computation | loop fusion | flops 2064384 | bytes 8257537 | tf_op jit(solution)/shard_map/jit(_where)/select_n | solution.py:297
  156.8 5.8 %collective-permute-done.34.r2 = bf16[2,2,64,768]{3,2,1,0:T(8,128)(2,1)S(1)} collective-permute-done((bf16[2,2,64,768]{3,2,1,0:T(8,128)(2,1)S(1)}, bf16[2,2,64,768]{3,2,1,0:T(8,128)(2,1)S(1)}, u32[]{:S(2)}, u32[]{:S(2)}) %collective-permute-start.34) | collective-permute-done | bytes 393248 | tf_op jit(solution)/shard_map/ppermute | solution.py:95
  162.6 3.5 %shard_map.104 = bf16[512,896]{1,0:T(8,128)(2,1)S(1)} custom-call(s32[3]{0:T(128)S(1)} %pad_add_fusion.at_ref, bf16[2,2,64,768]{3,2,1,0:T(8,128)(2,1)S(1)} %pad_maximum_fusion.1.s0, bf16[2,2,64,768]{3,2,1,0:T(8,128)(2,1)S(1)} %collective-permute-done.25.r0, bf16[2,2,64,768]{3,2,1,0:T(8,128)(2,1)S(1)} %pad_maximum_fusion.2.s1, ...), custom_call_target="tpu_custom_call" | custom-call | flops 2113929216 | bytes 6291456 | tf_op jit(solution)/shard_map/pallas_call | solution.py:261
  166.1 15.0 %all_to_all.15.got_ref = bf16[8,64,896]{2,1,0:T(8,128)(2,1)S(1)} all-to-all(bf16[8,64,896]{2,1,0:T(8,128)(2,1)S(1)} %bitcast.97), channel_id=1, replica_groups={{0,16,32,48,64,80,96,112},{8,24,40,56,72,88,104,120},{1,17,33,49,65,81,..., dimensions={0} | all-to-all | bytes 1835008 | tf_op jit(solution)/shard_map/all_to_all | solution.py:99
  (85 shorter events, 11.9 us)
Async XLA Ops:
  0.0 63.5 %copy-start = (bf16[2,512,896]{2,1,0:T(8,128)(2,1)S(1)}, bf16[2,512,896]{2,1,0:T(8,128)(2,1)}, u32[]{:S(2)}) copy-start(bf16[2,512,896]{2,1,0:T(8,128)(2,1)} %param.14) | copy-start | bytes 5505028
  0.0 29.3 %collective-permute-start.1 = (bf16[896,1152]{1,0:T(8,128)(2,1)}, bf16[896,1152]{1,0:T(8,128)(2,1)}, u32[]{:S(2)}, u32[]{:S(2)}) collective-permute-start(bf16[896,1152]{1,0:T(8,128)(2,1)} %param.17), channel_id=1, source_target_pairs={{0,8},{8,0},{16,24},{24,16},{32,40},{40,32},{48,56},{56,48},{64,72... | collective-permute-start | bytes 6193160 | tf_op jit(solution)/shard_map/ppermute | solution.py:91
  0.0 29.3 %collective-permute-start.2 = (bf16[896,1152]{1,0:T(8,128)(2,1)}, bf16[896,1152]{1,0:T(8,128)(2,1)}, u32[]{:S(2)}, u32[]{:S(2)}) collective-permute-start(bf16[896,1152]{1,0:T(8,128)(2,1)} %param.18), channel_id=1, source_target_pairs={{0,8},{8,0},{16,24},{24,16},{32,40},{40,32},{48,56},{56,48},{64,72... | collective-permute-start | bytes 6193160 | tf_op jit(solution)/shard_map/ppermute | solution.py:91
  0.5 28.8 %collective-permute-start.3 = (bf16[1152,896]{1,0:T(8,128)(2,1)}, bf16[1152,896]{1,0:T(8,128)(2,1)}, u32[]{:S(2)}, u32[]{:S(2)}) collective-permute-start(bf16[1152,896]{1,0:T(8,128)(2,1)} %param.19), channel_id=1, source_target_pairs={{0,8},{8,0},{16,24},{24,16},{32,40},{40,32},{48,56},{56,48},{64,72... | collective-permute-start | bytes 6193160 | tf_op jit(solution)/shard_map/ppermute | solution.py:91
  0.5 28.7 %collective-permute-start = (bf16[1024,896]{1,0:T(8,128)(2,1)}, bf16[1024,896]{1,0:T(8,128)(2,1)}, u32[]{:S(2)}, u32[]{:S(2)}) collective-permute-start(bf16[1024,896]{1,0:T(8,128)(2,1)} %param.16), channel_id=1, source_target_pairs={{0,8},{8,0},{16,24},{24,16},{32,40},{40,32},{48,56},{56,48},{64,72... | collective-permute-start | bytes 5505032 | tf_op jit(solution)/shard_map/ppermute | solution.py:91
  12.5 16.7 %all-to-all-start = ((bf16[8,8,2048]{2,1,0:T(8,128)(2,1)}), bf16[8,8,2048]{2,1,0:T(8,128)(2,1)S(1)}, u32[]{:S(2)}, u32[]{:S(2)}) async-start(bf16[8,8,2048]{2,1,0:T(8,128)(2,1)} %bitcast.96), calls=%async_computation | async-start | bytes 524288 | tf_op jit(solution)/shard_map/all_to_all | solution.py:99
  29.3 18.8 %copy-start.4 = (bf16[1024,896]{1,0:T(8,128)(2,1)S(1)}, bf16[1024,896]{1,0:T(8,128)(2,1)}, u32[]{:S(2)}) copy-start(bf16[1024,896]{1,0:T(8,128)(2,1)} %param.16) | copy-start | bytes 5505028
  29.3 5.7 %collective-permute-start.10 = (bf16[64,640]{1,0:T(8,128)(2,1)S(1)}, bf16[64,640]{1,0:T(8,128)(2,1)S(1)}, u32[]{:S(2)}, u32[]{:S(2)}) collective-permute-start(bf16[64,640]{1,0:T(8,128)(2,1)S(1)} %get-tuple-element.47), channel_id=1, source_target_pairs={{0,3},{1,2},{2,1},{3,0},{4,7},{5,6},{6,5},{7,4},{8,11},{9,10},{10,... | collective-permute-start | bytes 245768 | tf_op jit(solution)/shard_map/ppermute | solution.py:95
  32.4 5.3 %collective-permute-start.7 = (bf16[64,640]{1,0:T(8,128)(2,1)S(1)}, bf16[64,640]{1,0:T(8,128)(2,1)S(1)}, u32[]{:S(2)}, u32[]{:S(2)}) collective-permute-start(bf16[64,640]{1,0:T(8,128)(2,1)S(1)} %get-tuple-element.48), channel_id=1, source_target_pairs={{0,1},{1,0},{2,3},{3,2},{4,5},{5,4},{6,7},{7,6},{8,9},{9,8},{10,11... | collective-permute-start | bytes 245768 | tf_op jit(solution)/shard_map/ppermute | solution.py:95
  32.7 6.2 %collective-permute-start.4 = (bf16[64,768]{1,0:T(8,128)(2,1)S(1)}, bf16[64,768]{1,0:T(8,128)(2,1)S(1)}, u32[]{:S(2)}, u32[]{:S(2)}) collective-permute-start(bf16[64,768]{1,0:T(8,128)(2,1)S(1)} %get-tuple-element.50), channel_id=1, source_target_pairs={{0,4},{1,5},{2,6},{3,7},{4,0},{5,1},{6,2},{7,3},{8,12},{9,13},{10,... | collective-permute-start | bytes 294920 | tf_op jit(solution)/shard_map/ppermute | solution.py:95
  35.1 5.4 %collective-permute-start.11 = (bf16[2,64,640]{2,1,0:T(8,128)(2,1)S(1)}, bf16[2,64,640]{2,1,0:T(8,128)(2,1)S(1)}, u32[]{:S(2)}, u32[]{:S(2)}) collective-permute-start(bf16[2,64,640]{2,1,0:T(8,128)(2,1)S(1)} %get-tuple-element.60), channel_id=1, source_target_pairs={{0,1},{1,0},{2,3},{3,2},{4,5},{5,4},{6,7},{7,6},{8,9},{9,8},{10,11... | collective-permute-start | bytes 491528 | tf_op jit(solution)/shard_map/ppermute | solution.py:95
  37.8 7.1 %collective-permute-start.8 = (bf16[2,64,640]{2,1,0:T(8,128)(2,1)S(1)}, bf16[2,64,640]{2,1,0:T(8,128)(2,1)S(1)}, u32[]{:S(2)}, u32[]{:S(2)}) collective-permute-start(bf16[2,64,640]{2,1,0:T(8,128)(2,1)S(1)} %get-tuple-element.62), channel_id=1, source_target_pairs={{0,4},{1,5},{2,6},{3,7},{4,0},{5,1},{6,2},{7,3},{8,12},{9,13},{10,... | collective-permute-start | bytes 491528 | tf_op jit(solution)/shard_map/ppermute | solution.py:95
  38.9 9.0 %collective-permute-start.5 = (bf16[2,64,768]{2,1,0:T(8,128)(2,1)S(1)}, bf16[2,64,768]{2,1,0:T(8,128)(2,1)S(1)}, u32[]{:S(2)}, u32[]{:S(2)}) collective-permute-start(bf16[2,64,768]{2,1,0:T(8,128)(2,1)S(1)} %get-tuple-element.58), channel_id=1, source_target_pairs={{0,3},{1,2},{2,1},{3,0},{4,7},{5,6},{6,5},{7,4},{8,11},{9,10},{10,... | collective-permute-start | bytes 589832 | tf_op jit(solution)/shard_map/ppermute | solution.py:95
  40.5 9.5 %collective-permute-start.12 = (bf16[2,2,64,640]{3,2,1,0:T(8,128)(2,1)S(1)}, bf16[2,2,64,640]{3,2,1,0:T(8,128)(2,1)S(1)}, u32[]{:S(2)}, u32[]{:S(2)}) collective-permute-start(bf16[2,2,64,640]{3,2,1,0:T(8,128)(2,1)S(1)} %pad_maximum_fusion.5.s2), channel_id=1, source_target_pairs={{0,4},{1,5},{2,6},{3,7},{4,0},{5,1},{6,2},{7,3},{8,12},{9,13},{10,... | collective-permute-start | bytes 983048 | tf_op jit(solution)/shard_map/ppermute | solution.py:95
  45.0 8.4 %collective-permute-start.9 = (bf16[2,2,64,640]{3,2,1,0:T(8,128)(2,1)S(1)}, bf16[2,2,64,640]{3,2,1,0:T(8,128)(2,1)S(1)}, u32[]{:S(2)}, u32[]{:S(2)}) collective-permute-start(bf16[2,2,64,640]{3,2,1,0:T(8,128)(2,1)S(1)} %pad_maximum_fusion.4.s1), channel_id=1, source_target_pairs={{0,3},{1,2},{2,1},{3,0},{4,7},{5,6},{6,5},{7,4},{8,11},{9,10},{10,... | collective-permute-start | bytes 983048 | tf_op jit(solution)/shard_map/ppermute | solution.py:95
  48.0 7.9 %collective-permute-start.6 = (bf16[2,2,64,768]{3,2,1,0:T(8,128)(2,1)S(1)}, bf16[2,2,64,768]{3,2,1,0:T(8,128)(2,1)S(1)}, u32[]{:S(2)}, u32[]{:S(2)}) collective-permute-start(bf16[2,2,64,768]{3,2,1,0:T(8,128)(2,1)S(1)} %pad_maximum_fusion.s0), channel_id=1, source_target_pairs={{0,1},{1,0},{2,3},{3,2},{4,5},{5,4},{6,7},{7,6},{8,9},{9,8},{10,11... | collective-permute-start | bytes 1179656 | tf_op jit(solution)/shard_map/ppermute | solution.py:95
  58.9 1.0 copy-start.2
  59.8 3.9 %copy-start.5 = (bf16[896]{0:T(1024)(128)(2,1)S(1)}, bf16[896]{0:T(1024)(128)(2,1)}, u32[]{:S(2)}) copy-start(bf16[896]{0:T(1024)(128)(2,1)} %param.15) | copy-start | bytes 5380
  59.8 15.9 %all-to-all-start.1 = ((bf16[8,64,896]{2,1,0:T(8,128)(2,1)}), bf16[8,64,896]{2,1,0:T(8,128)(2,1)S(1)}, u32[]{:S(2)}, u32[]{:S(2)}) async-start(bf16[8,64,896]{2,1,0:T(8,128)(2,1)} %copy-done.2), calls=%async_computation.1 | async-start | bytes 1835008 | tf_op jit(solution)/shard_map/all_to_all | solution.py:99
  75.9 6.4 %collective-permute-start.13 = (bf16[64,896]{1,0:T(8,128)(2,1)S(1)}, bf16[64,896]{1,0:T(8,128)(2,1)S(1)}, u32[]{:S(2)}, u32[]{:S(2)}) collective-permute-start(bf16[64,896]{1,0:T(8,128)(2,1)S(1)} %get-tuple-element.20), channel_id=1, source_target_pairs={{0,64},{8,72},{16,80},{24,88},{32,96},{40,104},{48,112},{56,120},{... | collective-permute-start | bytes 344072 | tf_op jit(solution)/shard_map/ppermute | solution.py:91
  82.3 8.5 %collective-permute-start.14 = (bf16[2,64,896]{2,1,0:T(8,128)(2,1)S(1)}, bf16[2,64,896]{2,1,0:T(8,128)(2,1)S(1)}, u32[]{:S(2)}, u32[]{:S(2)}) collective-permute-start(bf16[2,64,896]{2,1,0:T(8,128)(2,1)S(1)} %pad_maximum_fusion.6.p0), channel_id=1, source_target_pairs={{0,16},{8,24},{16,0},{24,8},{32,48},{40,56},{48,32},{56,40},{64,80... | collective-permute-start | bytes 688136 | tf_op jit(solution)/shard_map/ppermute | solution.py:91
  83.4 8.7 %collective-permute-start.15 = (bf16[2,64,896]{2,1,0:T(8,128)(2,1)S(1)}, bf16[2,64,896]{2,1,0:T(8,128)(2,1)S(1)}, u32[]{:S(2)}, u32[]{:S(2)}) collective-permute-start(bf16[2,64,896]{2,1,0:T(8,128)(2,1)S(1)} %pad_maximum_fusion.6.p0), channel_id=1, source_target_pairs={{0,32},{8,40},{16,48},{24,56},{32,0},{40,8},{48,16},{56,24},{64,96... | collective-permute-start | bytes 688136 | tf_op jit(solution)/shard_map/ppermute | solution.py:91
  85.5 8.9 %collective-permute-start.16 = (bf16[2,64,896]{2,1,0:T(8,128)(2,1)S(1)}, bf16[2,64,896]{2,1,0:T(8,128)(2,1)S(1)}, u32[]{:S(2)}, u32[]{:S(2)}) collective-permute-start(bf16[2,64,896]{2,1,0:T(8,128)(2,1)S(1)} %pad_maximum_fusion.6.p0), channel_id=1, source_target_pairs={{0,48},{8,56},{16,32},{24,40},{32,16},{40,24},{48,0},{56,8},{64,11... | collective-permute-start | bytes 688136 | tf_op jit(solution)/shard_map/ppermute | solution.py:91
  100.6 17.0 %collective-permute-start.26 = (bf16[2,2,64,1536]{3,2,1,0:T(8,128)(2,1)S(1)}, bf16[2,2,64,1536]{3,2,1,0:T(8,128)(2,1)S(1)}, u32[]{:S(2)}, u32[]{:S(2)}) collective-permute-start(bf16[2,2,64,1536]{3,2,1,0:T(8,128)(2,1)S(1)} %get-tuple-element.28), channel_id=1, source_target_pairs={{0,3},{1,2},{2,1},{3,0},{4,7},{5,6},{6,5},{7,4},{8,11},{9,10},{10,... | collective-permute-start | bytes 2359304 | tf_op jit(solution)/shard_map/ppermute | solution.py:95
  100.7 18.1 %collective-permute-start.17 = (bf16[2,2,64,1536]{3,2,1,0:T(8,128)(2,1)S(1)}, bf16[2,2,64,1536]{3,2,1,0:T(8,128)(2,1)S(1)}, u32[]{:S(2)}, u32[]{:S(2)}) collective-permute-start(bf16[2,2,64,1536]{3,2,1,0:T(8,128)(2,1)S(1)} %get-tuple-element.24), channel_id=1, source_target_pairs={{0,1},{1,0},{2,3},{3,2},{4,5},{5,4},{6,7},{7,6},{8,9},{9,8},{10,11... | collective-permute-start | bytes 2359304 | tf_op jit(solution)/shard_map/ppermute | solution.py:95
  100.8 19.1 %collective-permute-start.20 = (bf16[2,2,64,1664]{3,2,1,0:T(8,128)(2,1)S(1)}, bf16[2,2,64,1664]{3,2,1,0:T(8,128)(2,1)S(1)}, u32[]{:S(2)}, u32[]{:S(2)}) collective-permute-start(bf16[2,2,64,1664]{3,2,1,0:T(8,128)(2,1)S(1)} %get-tuple-element.26), channel_id=1, source_target_pairs={{0,4},{1,5},{2,6},{3,7},{4,0},{5,1},{6,2},{7,3},{8,12},{9,13},{10,... | collective-permute-start | bytes 2555912 | tf_op jit(solution)/shard_map/ppermute | solution.py:95
  117.7 9.3 %collective-permute-start.27 = (bf16[2,64,1536]{2,1,0:T(8,128)(2,1)S(1)}, bf16[2,64,1536]{2,1,0:T(8,128)(2,1)S(1)}, u32[]{:S(2)}, u32[]{:S(2)}) collective-permute-start(bf16[2,64,1536]{2,1,0:T(8,128)(2,1)S(1)} %fusion.4), channel_id=1, source_target_pairs={{0,4},{1,5},{2,6},{3,7},{4,0},{5,1},{6,2},{7,3},{8,12},{9,13},{10,... | collective-permute-start | bytes 1179656 | tf_op jit(solution)/shard_map/ppermute | solution.py:95
  118.9 10.4 %collective-permute-start.18 = (bf16[2,64,1536]{2,1,0:T(8,128)(2,1)S(1)}, bf16[2,64,1536]{2,1,0:T(8,128)(2,1)S(1)}, u32[]{:S(2)}, u32[]{:S(2)}) collective-permute-start(bf16[2,64,1536]{2,1,0:T(8,128)(2,1)S(1)} %fusion.3), channel_id=1, source_target_pairs={{0,3},{1,2},{2,1},{3,0},{4,7},{5,6},{6,5},{7,4},{8,11},{9,10},{10,... | collective-permute-start | bytes 1179656 | tf_op jit(solution)/shard_map/ppermute | solution.py:95
  120.0 10.4 %collective-permute-start.21 = (bf16[2,64,1664]{2,1,0:T(8,128)(2,1)S(1)}, bf16[2,64,1664]{2,1,0:T(8,128)(2,1)S(1)}, u32[]{:S(2)}, u32[]{:S(2)}) collective-permute-start(bf16[2,64,1664]{2,1,0:T(8,128)(2,1)S(1)} %fusion), channel_id=1, source_target_pairs={{0,1},{1,0},{2,3},{3,2},{4,5},{5,4},{6,7},{7,6},{8,9},{9,8},{10,11... | collective-permute-start | bytes 1277960 | tf_op jit(solution)/shard_map/ppermute | solution.py:95
  127.1 6.4 %collective-permute-start.28 = (bf16[64,1536]{1,0:T(8,128)(2,1)S(1)}, bf16[64,1536]{1,0:T(8,128)(2,1)S(1)}, u32[]{:S(2)}, u32[]{:S(2)}) collective-permute-start(bf16[64,1536]{1,0:T(8,128)(2,1)S(1)} %fusion.5), channel_id=1, source_target_pairs={{0,1},{1,0},{2,3},{3,2},{4,5},{5,4},{6,7},{7,6},{8,9},{9,8},{10,11... | collective-permute-start | bytes 589832 | tf_op jit(solution)/shard_map/ppermute | solution.py:95
  129.4 6.0 %collective-permute-start.19 = (bf16[64,1536]{1,0:T(8,128)(2,1)S(1)}, bf16[64,1536]{1,0:T(8,128)(2,1)S(1)}, u32[]{:S(2)}, u32[]{:S(2)}) collective-permute-start(bf16[64,1536]{1,0:T(8,128)(2,1)S(1)} %fusion.7), channel_id=1, source_target_pairs={{0,4},{1,5},{2,6},{3,7},{4,0},{5,1},{6,2},{7,3},{8,12},{9,13},{10,... | collective-permute-start | bytes 589832 | tf_op jit(solution)/shard_map/ppermute | solution.py:95
  130.5 7.1 %collective-permute-start.22 = (bf16[64,1664]{1,0:T(8,128)(2,1)S(1)}, bf16[64,1664]{1,0:T(8,128)(2,1)S(1)}, u32[]{:S(2)}, u32[]{:S(2)}) collective-permute-start(bf16[64,1664]{1,0:T(8,128)(2,1)S(1)} %fusion.1), channel_id=1, source_target_pairs={{0,3},{1,2},{2,1},{3,0},{4,7},{5,6},{6,5},{7,4},{8,11},{9,10},{10,... | collective-permute-start | bytes 638984 | tf_op jit(solution)/shard_map/ppermute | solution.py:95
  138.2 6.9 %collective-permute-start.32 = (bf16[64,768]{1,0:T(8,128)(2,1)S(1)}, bf16[64,768]{1,0:T(8,128)(2,1)S(1)}, u32[]{:S(2)}, u32[]{:S(2)}) collective-permute-start(bf16[64,768]{1,0:T(8,128)(2,1)S(1)} %pad_maximum_fusion.15), channel_id=1, source_target_pairs={{0,3},{1,2},{2,1},{3,0},{4,7},{5,6},{6,5},{7,4},{8,11},{9,10},{10,... | collective-permute-start | bytes 294920 | tf_op jit(solution)/shard_map/ppermute | solution.py:95
  140.2 5.7 %collective-permute-start.29 = (bf16[64,768]{1,0:T(8,128)(2,1)S(1)}, bf16[64,768]{1,0:T(8,128)(2,1)S(1)}, u32[]{:S(2)}, u32[]{:S(2)}) collective-permute-start(bf16[64,768]{1,0:T(8,128)(2,1)S(1)} %pad_maximum_fusion.14), channel_id=1, source_target_pairs={{0,1},{1,0},{2,3},{3,2},{4,5},{5,4},{6,7},{7,6},{8,9},{9,8},{10,11... | collective-permute-start | bytes 294920 | tf_op jit(solution)/shard_map/ppermute | solution.py:95
  140.3 6.8 %collective-permute-start.23 = (bf16[64,768]{1,0:T(8,128)(2,1)S(1)}, bf16[64,768]{1,0:T(8,128)(2,1)S(1)}, u32[]{:S(2)}, u32[]{:S(2)}) collective-permute-start(bf16[64,768]{1,0:T(8,128)(2,1)S(1)} %pad_maximum_fusion.13), channel_id=1, source_target_pairs={{0,4},{1,5},{2,6},{3,7},{4,0},{5,1},{6,2},{7,3},{8,12},{9,13},{10,... | collective-permute-start | bytes 294920 | tf_op jit(solution)/shard_map/ppermute | solution.py:95
  145.1 9.7 %copy-start.3 = (bf16[1152,896]{1,0:T(8,128)(2,1)S(1)}, bf16[1152,896]{1,0:T(8,128)(2,1)}, u32[]{:S(2)}) copy-start(bf16[1152,896]{1,0:T(8,128)(2,1)} %param.19) | copy-start | bytes 6193156
  145.1 5.9 %collective-permute-start.33 = (bf16[2,64,768]{2,1,0:T(8,128)(2,1)S(1)}, bf16[2,64,768]{2,1,0:T(8,128)(2,1)S(1)}, u32[]{:S(2)}, u32[]{:S(2)}) collective-permute-start(bf16[2,64,768]{2,1,0:T(8,128)(2,1)S(1)} %get-tuple-element.52), channel_id=1, source_target_pairs={{0,1},{1,0},{2,3},{3,2},{4,5},{5,4},{6,7},{7,6},{8,9},{9,8},{10,11... | collective-permute-start | bytes 589832 | tf_op jit(solution)/shard_map/ppermute | solution.py:95
  145.9 6.2 %collective-permute-start.30 = (bf16[2,64,768]{2,1,0:T(8,128)(2,1)S(1)}, bf16[2,64,768]{2,1,0:T(8,128)(2,1)S(1)}, u32[]{:S(2)}, u32[]{:S(2)}) collective-permute-start(bf16[2,64,768]{2,1,0:T(8,128)(2,1)S(1)} %get-tuple-element.54), channel_id=1, source_target_pairs={{0,4},{1,5},{2,6},{3,7},{4,0},{5,1},{6,2},{7,3},{8,12},{9,13},{10,... | collective-permute-start | bytes 589832 | tf_op jit(solution)/shard_map/ppermute | solution.py:95
  147.1 7.0 %collective-permute-start.24 = (bf16[2,64,768]{2,1,0:T(8,128)(2,1)S(1)}, bf16[2,64,768]{2,1,0:T(8,128)(2,1)S(1)}, u32[]{:S(2)}, u32[]{:S(2)}) collective-permute-start(bf16[2,64,768]{2,1,0:T(8,128)(2,1)S(1)} %get-tuple-element.56), channel_id=1, source_target_pairs={{0,3},{1,2},{2,1},{3,0},{4,7},{5,6},{6,5},{7,4},{8,11},{9,10},{10,... | collective-permute-start | bytes 589832 | tf_op jit(solution)/shard_map/ppermute | solution.py:95
  151.0 11.5 %collective-permute-start.34 = (bf16[2,2,64,768]{3,2,1,0:T(8,128)(2,1)S(1)}, bf16[2,2,64,768]{3,2,1,0:T(8,128)(2,1)S(1)}, u32[]{:S(2)}, u32[]{:S(2)}) collective-permute-start(bf16[2,2,64,768]{3,2,1,0:T(8,128)(2,1)S(1)} %pad_maximum_fusion.3.s2), channel_id=1, source_target_pairs={{0,4},{1,5},{2,6},{3,7},{4,0},{5,1},{6,2},{7,3},{8,12},{9,13},{10,... | collective-permute-start | bytes 1179656 | tf_op jit(solution)/shard_map/ppermute | solution.py:95
  152.2 10.4 %collective-permute-start.31 = (bf16[2,2,64,768]{3,2,1,0:T(8,128)(2,1)S(1)}, bf16[2,2,64,768]{3,2,1,0:T(8,128)(2,1)S(1)}, u32[]{:S(2)}, u32[]{:S(2)}) collective-permute-start(bf16[2,2,64,768]{3,2,1,0:T(8,128)(2,1)S(1)} %pad_maximum_fusion.2.s1), channel_id=1, source_target_pairs={{0,3},{1,2},{2,1},{3,0},{4,7},{5,6},{6,5},{7,4},{8,11},{9,10},{10,... | collective-permute-start | bytes 1179656 | tf_op jit(solution)/shard_map/ppermute | solution.py:95
  154.1 8.5 %collective-permute-start.25 = (bf16[2,2,64,768]{3,2,1,0:T(8,128)(2,1)S(1)}, bf16[2,2,64,768]{3,2,1,0:T(8,128)(2,1)S(1)}, u32[]{:S(2)}, u32[]{:S(2)}) collective-permute-start(bf16[2,2,64,768]{3,2,1,0:T(8,128)(2,1)S(1)} %pad_maximum_fusion.1.s0), channel_id=1, source_target_pairs={{0,1},{1,0},{2,3},{3,2},{4,5},{5,4},{6,7},{7,6},{8,9},{9,8},{10,11... | collective-permute-start | bytes 1179656 | tf_op jit(solution)/shard_map/ppermute | solution.py:95
  162.6 19.4 %copy-start.1 = (bf16[2,512,896]{2,1,0:T(8,128)(2,1)S(1)}, bf16[2,512,896]{2,1,0:T(8,128)(2,1)}, u32[]{:S(2)}) copy-start(bf16[2,512,896]{2,1,0:T(8,128)(2,1)} %param.14) | copy-start | bytes 5505028

commit v5 on v4

--- a/solution.py
+++ b/solution.py
@@ -22,7 +22,7 @@
 NP = len(ORDER)
 
 
-def attend_kernel(len_ref, q_ref, k_hbm, v_hbm, o_ref, k_ref, v_ref, k_sem, v_sem):
+def attend_kernel(len_ref, q_ref, k_hbm, v_hbm, o_ref, k_ref, v_ref, rows_ref, k_sem, v_sem):
     nm, r, h, hd = q_ref.shape
     l = k_ref.shape[1]
     for i in range(nm * r):
@@ -31,8 +31,7 @@
         pltpu.make_async_copy(v_hbm.at[m, t], v_ref.at[i], v_sem.at[i]).start()
     offsets = lax.broadcasted_iota(jnp.int32, (h, l), 1)
 
-    @pl.loop(0, nm * r // 2)
-    def _(step):
+    for step in range(nm * r // 2):
         outs = []
         for u in range(2):
             i = step * 2 + u
@@ -58,7 +57,13 @@
                 peak = jnp.max(jnp.abs(block), axis=1, keepdims=True)
                 scale = (peak + 1e-06).astype(BF).astype(F32)
                 levels = jnp.clip(jnp.floor(127.0 * block / scale + 0.5), -127.0, 127.0)
-                o_ref[step * 2 + u, :, cols] = (levels * scale / 127.0).astype(BF)
+                value = levels * scale / 127.0
+                for head in range(h):
+                    chip, at = divmod(head, h // NQ)
+                    lanes = slice(at * hd + b * QB, at * hd + (b + 1) * QB)
+                    rows_ref[chip, step * 2 + u : step * 2 + u + 1, lanes] = value[head : head + 1]
+
+    o_ref[...] = rows_ref[...].astype(BF)
 
 
 def attend(q, k, v, lengths):
@@ -66,7 +71,7 @@
     n, l = nm * r, k.shape[2]
     return pl.pallas_call(
         attend_kernel,
-        out_shape=jax.ShapeDtypeStruct((n, h, hd), BF),
+        out_shape=jax.ShapeDtypeStruct((NQ, n, h * hd // NQ), BF),
         in_specs=[
             pl.BlockSpec(memory_space=pltpu.SMEM),
             pl.BlockSpec(memory_space=pltpu.VMEM),
@@ -77,6 +82,7 @@
         scratch_shapes=[
             pltpu.VMEM((n, l, hd), BF),
             pltpu.VMEM((n, l, hd), BF),
+            pltpu.VMEM((NQ, n, h * hd // NQ), F32),
             pltpu.SemaphoreType.DMA((n,)),
             pltpu.SemaphoreType.DMA((n,)),
         ],
@@ -345,7 +351,7 @@
     gain = norm_gain.reshape(1, w)
 
     out = attend(queries, cache_keys, cache_values, lengths)
-    got = over_chips(out.reshape(n, NQ, -1).transpose(1, 0, 2)).reshape(NQ * n, -1)
+    got = over_chips(out).reshape(NQ * n, -1)
 
     got, out_sib, gate_sib, up_sib, down_sib = lax.optimization_barrier(
         (got, out_sib, gate_sib, up_sib, down_sib)

time: 183 us -> 181 us (0.989)
  local copies, waits for them, and re-layouts: 3.14 us -> 1.2 us
    reshape x2 -> x0, local copies, waits for them, and re-layouts: 1.94 us -> none  [local(): out.reshape(n, NQ, -1).transpose(1, 0, 2)]
  transfers between devices with their start and end apart: 37 -> 37, of which waited for: 22 -> 22; matrix products, arithmetic and copies ran while one was open for 6% -> 5% of each run, Pallas kernels for 5% -> 5%
where the time goes in v5:
time: 181 us; the launch traced here: 180 us
  waiting for transfers between devices  89.4 us (49%)
  starting transfers between devices  41.6 us (23%)
  Pallas kernels  23.3 us (13%)
  blocking collectives  15 us (8%)
  other arithmetic  9.31 us (5%)
    ppermute x27, waiting for transfers between devices, fx(): return lax.ppermute(x, 'ffn', [(i, i ^ k) for i in range(N_FFN)])  59.1 us
    ppermute x27, starting transfers between devices, fx(): return lax.ppermute(x, 'ffn', [(i, i ^ k) for i in range(N_FFN)])  23.7 us
    all_to_all x2, waiting for transfers between devices, over_chips(): return lax.all_to_all(x, 'attn', 0, 0, axis_index_groups=PLANES)  20.9 us
    all_to_all x1, blocking collectives, over_chips(): return lax.all_to_all(x, 'attn', 0, 0, axis_index_groups=PLANES)  15 us
    all_to_all x2, starting transfers between devices, over_chips(): return lax.all_to_all(x, 'attn', 0, 0, axis_index_groups=PLANES)  11.4 us
    pallas_call x1, Pallas kernels, attend(): pl.pallas_call(attend_kernel, out_shape=jax.ShapeDtypeStruct((NQ, n, h *...  9.61 us
    ppermute x8, waiting for transfers between devices, ax(): return lax.ppermute(x, 'attn', [(i, i ^ k) for i in range(N_ATTN)])  9.35 us
    select_n x3, other arithmetic, by_core(): return (jnp.where(a % 2 == 0, own, sib), jnp.where(a % 2 == 0, sib, own))  7.59 us
  transfers between devices with their start and end apart: 37, of which 22 were waited for; matrix products, arithmetic and copies ran while one was open for 5% of the time, Pallas kernels for 5%

profile of v5, /device:TPU:0, one launch (start us, length us, event | category | flops | bytes accessed | tf_op | source)
XLA Modules:
  0.0 180.1 jit_solution(6604260734343825862)
XLA Ops:
  1.0 9.6 %shard_map.100 = bf16[8,8,2048]{2,1,0:T(8,128)(2,1)} custom-call(s32[2,4]{1,0:T(2,128)} %len_ref.1, bf16[2,4,64,256]{3,2,1,0:T(8,128)(2,1)} %q_ref.1, bf16[2,4,1536,256]{3,2,1,0:T(8,128)(2,1)} %k_hbm.1, bf16[2,4,1536,256]{3,2,1,0:T(8,128)(2,1)} %v_hbm.1), custom_call_target="tpu_custom_call" | custom-call | flops 805306368 | bytes 12582912 | tf_op jit(solution)/shard_map/pallas_call | solution.py:72
  10.6 7.7 %all-to-all-start = ((bf16[8,8,2048]{2,1,0:T(8,128)(2,1)}), bf16[8,8,2048]{2,1,0:T(8,128)(2,1)S(1)}, u32[]{:S(2)}, u32[]{:S(2)}) async-start(bf16[8,8,2048]{2,1,0:T(8,128)(2,1)} %shard_map.100), calls=%async_computation | async-start | bytes 524288 | tf_op jit(solution)/shard_map/all_to_all | solution.py:105
  18.4 9.0 %all-to-all-done = bf16[8,8,2048]{2,1,0:T(8,128)(2,1)S(1)} async-done(((bf16[8,8,2048]{2,1,0:T(8,128)(2,1)}), bf16[8,8,2048]{2,1,0:T(8,128)(2,1)S(1)}, u32[]{:S(2)}, u32[]{:S(2)}) %all-to-all-start) | async-done | bytes 262176 | tf_op jit(solution)/shard_map/all_to_all | solution.py:105
  27.5 3.1 %collective-permute-start.10 = (bf16[64,640]{1,0:T(8,128)(2,1)S(1)}, bf16[64,640]{1,0:T(8,128)(2,1)S(1)}, u32[]{:S(2)}, u32[]{:S(2)}) collective-permute-start(bf16[64,640]{1,0:T(8,128)(2,1)S(1)} %get-tuple-element.47), channel_id=1, source_target_pairs={{0,3},{1,2},{2,1},{3,0},{4,7},{5,6},{6,5},{7,4},{8,11},{9,10},{10,... | collective-permute-start | bytes 245768 | tf_op jit(solution)/shard_map/ppermute | solution.py:101
  30.8 1.0 collective-permute-start.4
  31.8 1.4 collective-permute-done.10
  33.8 2.1 %collective-permute-done.7 = bf16[64,640]{1,0:T(8,128)(2,1)S(1)} collective-permute-done((bf16[64,640]{1,0:T(8,128)(2,1)S(1)}, bf16[64,640]{1,0:T(8,128)(2,1)S(1)}, u32[]{:S(2)}, u32[]{:S(2)}) %collective-permute-start.7) | collective-permute-done | bytes 81952 | tf_op jit(solution)/shard_map/ppermute | solution.py:101
  35.9 1.1 collective-permute-start.8
  37.6 1.0 collective-permute-done.11
  38.7 1.1 collective-permute-start.12
  39.8 3.3 %collective-permute-done.8 = bf16[2,64,640]{2,1,0:T(8,128)(2,1)S(1)} collective-permute-done((bf16[2,64,640]{2,1,0:T(8,128)(2,1)S(1)}, bf16[2,64,640]{2,1,0:T(8,128)(2,1)S(1)}, u32[]{:S(2)}, u32[]{:S(2)}) %collective-permute-start.8) | collective-permute-done | bytes 163872 | tf_op jit(solution)/shard_map/ppermute | solution.py:101
  43.2 2.9 %collective-permute-done.5 = bf16[2,64,768]{2,1,0:T(8,128)(2,1)S(1)} collective-permute-done((bf16[2,64,768]{2,1,0:T(8,128)(2,1)S(1)}, bf16[2,64,768]{2,1,0:T(8,128)(2,1)S(1)}, u32[]{:S(2)}, u32[]{:S(2)}) %collective-permute-start.5) | collective-permute-done | bytes 196640 | tf_op jit(solution)/shard_map/ppermute | solution.py:101
  46.2 1.9 %broadcast_select_fusion.6 = (bf16[1024,896]{1,0:T(8,128)(2,1)S(1)}, bf16[1024,896]{1,0:T(8,128)(2,1)S(1)}) fusion(bf16[1024,896]{1,0:T(8,128)(2,1)} %collective-permute-done, bf16[1024,896]{1,0:T(8,128)(2,1)S(1)} %copy-done.4, pred[]{:T(512)S(6)} %eq.20), kind=kLoop, calls=%fused_computation.6 | loop fusion | flops 1835008 | bytes 7340033 | tf_op jit(solution)/shard_map/jit(_where)/select_n | solution.py:303
  48.1 3.3 %collective-permute-done.9.r1 = bf16[2,2,64,640]{3,2,1,0:T(8,128)(2,1)S(1)} collective-permute-done((bf16[2,2,64,640]{3,2,1,0:T(8,128)(2,1)S(1)}, bf16[2,2,64,640]{3,2,1,0:T(8,128)(2,1)S(1)}, u32[]{:S(2)}, u32[]{:S(2)}) %collective-permute-start.9) | collective-permute-done | bytes 327712 | tf_op jit(solution)/shard_map/ppermute | solution.py:101
  51.5 2.5 %collective-permute-done.6.r0 = bf16[2,2,64,768]{3,2,1,0:T(8,128)(2,1)S(1)} collective-permute-done((bf16[2,2,64,768]{3,2,1,0:T(8,128)(2,1)S(1)}, bf16[2,2,64,768]{3,2,1,0:T(8,128)(2,1)S(1)}, u32[]{:S(2)}, u32[]{:S(2)}) %collective-permute-start.6) | collective-permute-done | bytes 393248 | tf_op jit(solution)/shard_map/ppermute | solution.py:101
  54.0 3.0 %shard_map.101 = bf16[8,64,896]{2,1,0:T(8,128)(2,1)S(1)} custom-call(s32[3]{0:T(128)S(1)} %pad_add_fusion.at_ref, bf16[2,2,64,768]{3,2,1,0:T(8,128)(2,1)S(1)} %pad_maximum_fusion.s0, bf16[2,2,64,768]{3,2,1,0:T(8,128)(2,1)S(1)} %collective-permute-done.6.r0, bf16[2,2,64,640]{3,2,1,0:T(8,128)(2,1)S(1)} %pad_maximum_fusion.4.s1, ...), custom_call_target="tpu_custom_call" | custom-call | flops 1879048192 | bytes 6291456 | tf_op jit(solution)/shard_map/pallas_call | solution.py:158
  58.0 3.7 %all-to-all-start.1 = ((bf16[8,64,896]{2,1,0:T(8,128)(2,1)}), bf16[8,64,896]{2,1,0:T(8,128)(2,1)S(1)}, u32[]{:S(2)}, u32[]{:S(2)}) async-start(bf16[8,64,896]{2,1,0:T(8,128)(2,1)} %copy-done.2), calls=%async_computation.1 | async-start | bytes 1835008 | tf_op jit(solution)/shard_map/all_to_all | solution.py:105
  61.9 12.0 %all-to-all-done.1.got_ref = bf16[8,64,896]{2,1,0:T(8,128)(2,1)S(1)} async-done(((bf16[8,64,896]{2,1,0:T(8,128)(2,1)}), bf16[8,64,896]{2,1,0:T(8,128)(2,1)S(1)}, u32[]{:S(2)}, u32[]{:S(2)}) %all-to-all-start.1) | async-done | bytes 917536 | tf_op jit(solution)/shard_map/all_to_all | solution.py:105
  74.7 5.8 %collective-permute-done.13 = bf16[64,896]{1,0:T(8,128)(2,1)S(1)} collective-permute-done((bf16[64,896]{1,0:T(8,128)(2,1)S(1)}, bf16[64,896]{1,0:T(8,128)(2,1)S(1)}, u32[]{:S(2)}, u32[]{:S(2)}) %collective-permute-start.13) | collective-permute-done | bytes 114720 | tf_op jit(solution)/shard_map/ppermute | solution.py:97
  80.5 1.0 collective-permute-start.14
  81.5 2.2 %collective-permute-start.15 = (bf16[2,64,896]{2,1,0:T(8,128)(2,1)S(1)}, bf16[2,64,896]{2,1,0:T(8,128)(2,1)S(1)}, u32[]{:S(2)}, u32[]{:S(2)}) collective-permute-start(bf16[2,64,896]{2,1,0:T(8,128)(2,1)S(1)} %pad_maximum_fusion.6.p0), channel_id=1, source_target_pairs={{0,32},{8,40},{16,48},{24,56},{32,0},{40,8},{48,16},{56,24},{64,96... | collective-permute-start | bytes 688136 | tf_op jit(solution)/shard_map/ppermute | solution.py:97
  83.7 1.6 collective-permute-start.16
  85.2 3.8 %broadcast_select_fusion.2 = (bf16[896,1152]{1,0:T(8,128)(2,1)S(1)}, bf16[896,1152]{1,0:T(8,128)(2,1)S(1)}, bf16[896,1152]{1,0:T(8,128)(2,1)S(1)}, bf16[896,1152]{1,0:T(8,128)(2,1)S(1)}) fusion(bf16[896,1152]{1,0:T(8,128)(2,1)} %collective-permute-done.2, bf16[896,1152]{1,0:T(8,128)(2,1)} %param.18, pred[]{:T(512)S(6)} %eq.20, bf16[896,1152]{1,0:T(8,128)(2,1)} %param.17, ...), kind=kLoop, calls=%fused_computation.2 | loop fusion | flops 4128768 | bytes 16515073 | tf_op jit(solution)/shard_map/jit(_where)/select_n | solution.py:303
  89.0 1.2 collective-permute-done.15.p2
  90.2 2.4 %collective-permute-done.16.p3 = bf16[2,64,896]{2,1,0:T(8,128)(2,1)S(1)} collective-permute-done((bf16[2,64,896]{2,1,0:T(8,128)(2,1)S(1)}, bf16[2,64,896]{2,1,0:T(8,128)(2,1)S(1)}, u32[]{:S(2)}, u32[]{:S(2)}) %collective-permute-start.16) | collective-permute-done | bytes 229408 | tf_op jit(solution)/shard_map/ppermute | solution.py:97
  92.6 6.2 %shard_map.103 = (bf16[2,2,64,1536]{3,2,1,0:T(8,128)(2,1)S(1)}, bf16[2,2,64,1536]{3,2,1,0:T(8,128)(2,1)S(1)}, bf16[2,2,64,1536]{3,2,1,0:T(8,128)(2,1)S(1)}, bf16...) custom-call(s32[3]{0:T(128)S(1)} %pad_add_fusion.at_ref, ...), custom_call_target="tpu_custom_call" | custom-call | flops 4227858432 | bytes 14680064 | tf_op jit(solution)/shard_map/pallas_call | solution.py:232
  98.9 1.1 collective-permute-start.20
  100.0 15.8 %collective-permute-done.26 = bf16[2,2,64,1536]{3,2,1,0:T(8,128)(2,1)S(1)} collective-permute-done((bf16[2,2,64,1536]{3,2,1,0:T(8,128)(2,1)S(1)}, bf16[2,2,64,1536]{3,2,1,0:T(8,128)(2,1)S(1)}, u32[]{:S(2)}, u32[]{:S(2)}) %collective-permute-start.26) | collective-permute-done | bytes 786464 | tf_op jit(solution)/shard_map/ppermute | solution.py:101
  115.9 1.1 collective-permute-start.27
  118.3 6.8 %collective-permute-done.27 = bf16[2,64,1536]{2,1,0:T(8,128)(2,1)S(1)} collective-permute-done((bf16[2,64,1536]{2,1,0:T(8,128)(2,1)S(1)}, bf16[2,64,1536]{2,1,0:T(8,128)(2,1)S(1)}, u32[]{:S(2)}, u32[]{:S(2)}) %collective-permute-start.27) | collective-permute-done | bytes 393248 | tf_op jit(solution)/shard_map/ppermute | solution.py:101
  125.3 2.1 %collective-permute-done.18 = bf16[2,64,1536]{2,1,0:T(8,128)(2,1)S(1)} collective-permute-done((bf16[2,64,1536]{2,1,0:T(8,128)(2,1)S(1)}, bf16[2,64,1536]{2,1,0:T(8,128)(2,1)S(1)}, u32[]{:S(2)}, u32[]{:S(2)}) %collective-permute-start.18) | collective-permute-done | bytes 393248 | tf_op jit(solution)/shard_map/ppermute | solution.py:101
  127.5 1.1 collective-permute-start.19
  128.7 1.9 %collective-permute-start.22 = (bf16[64,1664]{1,0:T(8,128)(2,1)S(1)}, bf16[64,1664]{1,0:T(8,128)(2,1)S(1)}, u32[]{:S(2)}, u32[]{:S(2)}) collective-permute-start(bf16[64,1664]{1,0:T(8,128)(2,1)S(1)} %fusion.1), channel_id=1, source_target_pairs={{0,3},{1,2},{2,1},{3,0},{4,7},{5,6},{6,5},{7,4},{8,11},{9,10},{10,... | collective-permute-start | bytes 638984 | tf_op jit(solution)/shard_map/ppermute | solution.py:101
  130.5 1.1 collective-permute-done.28
  131.7 1.8 %collective-permute-done.19 = bf16[64,1536]{1,0:T(8,128)(2,1)S(1)} collective-permute-done((bf16[64,1536]{1,0:T(8,128)(2,1)S(1)}, bf16[64,1536]{1,0:T(8,128)(2,1)S(1)}, u32[]{:S(2)}, u32[]{:S(2)}) %collective-permute-start.19) | collective-permute-done | bytes 196640 | tf_op jit(solution)/shard_map/ppermute | solution.py:101
  133.6 2.2 %collective-permute-done.22 = bf16[64,1664]{1,0:T(8,128)(2,1)S(1)} collective-permute-done((bf16[64,1664]{1,0:T(8,128)(2,1)S(1)}, bf16[64,1664]{1,0:T(8,128)(2,1)S(1)}, u32[]{:S(2)}, u32[]{:S(2)}) %collective-permute-start.22) | collective-permute-done | bytes 213024 | tf_op jit(solution)/shard_map/ppermute | solution.py:101
  136.3 2.0 %collective-permute-start.32 = (bf16[64,768]{1,0:T(8,128)(2,1)S(1)}, bf16[64,768]{1,0:T(8,128)(2,1)S(1)}, u32[]{:S(2)}, u32[]{:S(2)}) collective-permute-start(bf16[64,768]{1,0:T(8,128)(2,1)S(1)} %pad_maximum_fusion.15), channel_id=1, source_target_pairs={{0,3},{1,2},{2,1},{3,0},{4,7},{5,6},{6,5},{7,4},{8,11},{9,10},{10,... | collective-permute-start | bytes 294920 | tf_op jit(solution)/shard_map/ppermute | solution.py:101
  138.4 1.1 collective-permute-start.23
  139.5 3.7 %collective-permute-done.32 = bf16[64,768]{1,0:T(8,128)(2,1)S(1)} collective-permute-done((bf16[64,768]{1,0:T(8,128)(2,1)S(1)}, bf16[64,768]{1,0:T(8,128)(2,1)S(1)}, u32[]{:S(2)}, u32[]{:S(2)}) %collective-permute-start.32) | collective-permute-done | bytes 98336 | tf_op jit(solution)/shard_map/ppermute | solution.py:101
  144.1 1.1 collective-permute-start.30
  145.2 1.4 collective-permute-start.24
  146.6 2.5 %collective-permute-done.33 = bf16[2,64,768]{2,1,0:T(8,128)(2,1)S(1)} collective-permute-done((bf16[2,64,768]{2,1,0:T(8,128)(2,1)S(1)}, bf16[2,64,768]{2,1,0:T(8,128)(2,1)S(1)}, u32[]{:S(2)}, u32[]{:S(2)}) %collective-permute-start.33) | collective-permute-done | bytes 196640 | tf_op jit(solution)/shard_map/ppermute | solution.py:101
  149.2 1.1 collective-permute-start.34
  150.3 1.9 %collective-permute-start.31 = (bf16[2,2,64,768]{3,2,1,0:T(8,128)(2,1)S(1)}, bf16[2,2,64,768]{3,2,1,0:T(8,128)(2,1)S(1)}, u32[]{:S(2)}, u32[]{:S(2)}) collective-permute-start(bf16[2,2,64,768]{3,2,1,0:T(8,128)(2,1)S(1)} %pad_maximum_fusion.2.s1), channel_id=1, source_target_pairs={{0,3},{1,2},{2,1},{3,0},{4,7},{5,6},{6,5},{7,4},{8,11},{9,10},{10,... | collective-permute-start | bytes 1179656 | tf_op jit(solution)/shard_map/ppermute | solution.py:101
  152.9 2.0 %broadcast_select_fusion = (bf16[1152,896]{1,0:T(8,128)(2,1)S(1)}, bf16[1152,896]{1,0:T(8,128)(2,1)S(1)}) fusion(bf16[1152,896]{1,0:T(8,128)(2,1)} %collective-permute-done.3, bf16[1152,896]{1,0:T(8,128)(2,1)S(1)} %copy-done.3, pred[]{:T(512)S(6)} %eq.20), kind=kLoop, calls=%fused_computation | loop fusion | flops 2064384 | bytes 8257537 | tf_op jit(solution)/shard_map/jit(_where)/select_n | solution.py:303
  154.9 5.8 %collective-permute-done.34.r2 = bf16[2,2,64,768]{3,2,1,0:T(8,128)(2,1)S(1)} collective-permute-done((bf16[2,2,64,768]{3,2,1,0:T(8,128)(2,1)S(1)}, bf16[2,2,64,768]{3,2,1,0:T(8,128)(2,1)S(1)}, u32[]{:S(2)}, u32[]{:S(2)}) %collective-permute-start.34) | collective-permute-done | bytes 393248 | tf_op jit(solution)/shard_map/ppermute | solution.py:101
  160.7 3.5 %shard_map.104 = bf16[512,896]{1,0:T(8,128)(2,1)S(1)} custom-call(s32[3]{0:T(128)S(1)} %pad_add_fusion.at_ref, bf16[2,2,64,768]{3,2,1,0:T(8,128)(2,1)S(1)} %pad_maximum_fusion.1.s0, bf16[2,2,64,768]{3,2,1,0:T(8,128)(2,1)S(1)} %collective-permute-done.25.r0, bf16[2,2,64,768]{3,2,1,0:T(8,128)(2,1)S(1)} %pad_maximum_fusion.2.s1, ...), custom_call_target="tpu_custom_call" | custom-call | flops 2113929216 | bytes 6291456 | tf_op jit(solution)/shard_map/pallas_call | solution.py:267
  164.3 15.0 %all_to_all.15.got_ref = bf16[8,64,896]{2,1,0:T(8,128)(2,1)S(1)} all-to-all(bf16[8,64,896]{2,1,0:T(8,128)(2,1)S(1)} %bitcast.94), channel_id=1, replica_groups={{0,16,32,48,64,80,96,112},{8,24,40,56,72,88,104,120},{1,17,33,49,65,81,..., dimensions={0} | all-to-all | bytes 1835008 | tf_op jit(solution)/shard_map/all_to_all | solution.py:105
  (83 shorter events, 10.1 us)
Async XLA Ops:
  0.0 61.7 %copy-start = (bf16[2,512,896]{2,1,0:T(8,128)(2,1)S(1)}, bf16[2,512,896]{2,1,0:T(8,128)(2,1)}, u32[]{:S(2)}) copy-start(bf16[2,512,896]{2,1,0:T(8,128)(2,1)} %param.14) | copy-start | bytes 5505028
  0.0 27.4 %collective-permute-start.1 = (bf16[896,1152]{1,0:T(8,128)(2,1)}, bf16[896,1152]{1,0:T(8,128)(2,1)}, u32[]{:S(2)}, u32[]{:S(2)}) collective-permute-start(bf16[896,1152]{1,0:T(8,128)(2,1)} %param.17), channel_id=1, source_target_pairs={{0,8},{8,0},{16,24},{24,16},{32,40},{40,32},{48,56},{56,48},{64,72... | collective-permute-start | bytes 6193160 | tf_op jit(solution)/shard_map/ppermute | solution.py:97
  0.0 27.4 %collective-permute-start.2 = (bf16[896,1152]{1,0:T(8,128)(2,1)}, bf16[896,1152]{1,0:T(8,128)(2,1)}, u32[]{:S(2)}, u32[]{:S(2)}) collective-permute-start(bf16[896,1152]{1,0:T(8,128)(2,1)} %param.18), channel_id=1, source_target_pairs={{0,8},{8,0},{16,24},{24,16},{32,40},{40,32},{48,56},{56,48},{64,72... | collective-permute-start | bytes 6193160 | tf_op jit(solution)/shard_map/ppermute | solution.py:97
  0.5 26.9 %collective-permute-start.3 = (bf16[1152,896]{1,0:T(8,128)(2,1)}, bf16[1152,896]{1,0:T(8,128)(2,1)}, u32[]{:S(2)}, u32[]{:S(2)}) collective-permute-start(bf16[1152,896]{1,0:T(8,128)(2,1)} %param.19), channel_id=1, source_target_pairs={{0,8},{8,0},{16,24},{24,16},{32,40},{40,32},{48,56},{56,48},{64,72... | collective-permute-start | bytes 6193160 | tf_op jit(solution)/shard_map/ppermute | solution.py:97
  0.5 26.9 %collective-permute-start = (bf16[1024,896]{1,0:T(8,128)(2,1)}, bf16[1024,896]{1,0:T(8,128)(2,1)}, u32[]{:S(2)}, u32[]{:S(2)}) collective-permute-start(bf16[1024,896]{1,0:T(8,128)(2,1)} %param.16), channel_id=1, source_target_pairs={{0,8},{8,0},{16,24},{24,16},{32,40},{40,32},{48,56},{56,48},{64,72... | collective-permute-start | bytes 5505032 | tf_op jit(solution)/shard_map/ppermute | solution.py:97
  10.6 16.7 %all-to-all-start = ((bf16[8,8,2048]{2,1,0:T(8,128)(2,1)}), bf16[8,8,2048]{2,1,0:T(8,128)(2,1)S(1)}, u32[]{:S(2)}, u32[]{:S(2)}) async-start(bf16[8,8,2048]{2,1,0:T(8,128)(2,1)} %shard_map.100), calls=%async_computation | async-start | bytes 524288 | tf_op jit(solution)/shard_map/all_to_all | solution.py:105
  27.4 18.8 %copy-start.4 = (bf16[1024,896]{1,0:T(8,128)(2,1)S(1)}, bf16[1024,896]{1,0:T(8,128)(2,1)}, u32[]{:S(2)}) copy-start(bf16[1024,896]{1,0:T(8,128)(2,1)} %param.16) | copy-start | bytes 5505028
  27.5 5.7 %collective-permute-start.10 = (bf16[64,640]{1,0:T(8,128)(2,1)S(1)}, bf16[64,640]{1,0:T(8,128)(2,1)S(1)}, u32[]{:S(2)}, u32[]{:S(2)}) collective-permute-start(bf16[64,640]{1,0:T(8,128)(2,1)S(1)} %get-tuple-element.47), channel_id=1, source_target_pairs={{0,3},{1,2},{2,1},{3,0},{4,7},{5,6},{6,5},{7,4},{8,11},{9,10},{10,... | collective-permute-start | bytes 245768 | tf_op jit(solution)/shard_map/ppermute | solution.py:101
  30.6 5.3 %collective-permute-start.7 = (bf16[64,640]{1,0:T(8,128)(2,1)S(1)}, bf16[64,640]{1,0:T(8,128)(2,1)S(1)}, u32[]{:S(2)}, u32[]{:S(2)}) collective-permute-start(bf16[64,640]{1,0:T(8,128)(2,1)S(1)} %get-tuple-element.48), channel_id=1, source_target_pairs={{0,1},{1,0},{2,3},{3,2},{4,5},{5,4},{6,7},{7,6},{8,9},{9,8},{10,11... | collective-permute-start | bytes 245768 | tf_op jit(solution)/shard_map/ppermute | solution.py:101
  30.8 6.3 %collective-permute-start.4 = (bf16[64,768]{1,0:T(8,128)(2,1)S(1)}, bf16[64,768]{1,0:T(8,128)(2,1)S(1)}, u32[]{:S(2)}, u32[]{:S(2)}) collective-permute-start(bf16[64,768]{1,0:T(8,128)(2,1)S(1)} %get-tuple-element.50), channel_id=1, source_target_pairs={{0,4},{1,5},{2,6},{3,7},{4,0},{5,1},{6,2},{7,3},{8,12},{9,13},{10,... | collective-permute-start | bytes 294920 | tf_op jit(solution)/shard_map/ppermute | solution.py:101
  33.2 5.4 %collective-permute-start.11 = (bf16[2,64,640]{2,1,0:T(8,128)(2,1)S(1)}, bf16[2,64,640]{2,1,0:T(8,128)(2,1)S(1)}, u32[]{:S(2)}, u32[]{:S(2)}) collective-permute-start(bf16[2,64,640]{2,1,0:T(8,128)(2,1)S(1)} %get-tuple-element.60), channel_id=1, source_target_pairs={{0,1},{1,0},{2,3},{3,2},{4,5},{5,4},{6,7},{7,6},{8,9},{9,8},{10,11... | collective-permute-start | bytes 491528 | tf_op jit(solution)/shard_map/ppermute | solution.py:101
  35.9 7.1 %collective-permute-start.8 = (bf16[2,64,640]{2,1,0:T(8,128)(2,1)S(1)}, bf16[2,64,640]{2,1,0:T(8,128)(2,1)S(1)}, u32[]{:S(2)}, u32[]{:S(2)}) collective-permute-start(bf16[2,64,640]{2,1,0:T(8,128)(2,1)S(1)} %get-tuple-element.62), channel_id=1, source_target_pairs={{0,4},{1,5},{2,6},{3,7},{4,0},{5,1},{6,2},{7,3},{8,12},{9,13},{10,... | collective-permute-start | bytes 491528 | tf_op jit(solution)/shard_map/ppermute | solution.py:101
  37.1 9.0 %collective-permute-start.5 = (bf16[2,64,768]{2,1,0:T(8,128)(2,1)S(1)}, bf16[2,64,768]{2,1,0:T(8,128)(2,1)S(1)}, u32[]{:S(2)}, u32[]{:S(2)}) collective-permute-start(bf16[2,64,768]{2,1,0:T(8,128)(2,1)S(1)} %get-tuple-element.58), channel_id=1, source_target_pairs={{0,3},{1,2},{2,1},{3,0},{4,7},{5,6},{6,5},{7,4},{8,11},{9,10},{10,... | collective-permute-start | bytes 589832 | tf_op jit(solution)/shard_map/ppermute | solution.py:101
  38.7 9.5 %collective-permute-start.12 = (bf16[2,2,64,640]{3,2,1,0:T(8,128)(2,1)S(1)}, bf16[2,2,64,640]{3,2,1,0:T(8,128)(2,1)S(1)}, u32[]{:S(2)}, u32[]{:S(2)}) collective-permute-start(bf16[2,2,64,640]{3,2,1,0:T(8,128)(2,1)S(1)} %pad_maximum_fusion.5.s2), channel_id=1, source_target_pairs={{0,4},{1,5},{2,6},{3,7},{4,0},{5,1},{6,2},{7,3},{8,12},{9,13},{10,... | collective-permute-start | bytes 983048 | tf_op jit(solution)/shard_map/ppermute | solution.py:101
  43.1 8.4 %collective-permute-start.9 = (bf16[2,2,64,640]{3,2,1,0:T(8,128)(2,1)S(1)}, bf16[2,2,64,640]{3,2,1,0:T(8,128)(2,1)S(1)}, u32[]{:S(2)}, u32[]{:S(2)}) collective-permute-start(bf16[2,2,64,640]{3,2,1,0:T(8,128)(2,1)S(1)} %pad_maximum_fusion.4.s1), channel_id=1, source_target_pairs={{0,3},{1,2},{2,1},{3,0},{4,7},{5,6},{6,5},{7,4},{8,11},{9,10},{10,... | collective-permute-start | bytes 983048 | tf_op jit(solution)/shard_map/ppermute | solution.py:101
  46.1 7.9 %collective-permute-start.6 = (bf16[2,2,64,768]{3,2,1,0:T(8,128)(2,1)S(1)}, bf16[2,2,64,768]{3,2,1,0:T(8,128)(2,1)S(1)}, u32[]{:S(2)}, u32[]{:S(2)}) collective-permute-start(bf16[2,2,64,768]{3,2,1,0:T(8,128)(2,1)S(1)} %pad_maximum_fusion.s0), channel_id=1, source_target_pairs={{0,1},{1,0},{2,3},{3,2},{4,5},{5,4},{6,7},{7,6},{8,9},{9,8},{10,11... | collective-permute-start | bytes 1179656 | tf_op jit(solution)/shard_map/ppermute | solution.py:101
  57.0 1.0 copy-start.2
  58.0 3.9 %copy-start.5 = (bf16[896]{0:T(1024)(128)(2,1)S(1)}, bf16[896]{0:T(1024)(128)(2,1)}, u32[]{:S(2)}) copy-start(bf16[896]{0:T(1024)(128)(2,1)} %param.15) | copy-start | bytes 5380
  58.0 15.9 %all-to-all-start.1 = ((bf16[8,64,896]{2,1,0:T(8,128)(2,1)}), bf16[8,64,896]{2,1,0:T(8,128)(2,1)S(1)}, u32[]{:S(2)}, u32[]{:S(2)}) async-start(bf16[8,64,896]{2,1,0:T(8,128)(2,1)} %copy-done.2), calls=%async_computation.1 | async-start | bytes 1835008 | tf_op jit(solution)/shard_map/all_to_all | solution.py:105
  74.1 6.4 %collective-permute-start.13 = (bf16[64,896]{1,0:T(8,128)(2,1)S(1)}, bf16[64,896]{1,0:T(8,128)(2,1)S(1)}, u32[]{:S(2)}, u32[]{:S(2)}) collective-permute-start(bf16[64,896]{1,0:T(8,128)(2,1)S(1)} %get-tuple-element.20), channel_id=1, source_target_pairs={{0,64},{8,72},{16,80},{24,88},{32,96},{40,104},{48,112},{56,120},{... | collective-permute-start | bytes 344072 | tf_op jit(solution)/shard_map/ppermute | solution.py:97
  80.5 8.5 %collective-permute-start.14 = (bf16[2,64,896]{2,1,0:T(8,128)(2,1)S(1)}, bf16[2,64,896]{2,1,0:T(8,128)(2,1)S(1)}, u32[]{:S(2)}, u32[]{:S(2)}) collective-permute-start(bf16[2,64,896]{2,1,0:T(8,128)(2,1)S(1)} %pad_maximum_fusion.6.p0), channel_id=1, source_target_pairs={{0,16},{8,24},{16,0},{24,8},{32,48},{40,56},{48,32},{56,40},{64,80... | collective-permute-start | bytes 688136 | tf_op jit(solution)/shard_map/ppermute | solution.py:97
  81.5 8.7 %collective-permute-start.15 = (bf16[2,64,896]{2,1,0:T(8,128)(2,1)S(1)}, bf16[2,64,896]{2,1,0:T(8,128)(2,1)S(1)}, u32[]{:S(2)}, u32[]{:S(2)}) collective-permute-start(bf16[2,64,896]{2,1,0:T(8,128)(2,1)S(1)} %pad_maximum_fusion.6.p0), channel_id=1, source_target_pairs={{0,32},{8,40},{16,48},{24,56},{32,0},{40,8},{48,16},{56,24},{64,96... | collective-permute-start | bytes 688136 | tf_op jit(solution)/shard_map/ppermute | solution.py:97
  83.7 8.9 %collective-permute-start.16 = (bf16[2,64,896]{2,1,0:T(8,128)(2,1)S(1)}, bf16[2,64,896]{2,1,0:T(8,128)(2,1)S(1)}, u32[]{:S(2)}, u32[]{:S(2)}) collective-permute-start(bf16[2,64,896]{2,1,0:T(8,128)(2,1)S(1)} %pad_maximum_fusion.6.p0), channel_id=1, source_target_pairs={{0,48},{8,56},{16,32},{24,40},{32,16},{40,24},{48,0},{56,8},{64,11... | collective-permute-start | bytes 688136 | tf_op jit(solution)/shard_map/ppermute | solution.py:97
  98.7 17.0 %collective-permute-start.26 = (bf16[2,2,64,1536]{3,2,1,0:T(8,128)(2,1)S(1)}, bf16[2,2,64,1536]{3,2,1,0:T(8,128)(2,1)S(1)}, u32[]{:S(2)}, u32[]{:S(2)}) collective-permute-start(bf16[2,2,64,1536]{3,2,1,0:T(8,128)(2,1)S(1)} %get-tuple-element.28), channel_id=1, source_target_pairs={{0,3},{1,2},{2,1},{3,0},{4,7},{5,6},{6,5},{7,4},{8,11},{9,10},{10,... | collective-permute-start | bytes 2359304 | tf_op jit(solution)/shard_map/ppermute | solution.py:101
  98.8 18.1 %collective-permute-start.17 = (bf16[2,2,64,1536]{3,2,1,0:T(8,128)(2,1)S(1)}, bf16[2,2,64,1536]{3,2,1,0:T(8,128)(2,1)S(1)}, u32[]{:S(2)}, u32[]{:S(2)}) collective-permute-start(bf16[2,2,64,1536]{3,2,1,0:T(8,128)(2,1)S(1)} %get-tuple-element.24), channel_id=1, source_target_pairs={{0,1},{1,0},{2,3},{3,2},{4,5},{5,4},{6,7},{7,6},{8,9},{9,8},{10,11... | collective-permute-start | bytes 2359304 | tf_op jit(solution)/shard_map/ppermute | solution.py:101
  98.9 19.1 %collective-permute-start.20 = (bf16[2,2,64,1664]{3,2,1,0:T(8,128)(2,1)S(1)}, bf16[2,2,64,1664]{3,2,1,0:T(8,128)(2,1)S(1)}, u32[]{:S(2)}, u32[]{:S(2)}) collective-permute-start(bf16[2,2,64,1664]{3,2,1,0:T(8,128)(2,1)S(1)} %get-tuple-element.26), channel_id=1, source_target_pairs={{0,4},{1,5},{2,6},{3,7},{4,0},{5,1},{6,2},{7,3},{8,12},{9,13},{10,... | collective-permute-start | bytes 2555912 | tf_op jit(solution)/shard_map/ppermute | solution.py:101
  115.9 9.3 %collective-permute-start.27 = (bf16[2,64,1536]{2,1,0:T(8,128)(2,1)S(1)}, bf16[2,64,1536]{2,1,0:T(8,128)(2,1)S(1)}, u32[]{:S(2)}, u32[]{:S(2)}) collective-permute-start(bf16[2,64,1536]{2,1,0:T(8,128)(2,1)S(1)} %fusion.4), channel_id=1, source_target_pairs={{0,4},{1,5},{2,6},{3,7},{4,0},{5,1},{6,2},{7,3},{8,12},{9,13},{10,... | collective-permute-start | bytes 1179656 | tf_op jit(solution)/shard_map/ppermute | solution.py:101
  117.0 10.4 %collective-permute-start.18 = (bf16[2,64,1536]{2,1,0:T(8,128)(2,1)S(1)}, bf16[2,64,1536]{2,1,0:T(8,128)(2,1)S(1)}, u32[]{:S(2)}, u32[]{:S(2)}) collective-permute-start(bf16[2,64,1536]{2,1,0:T(8,128)(2,1)S(1)} %fusion.3), channel_id=1, source_target_pairs={{0,3},{1,2},{2,1},{3,0},{4,7},{5,6},{6,5},{7,4},{8,11},{9,10},{10,... | collective-permute-start | bytes 1179656 | tf_op jit(solution)/shard_map/ppermute | solution.py:101
  118.2 10.4 %collective-permute-start.21 = (bf16[2,64,1664]{2,1,0:T(8,128)(2,1)S(1)}, bf16[2,64,1664]{2,1,0:T(8,128)(2,1)S(1)}, u32[]{:S(2)}, u32[]{:S(2)}) collective-permute-start(bf16[2,64,1664]{2,1,0:T(8,128)(2,1)S(1)} %fusion), channel_id=1, source_target_pairs={{0,1},{1,0},{2,3},{3,2},{4,5},{5,4},{6,7},{7,6},{8,9},{9,8},{10,11... | collective-permute-start | bytes 1277960 | tf_op jit(solution)/shard_map/ppermute | solution.py:101
  125.2 6.4 %collective-permute-start.28 = (bf16[64,1536]{1,0:T(8,128)(2,1)S(1)}, bf16[64,1536]{1,0:T(8,128)(2,1)S(1)}, u32[]{:S(2)}, u32[]{:S(2)}) collective-permute-start(bf16[64,1536]{1,0:T(8,128)(2,1)S(1)} %fusion.5), channel_id=1, source_target_pairs={{0,1},{1,0},{2,3},{3,2},{4,5},{5,4},{6,7},{7,6},{8,9},{9,8},{10,11... | collective-permute-start | bytes 589832 | tf_op jit(solution)/shard_map/ppermute | solution.py:101
  127.5 6.0 %collective-permute-start.19 = (bf16[64,1536]{1,0:T(8,128)(2,1)S(1)}, bf16[64,1536]{1,0:T(8,128)(2,1)S(1)}, u32[]{:S(2)}, u32[]{:S(2)}) collective-permute-start(bf16[64,1536]{1,0:T(8,128)(2,1)S(1)} %fusion.7), channel_id=1, source_target_pairs={{0,4},{1,5},{2,6},{3,7},{4,0},{5,1},{6,2},{7,3},{8,12},{9,13},{10,... | collective-permute-start | bytes 589832 | tf_op jit(solution)/shard_map/ppermute | solution.py:101
  128.7 7.1 %collective-permute-start.22 = (bf16[64,1664]{1,0:T(8,128)(2,1)S(1)}, bf16[64,1664]{1,0:T(8,128)(2,1)S(1)}, u32[]{:S(2)}, u32[]{:S(2)}) collective-permute-start(bf16[64,1664]{1,0:T(8,128)(2,1)S(1)} %fusion.1), channel_id=1, source_target_pairs={{0,3},{1,2},{2,1},{3,0},{4,7},{5,6},{6,5},{7,4},{8,11},{9,10},{10,... | collective-permute-start | bytes 638984 | tf_op jit(solution)/shard_map/ppermute | solution.py:101
  136.3 6.9 %collective-permute-start.32 = (bf16[64,768]{1,0:T(8,128)(2,1)S(1)}, bf16[64,768]{1,0:T(8,128)(2,1)S(1)}, u32[]{:S(2)}, u32[]{:S(2)}) collective-permute-start(bf16[64,768]{1,0:T(8,128)(2,1)S(1)} %pad_maximum_fusion.15), channel_id=1, source_target_pairs={{0,3},{1,2},{2,1},{3,0},{4,7},{5,6},{6,5},{7,4},{8,11},{9,10},{10,... | collective-permute-start | bytes 294920 | tf_op jit(solution)/shard_map/ppermute | solution.py:101
  138.3 5.7 %collective-permute-start.29 = (bf16[64,768]{1,0:T(8,128)(2,1)S(1)}, bf16[64,768]{1,0:T(8,128)(2,1)S(1)}, u32[]{:S(2)}, u32[]{:S(2)}) collective-permute-start(bf16[64,768]{1,0:T(8,128)(2,1)S(1)} %pad_maximum_fusion.14), channel_id=1, source_target_pairs={{0,1},{1,0},{2,3},{3,2},{4,5},{5,4},{6,7},{7,6},{8,9},{9,8},{10,11... | collective-permute-start | bytes 294920 | tf_op jit(solution)/shard_map/ppermute | solution.py:101
  138.4 6.8 %collective-permute-start.23 = (bf16[64,768]{1,0:T(8,128)(2,1)S(1)}, bf16[64,768]{1,0:T(8,128)(2,1)S(1)}, u32[]{:S(2)}, u32[]{:S(2)}) collective-permute-start(bf16[64,768]{1,0:T(8,128)(2,1)S(1)} %pad_maximum_fusion.13), channel_id=1, source_target_pairs={{0,4},{1,5},{2,6},{3,7},{4,0},{5,1},{6,2},{7,3},{8,12},{9,13},{10,... | collective-permute-start | bytes 294920 | tf_op jit(solution)/shard_map/ppermute | solution.py:101
  143.2 9.7 %copy-start.3 = (bf16[1152,896]{1,0:T(8,128)(2,1)S(1)}, bf16[1152,896]{1,0:T(8,128)(2,1)}, u32[]{:S(2)}) copy-start(bf16[1152,896]{1,0:T(8,128)(2,1)} %param.19) | copy-start | bytes 6193156
  143.2 5.9 %collective-permute-start.33 = (bf16[2,64,768]{2,1,0:T(8,128)(2,1)S(1)}, bf16[2,64,768]{2,1,0:T(8,128)(2,1)S(1)}, u32[]{:S(2)}, u32[]{:S(2)}) collective-permute-start(bf16[2,64,768]{2,1,0:T(8,128)(2,1)S(1)} %get-tuple-element.52), channel_id=1, source_target_pairs={{0,1},{1,0},{2,3},{3,2},{4,5},{5,4},{6,7},{7,6},{8,9},{9,8},{10,11... | collective-permute-start | bytes 589832 | tf_op jit(solution)/shard_map/ppermute | solution.py:101
  144.1 6.2 %collective-permute-start.30 = (bf16[2,64,768]{2,1,0:T(8,128)(2,1)S(1)}, bf16[2,64,768]{2,1,0:T(8,128)(2,1)S(1)}, u32[]{:S(2)}, u32[]{:S(2)}) collective-permute-start(bf16[2,64,768]{2,1,0:T(8,128)(2,1)S(1)} %get-tuple-element.54), channel_id=1, source_target_pairs={{0,4},{1,5},{2,6},{3,7},{4,0},{5,1},{6,2},{7,3},{8,12},{9,13},{10,... | collective-permute-start | bytes 589832 | tf_op jit(solution)/shard_map/ppermute | solution.py:101
  145.2 7.0 %collective-permute-start.24 = (bf16[2,64,768]{2,1,0:T(8,128)(2,1)S(1)}, bf16[2,64,768]{2,1,0:T(8,128)(2,1)S(1)}, u32[]{:S(2)}, u32[]{:S(2)}) collective-permute-start(bf16[2,64,768]{2,1,0:T(8,128)(2,1)S(1)} %get-tuple-element.56), channel_id=1, source_target_pairs={{0,3},{1,2},{2,1},{3,0},{4,7},{5,6},{6,5},{7,4},{8,11},{9,10},{10,... | collective-permute-start | bytes 589832 | tf_op jit(solution)/shard_map/ppermute | solution.py:101
  149.2 11.5 %collective-permute-start.34 = (bf16[2,2,64,768]{3,2,1,0:T(8,128)(2,1)S(1)}, bf16[2,2,64,768]{3,2,1,0:T(8,128)(2,1)S(1)}, u32[]{:S(2)}, u32[]{:S(2)}) collective-permute-start(bf16[2,2,64,768]{3,2,1,0:T(8,128)(2,1)S(1)} %pad_maximum_fusion.3.s2), channel_id=1, source_target_pairs={{0,4},{1,5},{2,6},{3,7},{4,0},{5,1},{6,2},{7,3},{8,12},{9,13},{10,... | collective-permute-start | bytes 1179656 | tf_op jit(solution)/shard_map/ppermute | solution.py:101
  150.3 10.4 %collective-permute-start.31 = (bf16[2,2,64,768]{3,2,1,0:T(8,128)(2,1)S(1)}, bf16[2,2,64,768]{3,2,1,0:T(8,128)(2,1)S(1)}, u32[]{:S(2)}, u32[]{:S(2)}) collective-permute-start(bf16[2,2,64,768]{3,2,1,0:T(8,128)(2,1)S(1)} %pad_maximum_fusion.2.s1), channel_id=1, source_target_pairs={{0,3},{1,2},{2,1},{3,0},{4,7},{5,6},{6,5},{7,4},{8,11},{9,10},{10,... | collective-permute-start | bytes 1179656 | tf_op jit(solution)/shard_map/ppermute | solution.py:101
  152.2 8.5 %collective-permute-start.25 = (bf16[2,2,64,768]{3,2,1,0:T(8,128)(2,1)S(1)}, bf16[2,2,64,768]{3,2,1,0:T(8,128)(2,1)S(1)}, u32[]{:S(2)}, u32[]{:S(2)}) collective-permute-start(bf16[2,2,64,768]{3,2,1,0:T(8,128)(2,1)S(1)} %pad_maximum_fusion.1.s0), channel_id=1, source_target_pairs={{0,1},{1,0},{2,3},{3,2},{4,5},{5,4},{6,7},{7,6},{8,9},{9,8},{10,11... | collective-permute-start | bytes 1179656 | tf_op jit(solution)/shard_map/ppermute | solution.py:101
  160.7 19.4 %copy-start.1 = (bf16[2,512,896]{2,1,0:T(8,128)(2,1)S(1)}, bf16[2,512,896]{2,1,0:T(8,128)(2,1)}, u32[]{:S(2)}) copy-start(bf16[2,512,896]{2,1,0:T(8,128)(2,1)} %param.14) | copy-start | bytes 5505028

commit v6 on v5

--- a/solution.py
+++ b/solution.py
@@ -18,8 +18,11 @@
 F32 = jnp.float32
 MIB = 2**20
 PLANES = [[2 * q + c for q in range(NQ)] for c in range(2)]
-ORDER = ((1, 3, 4), (3, 4, 1), (4, 1, 3))
+ORDER = ((4, 1, 3), (1, 3, 4), (3, 4, 1))
 NP = len(ORDER)
+
+
+ATTEND_GROUPS = ((0,), (1,), (2, 3), (4, 5, 6, 7))
 
 
 def attend_kernel(len_ref, q_ref, k_hbm, v_hbm, o_ref, k_ref, v_ref, rows_ref, k_sem, v_sem):
@@ -31,15 +34,13 @@
         pltpu.make_async_copy(v_hbm.at[m, t], v_ref.at[i], v_sem.at[i]).start()
     offsets = lax.broadcasted_iota(jnp.int32, (h, l), 1)
 
-    for step in range(nm * r // 2):
+    for group in ATTEND_GROUPS:
         outs = []
-        for u in range(2):
-            i = step * 2 + u
+        for i in group:
             m, t = i // r, i % r
             pltpu.make_async_copy(k_hbm.at[m, t], k_ref.at[i], k_sem.at[i]).wait()
             pltpu.make_async_copy(v_hbm.at[m, t], v_ref.at[i], v_sem.at[i]).wait()
-        for u in range(2):
-            i = step * 2 + u
+        for i in group:
             m, t = i // r, i % r
             scores = lax.dot_general(
                 q_ref[m, t], k_ref[i], (((1,), (1,)), ((), ())), preferred_element_type=F32
@@ -50,10 +51,10 @@
             outs.append(
                 jnp.dot(weights.astype(BF), v_ref[i], preferred_element_type=F32) / totals
             )
-        for u in range(2):
+        for i, out in zip(group, outs):
             for b in range(hd // QB):
                 cols = slice(b * QB, (b + 1) * QB)
-                block = outs[u][:, cols]
+                block = out[:, cols]
                 peak = jnp.max(jnp.abs(block), axis=1, keepdims=True)
                 scale = (peak + 1e-06).astype(BF).astype(F32)
                 levels = jnp.clip(jnp.floor(127.0 * block / scale + 0.5), -127.0, 127.0)
@@ -61,7 +62,7 @@
                 for head in range(h):
                     chip, at = divmod(head, h // NQ)
                     lanes = slice(at * hd + b * QB, at * hd + (b + 1) * QB)
-                    rows_ref[chip, step * 2 + u : step * 2 + u + 1, lanes] = value[head : head + 1]
+                    rows_ref[chip, i : i + 1, lanes] = value[head : head + 1]
 
     o_ref[...] = rows_ref[...].astype(BF)
 
@@ -353,8 +354,8 @@
     out = attend(queries, cache_keys, cache_values, lengths)
     got = over_chips(out).reshape(NQ * n, -1)
 
-    got, out_sib, gate_sib, up_sib, down_sib = lax.optimization_barrier(
-        (got, out_sib, gate_sib, up_sib, down_sib)
+    got, out_sib, gate_sib, up_sib, down_sib, res, gain, at = lax.optimization_barrier(
+        (got, out_sib, gate_sib, up_sib, down_sib, res, gain, at)
     )
     pieces = gather_ffn([got[:, x:y] for x, y in zip(PROJECT_CUTS, PROJECT_CUTS[1:])])
     part = project(at, pieces, *by_core(a, out_weight, out_sib))

time: 181 us -> 178 us (0.983)
  waiting for transfers between devices: 89.4 us -> 65.6 us
  blocking collectives: 15 us -> 31.9 us
  starting transfers between devices: 41.6 us -> 48.4 us
    all_to_all x1 -> x2, blocking collectives: 15 us -> 31.9 us  [over_chips(): return lax.all_to_all(x, 'attn', 0, 0, axis_index_groups=PLANES)]
    all_to_all x2 -> x1, waiting for transfers between devices: 20.9 us -> 8.68 us  [over_chips(): return lax.all_to_all(x, 'attn', 0, 0, axis_index_groups=PLANES)]
    ppermute x27, waiting for transfers between devices: 59.1 us -> 46.8 us  [fx(): return lax.ppermute(x, 'ffn', [(i, i ^ k) for i in range(N_FFN)])]
    ppermute x27, starting transfers between devices: 23.7 us -> 34.3 us  [fx(): return lax.ppermute(x, 'ffn', [(i, i ^ k) for i in range(N_FFN)])]
    all_to_all x2 -> x1, starting transfers between devices: 11.4 us -> 7.72 us  [over_chips(): return lax.all_to_all(x, 'attn', 0, 0, axis_index_groups=PLANES)]
  transfers between devices with their start and end apart: 37 -> 36, of which waited for: 22 -> 26; matrix products, arithmetic and copies ran while one was open for 5% -> 4% of each run, Pallas kernels for 5% -> 5%
where the time goes in v6:
time: 178 us
  waiting for transfers between devices  65.6 us (37%)
  starting transfers between devices  48.4 us (27%)
  blocking collectives  31.9 us (18%)
  Pallas kernels  22.8 us (13%)
  other arithmetic  8.19 us (5%)
    ppermute x27, waiting for transfers between devices, fx(): return lax.ppermute(x, 'ffn', [(i, i ^ k) for i in range(N_FFN)])  46.8 us
    ppermute x27, starting transfers between devices, fx(): return lax.ppermute(x, 'ffn', [(i, i ^ k) for i in range(N_FFN)])  34.3 us
    all_to_all x2, blocking collectives, over_chips(): return lax.all_to_all(x, 'attn', 0, 0, axis_index_groups=PLANES)  31.9 us
    ppermute x8, waiting for transfers between devices, ax(): return lax.ppermute(x, 'attn', [(i, i ^ k) for i in range(N_ATTN)])  10.1 us
    pallas_call x1, Pallas kernels, attend(): pl.pallas_call(attend_kernel, out_shape=jax.ShapeDtypeStruct((NQ, n, h *...  9.15 us
    all_to_all x1, waiting for transfers between devices, over_chips(): return lax.all_to_all(x, 'attn', 0, 0, axis_index_groups=PLANES)  8.68 us
    all_to_all x1, starting transfers between devices, over_chips(): return lax.all_to_all(x, 'attn', 0, 0, axis_index_groups=PLANES)  7.72 us
    select_n x3, other arithmetic, by_core(): return (jnp.where(a % 2 == 0, own, sib), jnp.where(a % 2 == 0, sib, own))  6.47 us
  transfers between devices with their start and end apart: 36, of which 26 were waited for; matrix products, arithmetic and copies ran while one was open for 4% of the time, Pallas kernels for 5%

profile of v6, /device:TPU:0, one launch (start us, length us, event | category | flops | bytes accessed | tf_op | source)
XLA Modules:
  0.0 177.5 jit_solution(15618844728832703560)
XLA Ops:
  1.0 9.2 %shard_map.100 = bf16[8,8,2048]{2,1,0:T(8,128)(2,1)} custom-call(s32[2,4]{1,0:T(2,128)} %len_ref.1, bf16[2,4,64,256]{3,2,1,0:T(8,128)(2,1)} %q_ref.1, bf16[2,4,1536,256]{3,2,1,0:T(8,128)(2,1)} %k_hbm.1, bf16[2,4,1536,256]{3,2,1,0:T(8,128)(2,1)} %v_hbm.1), custom_call_target="tpu_custom_call" | custom-call | flops 805306368 | bytes 12582912 | tf_op jit(solution)/shard_map/pallas_call | solution.py:73
  10.2 7.7 %all-to-all-start = ((bf16[8,8,2048]{2,1,0:T(8,128)(2,1)}), bf16[8,8,2048]{2,1,0:T(8,128)(2,1)S(1)}, u32[]{:S(2)}, u32[]{:S(2)}) async-start(bf16[8,8,2048]{2,1,0:T(8,128)(2,1)} %shard_map.100), calls=%async_computation | async-start | bytes 524288 | tf_op jit(solution)/shard_map/all_to_all | solution.py:106
  18.2 8.7 %all-to-all-done = bf16[8,8,2048]{2,1,0:T(8,128)(2,1)S(1)} async-done(((bf16[8,8,2048]{2,1,0:T(8,128)(2,1)}), bf16[8,8,2048]{2,1,0:T(8,128)(2,1)S(1)}, u32[]{:S(2)}, u32[]{:S(2)}) %all-to-all-start) | async-done | bytes 262176 | tf_op jit(solution)/shard_map/all_to_all | solution.py:106
  27.0 1.1 collective-permute-start.7
  28.1 3.1 %collective-permute-start.4 = (bf16[64,768]{1,0:T(8,128)(2,1)S(1)}, bf16[64,768]{1,0:T(8,128)(2,1)S(1)}, u32[]{:S(2)}, u32[]{:S(2)}) collective-permute-start(bf16[64,768]{1,0:T(8,128)(2,1)S(1)} %get-tuple-element.56), channel_id=1, source_target_pairs={{0,3},{1,2},{2,1},{3,0},{4,7},{5,6},{6,5},{7,4},{8,11},{9,10},{10,... | collective-permute-start | bytes 294920 | tf_op jit(solution)/shard_map/ppermute | solution.py:102
  31.6 3.1 %collective-permute-start.8 = (bf16[2,64,640]{2,1,0:T(8,128)(2,1)S(1)}, bf16[2,64,640]{2,1,0:T(8,128)(2,1)S(1)}, u32[]{:S(2)}, u32[]{:S(2)}) collective-permute-start(bf16[2,64,640]{2,1,0:T(8,128)(2,1)S(1)} %get-tuple-element.68), channel_id=1, source_target_pairs={{0,3},{1,2},{2,1},{3,0},{4,7},{5,6},{6,5},{7,4},{8,11},{9,10},{10,... | collective-permute-start | bytes 491528 | tf_op jit(solution)/shard_map/ppermute | solution.py:102
  34.6 1.0 collective-permute-done.10
  35.7 1.1 collective-permute-start.11
  37.0 1.1 collective-permute-done.8
  39.0 2.0 %collective-permute-done.11 = bf16[2,64,640]{2,1,0:T(8,128)(2,1)S(1)} collective-permute-done((bf16[2,64,640]{2,1,0:T(8,128)(2,1)S(1)}, bf16[2,64,640]{2,1,0:T(8,128)(2,1)S(1)}, u32[]{:S(2)}, u32[]{:S(2)}) %collective-permute-start.11) | collective-permute-done | bytes 163872 | tf_op jit(solution)/shard_map/ppermute | solution.py:102
  41.4 2.5 %collective-permute-done.5 = bf16[2,64,768]{2,1,0:T(8,128)(2,1)S(1)} collective-permute-done((bf16[2,64,768]{2,1,0:T(8,128)(2,1)S(1)}, bf16[2,64,768]{2,1,0:T(8,128)(2,1)S(1)}, u32[]{:S(2)}, u32[]{:S(2)}) %collective-permute-start.5) | collective-permute-done | bytes 196640 | tf_op jit(solution)/shard_map/ppermute | solution.py:102
  44.0 1.1 collective-permute-start.6
  45.2 1.9 %broadcast_select_fusion.6 = (bf16[1024,896]{1,0:T(8,128)(2,1)S(1)}, bf16[1024,896]{1,0:T(8,128)(2,1)S(1)}) fusion(bf16[1024,896]{1,0:T(8,128)(2,1)} %collective-permute-done, bf16[1024,896]{1,0:T(8,128)(2,1)S(1)} %copy-done.5, pred[]{:T(512)S(6)} %eq.20), kind=kLoop, calls=%fused_computation.6 | loop fusion | flops 1835008 | bytes 7340033 | tf_op jit(solution)/shard_map/jit(_where)/select_n | solution.py:304
  47.5 2.0 %collective-permute-done.12.r2 = bf16[2,2,64,640]{3,2,1,0:T(8,128)(2,1)S(1)} collective-permute-done((bf16[2,2,64,640]{3,2,1,0:T(8,128)(2,1)S(1)}, bf16[2,2,64,640]{3,2,1,0:T(8,128)(2,1)S(1)}, u32[]{:S(2)}, u32[]{:S(2)}) %collective-permute-start.12) | collective-permute-done | bytes 327712 | tf_op jit(solution)/shard_map/ppermute | solution.py:102
  49.5 2.4 %collective-permute-done.6.r0 = bf16[2,2,64,768]{3,2,1,0:T(8,128)(2,1)S(1)} collective-permute-done((bf16[2,2,64,768]{3,2,1,0:T(8,128)(2,1)S(1)}, bf16[2,2,64,768]{3,2,1,0:T(8,128)(2,1)S(1)}, u32[]{:S(2)}, u32[]{:S(2)}) %collective-permute-start.6) | collective-permute-done | bytes 393248 | tf_op jit(solution)/shard_map/ppermute | solution.py:102
  51.9 3.0 %shard_map.101 = bf16[8,64,896]{2,1,0:T(8,128)(2,1)S(1)} custom-call(s32[3]{0:T(128)S(1)} %pad_add_fusion.at_ref, bf16[2,2,64,768]{3,2,1,0:T(8,128)(2,1)S(1)} %pad_maximum_fusion.s0, bf16[2,2,64,768]{3,2,1,0:T(8,128)(2,1)S(1)} %collective-permute-done.6.r0, bf16[2,2,64,640]{3,2,1,0:T(8,128)(2,1)S(1)} %pad_maximum_fusion.4.s1, ...), custom_call_target="tpu_custom_call" | custom-call | flops 1879048192 | bytes 6291456 | tf_op jit(solution)/shard_map/pallas_call | solution.py:159
  54.9 15.5 %all_to_all.15.got_ref = bf16[8,64,896]{2,1,0:T(8,128)(2,1)S(1)} all-to-all(bf16[8,64,896]{2,1,0:T(8,128)(2,1)S(1)} %shard_map.101), channel_id=1, replica_groups={{0,16,32,48,64,80,96,112},{8,24,40,56,72,88,104,120},{1,17,33,49,65,81,..., dimensions={0} | all-to-all | bytes 1835008 | tf_op jit(solution)/shard_map/all_to_all | solution.py:106
  71.2 5.7 %collective-permute-done.13 = bf16[64,896]{1,0:T(8,128)(2,1)S(1)} collective-permute-done((bf16[64,896]{1,0:T(8,128)(2,1)S(1)}, bf16[64,896]{1,0:T(8,128)(2,1)S(1)}, u32[]{:S(2)}, u32[]{:S(2)}) %collective-permute-start.13) | collective-permute-done | bytes 114720 | tf_op jit(solution)/shard_map/ppermute | solution.py:98
  77.9 1.9 %collective-permute-start.15 = (bf16[2,64,896]{2,1,0:T(8,128)(2,1)S(1)}, bf16[2,64,896]{2,1,0:T(8,128)(2,1)S(1)}, u32[]{:S(2)}, u32[]{:S(2)}) collective-permute-start(bf16[2,64,896]{2,1,0:T(8,128)(2,1)S(1)} %pad_maximum_fusion.6.p0), channel_id=1, source_target_pairs={{0,32},{8,40},{16,48},{24,56},{32,0},{40,8},{48,16},{56,24},{64,96... | collective-permute-start | bytes 688136 | tf_op jit(solution)/shard_map/ppermute | solution.py:98
  79.8 1.9 %collective-permute-start.16 = (bf16[2,64,896]{2,1,0:T(8,128)(2,1)S(1)}, bf16[2,64,896]{2,1,0:T(8,128)(2,1)S(1)}, u32[]{:S(2)}, u32[]{:S(2)}) collective-permute-start(bf16[2,64,896]{2,1,0:T(8,128)(2,1)S(1)} %pad_maximum_fusion.6.p0), channel_id=1, source_target_pairs={{0,48},{8,56},{16,32},{24,40},{32,16},{40,24},{48,0},{56,8},{64,11... | collective-permute-start | bytes 688136 | tf_op jit(solution)/shard_map/ppermute | solution.py:98
  81.8 2.6 %broadcast_select_fusion.2 = (bf16[896,1152]{1,0:T(8,128)(2,1)S(1)}, bf16[896,1152]{1,0:T(8,128)(2,1)S(1)}, bf16[896,1152]{1,0:T(8,128)(2,1)S(1)}, bf16[896,1152]{1,0:T(8,128)(2,1)S(1)}) fusion(bf16[896,1152]{1,0:T(8,128)(2,1)} %collective-permute-done.2, bf16[896,1152]{1,0:T(8,128)(2,1)S(1)} %copy-done.2, pred[]{:T(512)S(6)} %eq.20, ...), kind=kLoop, calls=%fused_computation.2 | loop fusion | flops 4128768 | bytes 16515073 | tf_op jit(solution)/shard_map/jit(_where)/select_n | solution.py:304
  84.4 2.0 %collective-permute-done.15.p2 = bf16[2,64,896]{2,1,0:T(8,128)(2,1)S(1)} collective-permute-done((bf16[2,64,896]{2,1,0:T(8,128)(2,1)S(1)}, bf16[2,64,896]{2,1,0:T(8,128)(2,1)S(1)}, u32[]{:S(2)}, u32[]{:S(2)}) %collective-permute-start.15) | collective-permute-done | bytes 229408 | tf_op jit(solution)/shard_map/ppermute | solution.py:98
  86.4 2.4 %collective-permute-done.16.p3 = bf16[2,64,896]{2,1,0:T(8,128)(2,1)S(1)} collective-permute-done((bf16[2,64,896]{2,1,0:T(8,128)(2,1)S(1)}, bf16[2,64,896]{2,1,0:T(8,128)(2,1)S(1)}, u32[]{:S(2)}, u32[]{:S(2)}) %collective-permute-start.16) | collective-permute-done | bytes 229408 | tf_op jit(solution)/shard_map/ppermute | solution.py:98
  88.7 6.1 %shard_map.103 = (bf16[2,2,64,1536]{3,2,1,0:T(8,128)(2,1)S(1)}, bf16[2,2,64,1536]{3,2,1,0:T(8,128)(2,1)S(1)}, bf16[2,2,64,1536]{3,2,1,0:T(8,128)(2,1)S(1)}, bf16...) custom-call(s32[3]{0:T(128)S(1)} %pad_add_fusion.at_ref, ...), custom_call_target="tpu_custom_call" | custom-call | flops 4227858432 | bytes 14680064 | tf_op jit(solution)/shard_map/pallas_call | solution.py:233
  96.2 1.1 collective-permute-start.20
  97.2 12.5 %collective-permute-done.17 = bf16[2,2,64,1536]{3,2,1,0:T(8,128)(2,1)S(1)} collective-permute-done((bf16[2,2,64,1536]{3,2,1,0:T(8,128)(2,1)S(1)}, bf16[2,2,64,1536]{3,2,1,0:T(8,128)(2,1)S(1)}, u32[]{:S(2)}, u32[]{:S(2)}) %collective-permute-start.17) | collective-permute-done | bytes 786464 | tf_op jit(solution)/shard_map/ppermute | solution.py:102
  110.0 2.1 %collective-permute-done.26 = bf16[2,2,64,1536]{3,2,1,0:T(8,128)(2,1)S(1)} collective-permute-done((bf16[2,2,64,1536]{3,2,1,0:T(8,128)(2,1)S(1)}, bf16[2,2,64,1536]{3,2,1,0:T(8,128)(2,1)S(1)}, u32[]{:S(2)}, u32[]{:S(2)}) %collective-permute-start.26) | collective-permute-done | bytes 786464 | tf_op jit(solution)/shard_map/ppermute | solution.py:102
  112.2 1.3 collective-permute-start.27
  113.5 1.4 collective-permute-done.20
  115.0 1.3 collective-permute-start.21
  116.3 3.3 %collective-permute-done.18 = bf16[2,64,1536]{2,1,0:T(8,128)(2,1)S(1)} collective-permute-done((bf16[2,64,1536]{2,1,0:T(8,128)(2,1)S(1)}, bf16[2,64,1536]{2,1,0:T(8,128)(2,1)S(1)}, u32[]{:S(2)}, u32[]{:S(2)}) %collective-permute-start.18) | collective-permute-done | bytes 393248 | tf_op jit(solution)/shard_map/ppermute | solution.py:102
  119.7 2.2 %collective-permute-start.19 = (bf16[64,1536]{1,0:T(8,128)(2,1)S(1)}, bf16[64,1536]{1,0:T(8,128)(2,1)S(1)}, u32[]{:S(2)}, u32[]{:S(2)}) collective-permute-start(bf16[64,1536]{1,0:T(8,128)(2,1)S(1)} %fusion.7), channel_id=1, source_target_pairs={{0,3},{1,2},{2,1},{3,0},{4,7},{5,6},{6,5},{7,4},{8,11},{9,10},{10,... | collective-permute-start | bytes 589832 | tf_op jit(solution)/shard_map/ppermute | solution.py:102
  123.3 2.6 %collective-permute-start.22 = (bf16[64,1664]{1,0:T(8,128)(2,1)S(1)}, bf16[64,1664]{1,0:T(8,128)(2,1)S(1)}, u32[]{:S(2)}, u32[]{:S(2)}) collective-permute-start(bf16[64,1664]{1,0:T(8,128)(2,1)S(1)} %fusion.1), channel_id=1, source_target_pairs={{0,1},{1,0},{2,3},{3,2},{4,5},{5,4},{6,7},{7,6},{8,9},{9,8},{10,11... | collective-permute-start | bytes 638984 | tf_op jit(solution)/shard_map/ppermute | solution.py:102
  125.9 1.7 collective-permute-done.19
  128.4 3.1 %collective-permute-done.22 = bf16[64,1664]{1,0:T(8,128)(2,1)S(1)} collective-permute-done((bf16[64,1664]{1,0:T(8,128)(2,1)S(1)}, bf16[64,1664]{1,0:T(8,128)(2,1)S(1)}, u32[]{:S(2)}, u32[]{:S(2)}) %collective-permute-start.22) | collective-permute-done | bytes 213024 | tf_op jit(solution)/shard_map/ppermute | solution.py:102
  132.7 3.3 %collective-permute-start.29 = (bf16[64,768]{1,0:T(8,128)(2,1)S(1)}, bf16[64,768]{1,0:T(8,128)(2,1)S(1)}, u32[]{:S(2)}, u32[]{:S(2)}) collective-permute-start(bf16[64,768]{1,0:T(8,128)(2,1)S(1)} %pad_maximum_fusion.14), channel_id=1, source_target_pairs={{0,4},{1,5},{2,6},{3,7},{4,0},{5,1},{6,2},{7,3},{8,12},{9,13},{10,... | collective-permute-start | bytes 294920 | tf_op jit(solution)/shard_map/ppermute | solution.py:102
  136.2 1.7 collective-permute-done.23
  137.9 2.4 %collective-permute-start.24 = (bf16[2,64,768]{2,1,0:T(8,128)(2,1)S(1)}, bf16[2,64,768]{2,1,0:T(8,128)(2,1)S(1)}, u32[]{:S(2)}, u32[]{:S(2)}) collective-permute-start(bf16[2,64,768]{2,1,0:T(8,128)(2,1)S(1)} %get-tuple-element.62), channel_id=1, source_target_pairs={{0,1},{1,0},{2,3},{3,2},{4,5},{5,4},{6,7},{7,6},{8,9},{9,8},{10,11... | collective-permute-start | bytes 589832 | tf_op jit(solution)/shard_map/ppermute | solution.py:102
  141.3 1.9 %collective-permute-start.33 = (bf16[2,64,768]{2,1,0:T(8,128)(2,1)S(1)}, bf16[2,64,768]{2,1,0:T(8,128)(2,1)S(1)}, u32[]{:S(2)}, u32[]{:S(2)}) collective-permute-start(bf16[2,64,768]{2,1,0:T(8,128)(2,1)S(1)} %get-tuple-element.58), channel_id=1, source_target_pairs={{0,4},{1,5},{2,6},{3,7},{4,0},{5,1},{6,2},{7,3},{8,12},{9,13},{10,... | collective-permute-start | bytes 589832 | tf_op jit(solution)/shard_map/ppermute | solution.py:102
  144.0 1.1 collective-permute-start.25
  145.1 2.2 %collective-permute-done.30 = bf16[2,64,768]{2,1,0:T(8,128)(2,1)S(1)} collective-permute-done((bf16[2,64,768]{2,1,0:T(8,128)(2,1)S(1)}, bf16[2,64,768]{2,1,0:T(8,128)(2,1)S(1)}, u32[]{:S(2)}, u32[]{:S(2)}) %collective-permute-start.30) | collective-permute-done | bytes 196640 | tf_op jit(solution)/shard_map/ppermute | solution.py:102
  147.5 2.3 %collective-permute-start.34 = (bf16[2,2,64,768]{3,2,1,0:T(8,128)(2,1)S(1)}, bf16[2,2,64,768]{3,2,1,0:T(8,128)(2,1)S(1)}, u32[]{:S(2)}, u32[]{:S(2)}) collective-permute-start(bf16[2,2,64,768]{3,2,1,0:T(8,128)(2,1)S(1)} %pad_maximum_fusion.3.s2), channel_id=1, source_target_pairs={{0,3},{1,2},{2,1},{3,0},{4,7},{5,6},{6,5},{7,4},{8,11},{9,10},{10,... | collective-permute-start | bytes 1179656 | tf_op jit(solution)/shard_map/ppermute | solution.py:102
  149.8 2.0 %broadcast_select_fusion = (bf16[1152,896]{1,0:T(8,128)(2,1)S(1)}, bf16[1152,896]{1,0:T(8,128)(2,1)S(1)}) fusion(bf16[1152,896]{1,0:T(8,128)(2,1)} %collective-permute-done.3, bf16[1152,896]{1,0:T(8,128)(2,1)S(1)} %copy-done.4, pred[]{:T(512)S(6)} %eq.20), kind=kLoop, calls=%fused_computation | loop fusion | flops 2064384 | bytes 8257537 | tf_op jit(solution)/shard_map/jit(_where)/select_n | solution.py:304
  151.7 1.2 collective-permute-done.25.r0
  153.0 2.2 %collective-permute-done.31.r1 = bf16[2,2,64,768]{3,2,1,0:T(8,128)(2,1)S(1)} collective-permute-done((bf16[2,2,64,768]{3,2,1,0:T(8,128)(2,1)S(1)}, bf16[2,2,64,768]{3,2,1,0:T(8,128)(2,1)S(1)}, u32[]{:S(2)}, u32[]{:S(2)}) %collective-permute-start.31) | collective-permute-done | bytes 393248 | tf_op jit(solution)/shard_map/ppermute | solution.py:102
  155.2 1.6 collective-permute-done.34.r2
  156.8 3.5 %shard_map.104 = bf16[512,896]{1,0:T(8,128)(2,1)S(1)} custom-call(s32[3]{0:T(128)S(1)} %pad_add_fusion.at_ref, bf16[2,2,64,768]{3,2,1,0:T(8,128)(2,1)S(1)} %pad_maximum_fusion.1.s0, bf16[2,2,64,768]{3,2,1,0:T(8,128)(2,1)S(1)} %collective-permute-done.25.r0, bf16[2,2,64,768]{3,2,1,0:T(8,128)(2,1)S(1)} %pad_maximum_fusion.2.s1, ...), custom_call_target="tpu_custom_call" | custom-call | flops 2113929216 | bytes 6291456 | tf_op jit(solution)/shard_map/pallas_call | solution.py:268
  160.3 16.4 %all_to_all.16.got_ref = bf16[8,64,896]{2,1,0:T(8,128)(2,1)S(1)} all-to-all(bf16[8,64,896]{2,1,0:T(8,128)(2,1)S(1)} %bitcast.94), channel_id=1, replica_groups={{0,16,32,48,64,80,96,112},{8,24,40,56,72,88,104,120},{1,17,33,49,65,81,..., dimensions={0} | all-to-all | bytes 1835008 | tf_op jit(solution)/shard_map/all_to_all | solution.py:106
  (84 shorter events, 13.5 us)
Async XLA Ops:
  0.0 17.9 %copy-start = (bf16[2,512,896]{2,1,0:T(8,128)(2,1)S(1)}, bf16[2,512,896]{2,1,0:T(8,128)(2,1)}, u32[]{:S(2)}) copy-start(bf16[2,512,896]{2,1,0:T(8,128)(2,1)} %param.14) | copy-start | bytes 5505028
  0.0 18.1 %copy-start.6 = (bf16[896]{0:T(1024)(128)(2,1)S(1)}, bf16[896]{0:T(1024)(128)(2,1)}, u32[]{:S(2)}) copy-start(bf16[896]{0:T(1024)(128)(2,1)} %param.15) | copy-start | bytes 5380
  0.0 26.9 %collective-permute-start.1 = (bf16[896,1152]{1,0:T(8,128)(2,1)}, bf16[896,1152]{1,0:T(8,128)(2,1)}, u32[]{:S(2)}, u32[]{:S(2)}) collective-permute-start(bf16[896,1152]{1,0:T(8,128)(2,1)} %param.17), channel_id=1, source_target_pairs={{0,8},{8,0},{16,24},{24,16},{32,40},{40,32},{48,56},{56,48},{64,72... | collective-permute-start | bytes 6193160 | tf_op jit(solution)/shard_map/ppermute | solution.py:98
  0.0 26.9 %collective-permute-start.2 = (bf16[896,1152]{1,0:T(8,128)(2,1)}, bf16[896,1152]{1,0:T(8,128)(2,1)}, u32[]{:S(2)}, u32[]{:S(2)}) collective-permute-start(bf16[896,1152]{1,0:T(8,128)(2,1)} %param.18), channel_id=1, source_target_pairs={{0,8},{8,0},{16,24},{24,16},{32,40},{40,32},{48,56},{56,48},{64,72... | collective-permute-start | bytes 6193160 | tf_op jit(solution)/shard_map/ppermute | solution.py:98
  0.5 26.4 %collective-permute-start.3 = (bf16[1152,896]{1,0:T(8,128)(2,1)}, bf16[1152,896]{1,0:T(8,128)(2,1)}, u32[]{:S(2)}, u32[]{:S(2)}) collective-permute-start(bf16[1152,896]{1,0:T(8,128)(2,1)} %param.19), channel_id=1, source_target_pairs={{0,8},{8,0},{16,24},{24,16},{32,40},{40,32},{48,56},{56,48},{64,72... | collective-permute-start | bytes 6193160 | tf_op jit(solution)/shard_map/ppermute | solution.py:98
  0.5 26.4 %collective-permute-start = (bf16[1024,896]{1,0:T(8,128)(2,1)}, bf16[1024,896]{1,0:T(8,128)(2,1)}, u32[]{:S(2)}, u32[]{:S(2)}) collective-permute-start(bf16[1024,896]{1,0:T(8,128)(2,1)} %param.16), channel_id=1, source_target_pairs={{0,8},{8,0},{16,24},{24,16},{32,40},{40,32},{48,56},{56,48},{64,72... | collective-permute-start | bytes 5505032 | tf_op jit(solution)/shard_map/ppermute | solution.py:98
  10.2 16.7 %all-to-all-start = ((bf16[8,8,2048]{2,1,0:T(8,128)(2,1)}), bf16[8,8,2048]{2,1,0:T(8,128)(2,1)S(1)}, u32[]{:S(2)}, u32[]{:S(2)}) async-start(bf16[8,8,2048]{2,1,0:T(8,128)(2,1)} %shard_map.100), calls=%async_computation | async-start | bytes 524288 | tf_op jit(solution)/shard_map/all_to_all | solution.py:106
  27.0 18.2 %copy-start.5 = (bf16[1024,896]{1,0:T(8,128)(2,1)S(1)}, bf16[1024,896]{1,0:T(8,128)(2,1)}, u32[]{:S(2)}) copy-start(bf16[1024,896]{1,0:T(8,128)(2,1)} %param.16) | copy-start | bytes 5505028
  27.0 4.5 %collective-permute-start.7 = (bf16[64,640]{1,0:T(8,128)(2,1)S(1)}, bf16[64,640]{1,0:T(8,128)(2,1)S(1)}, u32[]{:S(2)}, u32[]{:S(2)}) collective-permute-start(bf16[64,640]{1,0:T(8,128)(2,1)S(1)} %get-tuple-element.54), channel_id=1, source_target_pairs={{0,4},{1,5},{2,6},{3,7},{4,0},{5,1},{6,2},{7,3},{8,12},{9,13},{10,... | collective-permute-start | bytes 245768 | tf_op jit(solution)/shard_map/ppermute | solution.py:102
  28.1 8.7 %collective-permute-start.4 = (bf16[64,768]{1,0:T(8,128)(2,1)S(1)}, bf16[64,768]{1,0:T(8,128)(2,1)S(1)}, u32[]{:S(2)}, u32[]{:S(2)}) collective-permute-start(bf16[64,768]{1,0:T(8,128)(2,1)S(1)} %get-tuple-element.56), channel_id=1, source_target_pairs={{0,3},{1,2},{2,1},{3,0},{4,7},{5,6},{6,5},{7,4},{8,11},{9,10},{10,... | collective-permute-start | bytes 294920 | tf_op jit(solution)/shard_map/ppermute | solution.py:102
  31.2 4.4 %collective-permute-start.10 = (bf16[64,640]{1,0:T(8,128)(2,1)S(1)}, bf16[64,640]{1,0:T(8,128)(2,1)S(1)}, u32[]{:S(2)}, u32[]{:S(2)}) collective-permute-start(bf16[64,640]{1,0:T(8,128)(2,1)S(1)} %get-tuple-element.53), channel_id=1, source_target_pairs={{0,1},{1,0},{2,3},{3,2},{4,5},{5,4},{6,7},{7,6},{8,9},{9,8},{10,11... | collective-permute-start | bytes 245768 | tf_op jit(solution)/shard_map/ppermute | solution.py:102
  31.6 6.6 %collective-permute-start.8 = (bf16[2,64,640]{2,1,0:T(8,128)(2,1)S(1)}, bf16[2,64,640]{2,1,0:T(8,128)(2,1)S(1)}, u32[]{:S(2)}, u32[]{:S(2)}) collective-permute-start(bf16[2,64,640]{2,1,0:T(8,128)(2,1)S(1)} %get-tuple-element.68), channel_id=1, source_target_pairs={{0,3},{1,2},{2,1},{3,0},{4,7},{5,6},{6,5},{7,4},{8,11},{9,10},{10,... | collective-permute-start | bytes 491528 | tf_op jit(solution)/shard_map/ppermute | solution.py:102
  35.7 5.4 %collective-permute-start.11 = (bf16[2,64,640]{2,1,0:T(8,128)(2,1)S(1)}, bf16[2,64,640]{2,1,0:T(8,128)(2,1)S(1)}, u32[]{:S(2)}, u32[]{:S(2)}) collective-permute-start(bf16[2,64,640]{2,1,0:T(8,128)(2,1)S(1)} %get-tuple-element.66), channel_id=1, source_target_pairs={{0,4},{1,5},{2,6},{3,7},{4,0},{5,1},{6,2},{7,3},{8,12},{9,13},{10,... | collective-permute-start | bytes 491528 | tf_op jit(solution)/shard_map/ppermute | solution.py:102
  36.8 7.2 %collective-permute-start.5 = (bf16[2,64,768]{2,1,0:T(8,128)(2,1)S(1)}, bf16[2,64,768]{2,1,0:T(8,128)(2,1)S(1)}, u32[]{:S(2)}, u32[]{:S(2)}) collective-permute-start(bf16[2,64,768]{2,1,0:T(8,128)(2,1)S(1)} %get-tuple-element.64), channel_id=1, source_target_pairs={{0,1},{1,0},{2,3},{3,2},{4,5},{5,4},{6,7},{7,6},{8,9},{9,8},{10,11... | collective-permute-start | bytes 589832 | tf_op jit(solution)/shard_map/ppermute | solution.py:102
  38.2 9.3 %collective-permute-start.9 = (bf16[2,2,64,640]{3,2,1,0:T(8,128)(2,1)S(1)}, bf16[2,2,64,640]{3,2,1,0:T(8,128)(2,1)S(1)}, u32[]{:S(2)}, u32[]{:S(2)}) collective-permute-start(bf16[2,2,64,640]{3,2,1,0:T(8,128)(2,1)S(1)} %pad_maximum_fusion.4.s1), channel_id=1, source_target_pairs={{0,1},{1,0},{2,3},{3,2},{4,5},{5,4},{6,7},{7,6},{8,9},{9,8},{10,11... | collective-permute-start | bytes 983048 | tf_op jit(solution)/shard_map/ppermute | solution.py:102
  41.1 8.4 %collective-permute-start.12 = (bf16[2,2,64,640]{3,2,1,0:T(8,128)(2,1)S(1)}, bf16[2,2,64,640]{3,2,1,0:T(8,128)(2,1)S(1)}, u32[]{:S(2)}, u32[]{:S(2)}) collective-permute-start(bf16[2,2,64,640]{3,2,1,0:T(8,128)(2,1)S(1)} %pad_maximum_fusion.5.s2), channel_id=1, source_target_pairs={{0,3},{1,2},{2,1},{3,0},{4,7},{5,6},{6,5},{7,4},{8,11},{9,10},{10,... | collective-permute-start | bytes 983048 | tf_op jit(solution)/shard_map/ppermute | solution.py:102
  44.0 7.9 %collective-permute-start.6 = (bf16[2,2,64,768]{3,2,1,0:T(8,128)(2,1)S(1)}, bf16[2,2,64,768]{3,2,1,0:T(8,128)(2,1)S(1)}, u32[]{:S(2)}, u32[]{:S(2)}) collective-permute-start(bf16[2,2,64,768]{3,2,1,0:T(8,128)(2,1)S(1)} %pad_maximum_fusion.s0), channel_id=1, source_target_pairs={{0,4},{1,5},{2,6},{3,7},{4,0},{5,1},{6,2},{7,3},{8,12},{9,13},{10,... | collective-permute-start | bytes 1179656 | tf_op jit(solution)/shard_map/ppermute | solution.py:102
  51.9 29.9 %copy-start.3 = (bf16[896,1152]{1,0:T(8,128)(2,1)S(1)}, bf16[896,1152]{1,0:T(8,128)(2,1)}, u32[]{:S(2)}) copy-start(bf16[896,1152]{1,0:T(8,128)(2,1)} %param.17) | copy-start | bytes 6193156
  54.9 26.9 %copy-start.2 = (bf16[896,1152]{1,0:T(8,128)(2,1)S(1)}, bf16[896,1152]{1,0:T(8,128)(2,1)}, u32[]{:S(2)}) copy-start(bf16[896,1152]{1,0:T(8,128)(2,1)} %param.18) | copy-start | bytes 6193156
  70.6 6.4 %collective-permute-start.13 = (bf16[64,896]{1,0:T(8,128)(2,1)S(1)}, bf16[64,896]{1,0:T(8,128)(2,1)S(1)}, u32[]{:S(2)}, u32[]{:S(2)}) collective-permute-start(bf16[64,896]{1,0:T(8,128)(2,1)S(1)} %get-tuple-element.26), channel_id=1, source_target_pairs={{0,64},{8,72},{16,80},{24,88},{32,96},{40,104},{48,112},{56,120},{... | collective-permute-start | bytes 344072 | tf_op jit(solution)/shard_map/ppermute | solution.py:98
  77.0 7.4 %collective-permute-start.14 = (bf16[2,64,896]{2,1,0:T(8,128)(2,1)S(1)}, bf16[2,64,896]{2,1,0:T(8,128)(2,1)S(1)}, u32[]{:S(2)}, u32[]{:S(2)}) collective-permute-start(bf16[2,64,896]{2,1,0:T(8,128)(2,1)S(1)} %pad_maximum_fusion.6.p0), channel_id=1, source_target_pairs={{0,16},{8,24},{16,0},{24,8},{32,48},{40,56},{48,32},{56,40},{64,80... | collective-permute-start | bytes 688136 | tf_op jit(solution)/shard_map/ppermute | solution.py:98
  77.9 8.5 %collective-permute-start.15 = (bf16[2,64,896]{2,1,0:T(8,128)(2,1)S(1)}, bf16[2,64,896]{2,1,0:T(8,128)(2,1)S(1)}, u32[]{:S(2)}, u32[]{:S(2)}) collective-permute-start(bf16[2,64,896]{2,1,0:T(8,128)(2,1)S(1)} %pad_maximum_fusion.6.p0), channel_id=1, source_target_pairs={{0,32},{8,40},{16,48},{24,56},{32,0},{40,8},{48,16},{56,24},{64,96... | collective-permute-start | bytes 688136 | tf_op jit(solution)/shard_map/ppermute | solution.py:98
  79.8 8.9 %collective-permute-start.16 = (bf16[2,64,896]{2,1,0:T(8,128)(2,1)S(1)}, bf16[2,64,896]{2,1,0:T(8,128)(2,1)S(1)}, u32[]{:S(2)}, u32[]{:S(2)}) collective-permute-start(bf16[2,64,896]{2,1,0:T(8,128)(2,1)S(1)} %pad_maximum_fusion.6.p0), channel_id=1, source_target_pairs={{0,48},{8,56},{16,32},{24,40},{32,16},{40,24},{48,0},{56,8},{64,11... | collective-permute-start | bytes 688136 | tf_op jit(solution)/shard_map/ppermute | solution.py:98
  94.9 14.9 %collective-permute-start.17 = (bf16[2,2,64,1536]{3,2,1,0:T(8,128)(2,1)S(1)}, bf16[2,2,64,1536]{3,2,1,0:T(8,128)(2,1)S(1)}, u32[]{:S(2)}, u32[]{:S(2)}) collective-permute-start(bf16[2,2,64,1536]{3,2,1,0:T(8,128)(2,1)S(1)} %get-tuple-element.30), channel_id=1, source_target_pairs={{0,4},{1,5},{2,6},{3,7},{4,0},{5,1},{6,2},{7,3},{8,12},{9,13},{10,... | collective-permute-start | bytes 2359304 | tf_op jit(solution)/shard_map/ppermute | solution.py:102
  95.9 16.2 %collective-permute-start.26 = (bf16[2,2,64,1536]{3,2,1,0:T(8,128)(2,1)S(1)}, bf16[2,2,64,1536]{3,2,1,0:T(8,128)(2,1)S(1)}, u32[]{:S(2)}, u32[]{:S(2)}) collective-permute-start(bf16[2,2,64,1536]{3,2,1,0:T(8,128)(2,1)S(1)} %get-tuple-element.34), channel_id=1, source_target_pairs={{0,1},{1,0},{2,3},{3,2},{4,5},{5,4},{6,7},{7,6},{8,9},{9,8},{10,11... | collective-permute-start | bytes 2359304 | tf_op jit(solution)/shard_map/ppermute | solution.py:102
  96.2 18.7 %collective-permute-start.20 = (bf16[2,2,64,1664]{3,2,1,0:T(8,128)(2,1)S(1)}, bf16[2,2,64,1664]{3,2,1,0:T(8,128)(2,1)S(1)}, u32[]{:S(2)}, u32[]{:S(2)}) collective-permute-start(bf16[2,2,64,1664]{3,2,1,0:T(8,128)(2,1)S(1)} %get-tuple-element.32), channel_id=1, source_target_pairs={{0,3},{1,2},{2,1},{3,0},{4,7},{5,6},{6,5},{7,4},{8,11},{9,10},{10,... | collective-permute-start | bytes 2555912 | tf_op jit(solution)/shard_map/ppermute | solution.py:102
  109.9 9.8 %collective-permute-start.18 = (bf16[2,64,1536]{2,1,0:T(8,128)(2,1)S(1)}, bf16[2,64,1536]{2,1,0:T(8,128)(2,1)S(1)}, u32[]{:S(2)}, u32[]{:S(2)}) collective-permute-start(bf16[2,64,1536]{2,1,0:T(8,128)(2,1)S(1)} %fusion.3), channel_id=1, source_target_pairs={{0,1},{1,0},{2,3},{3,2},{4,5},{5,4},{6,7},{7,6},{8,9},{9,8},{10,11... | collective-permute-start | bytes 1179656 | tf_op jit(solution)/shard_map/ppermute | solution.py:102
  112.2 9.7 %collective-permute-start.27 = (bf16[2,64,1536]{2,1,0:T(8,128)(2,1)S(1)}, bf16[2,64,1536]{2,1,0:T(8,128)(2,1)S(1)}, u32[]{:S(2)}, u32[]{:S(2)}) collective-permute-start(bf16[2,64,1536]{2,1,0:T(8,128)(2,1)S(1)} %fusion.4), channel_id=1, source_target_pairs={{0,3},{1,2},{2,1},{3,0},{4,7},{5,6},{6,5},{7,4},{8,11},{9,10},{10,... | collective-permute-start | bytes 1179656 | tf_op jit(solution)/shard_map/ppermute | solution.py:102
  115.0 8.2 %collective-permute-start.21 = (bf16[2,64,1664]{2,1,0:T(8,128)(2,1)S(1)}, bf16[2,64,1664]{2,1,0:T(8,128)(2,1)S(1)}, u32[]{:S(2)}, u32[]{:S(2)}) collective-permute-start(bf16[2,64,1664]{2,1,0:T(8,128)(2,1)S(1)} %fusion), channel_id=1, source_target_pairs={{0,4},{1,5},{2,6},{3,7},{4,0},{5,1},{6,2},{7,3},{8,12},{9,13},{10,... | collective-permute-start | bytes 1277960 | tf_op jit(solution)/shard_map/ppermute | solution.py:102
  119.7 7.9 %collective-permute-start.19 = (bf16[64,1536]{1,0:T(8,128)(2,1)S(1)}, bf16[64,1536]{1,0:T(8,128)(2,1)S(1)}, u32[]{:S(2)}, u32[]{:S(2)}) collective-permute-start(bf16[64,1536]{1,0:T(8,128)(2,1)S(1)} %fusion.7), channel_id=1, source_target_pairs={{0,3},{1,2},{2,1},{3,0},{4,7},{5,6},{6,5},{7,4},{8,11},{9,10},{10,... | collective-permute-start | bytes 589832 | tf_op jit(solution)/shard_map/ppermute | solution.py:102
  122.0 6.3 %collective-permute-start.28 = (bf16[64,1536]{1,0:T(8,128)(2,1)S(1)}, bf16[64,1536]{1,0:T(8,128)(2,1)S(1)}, u32[]{:S(2)}, u32[]{:S(2)}) collective-permute-start(bf16[64,1536]{1,0:T(8,128)(2,1)S(1)} %fusion.5), channel_id=1, source_target_pairs={{0,4},{1,5},{2,6},{3,7},{4,0},{5,1},{6,2},{7,3},{8,12},{9,13},{10,... | collective-permute-start | bytes 589832 | tf_op jit(solution)/shard_map/ppermute | solution.py:102
  123.3 8.1 %collective-permute-start.22 = (bf16[64,1664]{1,0:T(8,128)(2,1)S(1)}, bf16[64,1664]{1,0:T(8,128)(2,1)S(1)}, u32[]{:S(2)}, u32[]{:S(2)}) collective-permute-start(bf16[64,1664]{1,0:T(8,128)(2,1)S(1)} %fusion.1), channel_id=1, source_target_pairs={{0,1},{1,0},{2,3},{3,2},{4,5},{5,4},{6,7},{7,6},{8,9},{9,8},{10,11... | collective-permute-start | bytes 638984 | tf_op jit(solution)/shard_map/ppermute | solution.py:102
  132.0 5.9 %collective-permute-start.23 = (bf16[64,768]{1,0:T(8,128)(2,1)S(1)}, bf16[64,768]{1,0:T(8,128)(2,1)S(1)}, u32[]{:S(2)}, u32[]{:S(2)}) collective-permute-start(bf16[64,768]{1,0:T(8,128)(2,1)S(1)} %pad_maximum_fusion.13), channel_id=1, source_target_pairs={{0,3},{1,2},{2,1},{3,0},{4,7},{5,6},{6,5},{7,4},{8,11},{9,10},{10,... | collective-permute-start | bytes 294920 | tf_op jit(solution)/shard_map/ppermute | solution.py:102
  132.7 7.5 %collective-permute-start.29 = (bf16[64,768]{1,0:T(8,128)(2,1)S(1)}, bf16[64,768]{1,0:T(8,128)(2,1)S(1)}, u32[]{:S(2)}, u32[]{:S(2)}) collective-permute-start(bf16[64,768]{1,0:T(8,128)(2,1)S(1)} %pad_maximum_fusion.14), channel_id=1, source_target_pairs={{0,4},{1,5},{2,6},{3,7},{4,0},{5,1},{6,2},{7,3},{8,12},{9,13},{10,... | collective-permute-start | bytes 294920 | tf_op jit(solution)/shard_map/ppermute | solution.py:102
  136.1 5.2 %collective-permute-start.32 = (bf16[64,768]{1,0:T(8,128)(2,1)S(1)}, bf16[64,768]{1,0:T(8,128)(2,1)S(1)}, u32[]{:S(2)}, u32[]{:S(2)}) collective-permute-start(bf16[64,768]{1,0:T(8,128)(2,1)S(1)} %pad_maximum_fusion.15), channel_id=1, source_target_pairs={{0,1},{1,0},{2,3},{3,2},{4,5},{5,4},{6,7},{7,6},{8,9},{9,8},{10,11... | collective-permute-start | bytes 294920 | tf_op jit(solution)/shard_map/ppermute | solution.py:102
  137.9 11.9 %copy-start.4 = (bf16[1152,896]{1,0:T(8,128)(2,1)S(1)}, bf16[1152,896]{1,0:T(8,128)(2,1)}, u32[]{:S(2)}) copy-start(bf16[1152,896]{1,0:T(8,128)(2,1)} %param.19) | copy-start | bytes 6193156
  137.9 6.0 %collective-permute-start.24 = (bf16[2,64,768]{2,1,0:T(8,128)(2,1)S(1)}, bf16[2,64,768]{2,1,0:T(8,128)(2,1)S(1)}, u32[]{:S(2)}, u32[]{:S(2)}) collective-permute-start(bf16[2,64,768]{2,1,0:T(8,128)(2,1)S(1)} %get-tuple-element.62), channel_id=1, source_target_pairs={{0,1},{1,0},{2,3},{3,2},{4,5},{5,4},{6,7},{7,6},{8,9},{9,8},{10,11... | collective-permute-start | bytes 589832 | tf_op jit(solution)/shard_map/ppermute | solution.py:102
  140.3 7.0 %collective-permute-start.30 = (bf16[2,64,768]{2,1,0:T(8,128)(2,1)S(1)}, bf16[2,64,768]{2,1,0:T(8,128)(2,1)S(1)}, u32[]{:S(2)}, u32[]{:S(2)}) collective-permute-start(bf16[2,64,768]{2,1,0:T(8,128)(2,1)S(1)} %get-tuple-element.60), channel_id=1, source_target_pairs={{0,3},{1,2},{2,1},{3,0},{4,7},{5,6},{6,5},{7,4},{8,11},{9,10},{10,... | collective-permute-start | bytes 589832 | tf_op jit(solution)/shard_map/ppermute | solution.py:102
  141.3 6.1 %collective-permute-start.33 = (bf16[2,64,768]{2,1,0:T(8,128)(2,1)S(1)}, bf16[2,64,768]{2,1,0:T(8,128)(2,1)S(1)}, u32[]{:S(2)}, u32[]{:S(2)}) collective-permute-start(bf16[2,64,768]{2,1,0:T(8,128)(2,1)S(1)} %get-tuple-element.58), channel_id=1, source_target_pairs={{0,4},{1,5},{2,6},{3,7},{4,0},{5,1},{6,2},{7,3},{8,12},{9,13},{10,... | collective-permute-start | bytes 589832 | tf_op jit(solution)/shard_map/ppermute | solution.py:102
  144.0 9.0 %collective-permute-start.25 = (bf16[2,2,64,768]{3,2,1,0:T(8,128)(2,1)S(1)}, bf16[2,2,64,768]{3,2,1,0:T(8,128)(2,1)S(1)}, u32[]{:S(2)}, u32[]{:S(2)}) collective-permute-start(bf16[2,2,64,768]{3,2,1,0:T(8,128)(2,1)S(1)} %pad_maximum_fusion.1.s0), channel_id=1, source_target_pairs={{0,4},{1,5},{2,6},{3,7},{4,0},{5,1},{6,2},{7,3},{8,12},{9,13},{10,... | collective-permute-start | bytes 1179656 | tf_op jit(solution)/shard_map/ppermute | solution.py:102
  147.3 7.9 %collective-permute-start.31 = (bf16[2,2,64,768]{3,2,1,0:T(8,128)(2,1)S(1)}, bf16[2,2,64,768]{3,2,1,0:T(8,128)(2,1)S(1)}, u32[]{:S(2)}, u32[]{:S(2)}) collective-permute-start(bf16[2,2,64,768]{3,2,1,0:T(8,128)(2,1)S(1)} %pad_maximum_fusion.2.s1), channel_id=1, source_target_pairs={{0,1},{1,0},{2,3},{3,2},{4,5},{5,4},{6,7},{7,6},{8,9},{9,8},{10,11... | collective-permute-start | bytes 1179656 | tf_op jit(solution)/shard_map/ppermute | solution.py:102
  147.5 9.3 %collective-permute-start.34 = (bf16[2,2,64,768]{3,2,1,0:T(8,128)(2,1)S(1)}, bf16[2,2,64,768]{3,2,1,0:T(8,128)(2,1)S(1)}, u32[]{:S(2)}, u32[]{:S(2)}) collective-permute-start(bf16[2,2,64,768]{3,2,1,0:T(8,128)(2,1)S(1)} %pad_maximum_fusion.3.s2), channel_id=1, source_target_pairs={{0,3},{1,2},{2,1},{3,0},{4,7},{5,6},{6,5},{7,4},{8,11},{9,10},{10,... | collective-permute-start | bytes 1179656 | tf_op jit(solution)/shard_map/ppermute | solution.py:102
  156.8 20.8 %copy-start.1 = (bf16[2,512,896]{2,1,0:T(8,128)(2,1)S(1)}, bf16[2,512,896]{2,1,0:T(8,128)(2,1)}, u32[]{:S(2)}) copy-start(bf16[2,512,896]{2,1,0:T(8,128)(2,1)} %param.14) | copy-start | bytes 5505028
